TPU v7x, 32 devices: a whole 2x2x4 slice. The times are simulated.
32 devices in a mesh: groups: 2 (over y), aux: 4 (over z), orb: 2 (over x), sub: 2 (over core).
Axes of the slice: x: 2, y: 2, z: 4, core: 2. Of those that a mesh axis runs over, the one named last changes fastest.
Arguments:
- three_index: bfloat16 [16, 32, 16, 128, 128], P(('groups', 'aux'), 'orb'), parts along dimension 0, may hold values from -0.125 to 0.125
- block_cols: int32 [8, 32, 16], P(('groups', 'aux'), 'orb'), parts along dimension 0, may hold values from 0 to 31, as said below
- live_count: int32 [8, 32], P(('groups', 'aux'), 'orb'), parts along dimension 0, may hold values from 1 to 16, as said below
- coefficients: bfloat16 [8192, 1024], P(('groups', 'orb'), 'sub'), parts along dimension 0, may hold values from -0.1875 to 0.1875
Outputs:
- exchange_matrix: float32 [8192, 4096], P(('groups', 'aux', 'sub'), 'orb'), parts along dimension 0
There are 2 independent parts, one for each index of `groups`. A program takes and returns all parts, laid end to end along the dimension named above; each array names one. Nothing has to cross between parts.
Inputs may be any that keep to these rules, and one draw needn't show every extreme that they name: `block_cols`: within each row of 16 entries the basis blocks are distinct. Only the first live_count[a, m] slots of basis block m for aux block a hold screened blocks; the other slots are padding whose contents are not used. Some entry equals 16 in every draw.
All inputs are finite; a program needn't handle non-finite values.
Results may differ from a plain program's by a relative error of at most 0.0018.
Values may be sent and summed in bfloat16 or wider, within the bound.
No kernel may reach another device: no remote copies, remote signals or barrier semaphores. Data moves between devices by JAX's collectives and lax.ppermute only.
A program may use at most 128 MiB of HBM per device.

v0:
```python
import jax
import jax.numpy as jnp
from jax import lax
from jax.sharding import PartitionSpec as P


def transform_padded(three_index, columns, counts, coeff_blocks):
    slot_ids = lax.broadcasted_iota(jnp.int32, columns.shape, 1)
    alive_mask = slot_ids < counts[:, None]
    masked = jnp.where(alive_mask[None, :, :, None, None], three_index, jnp.zeros_like(three_index))
    picked = coeff_blocks[columns]
    return jnp.einsum("pmsrc,msci->pmri", masked, picked, preferred_element_type=jnp.float32)


def shards(three_index, block_cols, live_count, coefficients):
    whole_coeff = lax.all_gather(coefficients, "orb", axis=0, tiled=True)
    block_side = three_index.shape[3]
    coeff_blocks = whole_coeff.reshape(
        whole_coeff.shape[0] // block_side, block_side, whole_coeff.shape[1]
    )
    columns = block_cols[0]
    counts = live_count[0]
    partial_half = transform_padded(three_index, columns, counts, coeff_blocks)
    functions = three_index.shape[0]
    transformed = partial_half.astype(jnp.bfloat16).reshape(functions, -1, partial_half.shape[3])
    every_row = lax.all_gather(transformed, "orb", axis=1, tiled=True)
    return lax.psum_scatter(
        jnp.einsum("pli,pni->ln", every_row, transformed, preferred_element_type=jnp.float32),
        ("aux", "sub"),
        scatter_dimension=0,
        tiled=True,
    )


def solution(mesh):
    return jax.shard_map(
        shards,
        mesh=mesh,
        in_specs=(
            P(("groups", "aux"), "orb", None, None, None),
            P(("groups", "aux"), "orb", None),
            P(("groups", "aux"), "orb"),
            P(("groups", "orb"), "sub"),
        ),
        out_specs=P(("groups", "aux", "sub"), "orb"),
        check_vma=False,
    )
```

profile of v0, /device:TPU:20, one launch (start us, length us, event | category | flops | bytes accessed | tf_op | source)
XLA Modules:
  0.0 566.1 jit_solution(2782063401388299060)
XLA Ops:
  6.5 0.0 all-gather.3.cloned.1.call-start
  6.5 0.7 all-gather.3.cloned.1.call-update
  7.3 0.0 all-gather.5.cloned.1.call-start
  7.3 0.7 compare_select_fusion
  8.0 0.1 reshape.58
  8.1 0.7 iota_compare_fusion
  8.8 57.9 %all-gather.3.cloned.1.call-done = bf16[4096,512]{1,0:T(8,128)(2,1)} async-done(((bf16[2048,512]{1,0:T(8,128)(2,1)}), bf16[4096,512]{1,0:T(8,128)(2,1)}) %all-gather.3.cloned.1.call-update) | async-done | bytes 4194320 | tf_op jit(solution)/shard_map/all_gather | solution.py:16
  66.7 16.1 %gather_fusion = bf16[256,128,512]{2,1,0:T(8,128)(2,1)} fusion(bf16[32,128,512]{2,1,0:T(8,128)(2,1)} %bitcast.24, s32[1024]{0:T(1024)S(1)} %pad_clamp_fusion), kind=kCustom, calls=%fused_computation | custom fusion | bytes 67109888 | tf_op jit(solution)/shard_map/gather | solution.py:11
  82.8 19.7 %fusion.2 = bf16[2,16,128,512]{3,2,0,1:T(8,128)(2,1)} fusion(bf16[16,16,128,512,1]{3,2,1,4,0:T(8,128)(2,1)} %bitcast.25, bf16[2,16,16,128,128]{4,3,2,1,0:T(8,128)(2,1)} %param.4, pred[16,16]{1,0:T(8,128)(4,1)S(1)} %iota_compare_fusion), kind=kOutput, calls=%fused_computation.6 | convolution fusion | flops 8600420352 | bytes 54526208 | tf_op jit(solution)/shard_map/pmsrc,msci->pmri/dot_general | solution.py:12
  102.4 4.6 copy.7
  107.0 0.0 all-gather.5.cloned.1.call-update
  107.0 0.0 reduce-scatter.2.cloned.1.call-start
  107.1 104.1 %all-gather.5.cloned.1.call-done = bf16[2,4096,512]{2,1,0:T(8,128)(2,1)} async-done(((bf16[2,2048,512]{2,1,0:T(8,128)(2,1)}), bf16[2,4096,512]{2,1,0:T(8,128)(2,1)}) %all-gather.5.cloned.1.call-update) | async-done | bytes 8388624 | tf_op jit(solution)/shard_map/all_gather | solution.py:26
  211.2 25.2 %convolution_bitcast_fusion = f32[4096,2048]{1,0:T(8,128)} fusion(bf16[2,4096,512]{2,1,0:T(8,128)(2,1)} %all-gather.5.cloned.1.call-done, bf16[2,2048,512]{2,1,0:T(8,128)(2,1)} %bitcast.27), kind=kOutput, calls=%fused_computation.1 | convolution fusion | flops 17179869184 | bytes 46137344 | tf_op jit(solution)/shard_map/pli,pni->ln/dot_general | solution.py:28
  236.4 0.0 reduce-scatter.2.cloned.1.call-update
  236.4 323.1 %reduce-scatter.2.cloned.1.call-done = f32[512,2048]{1,0:T(8,128)} async-done(((f32[4096,2048]{1,0:T(8,128)}), f32[512,2048]{1,0:T(8,128)}) %reduce-scatter.2.cloned.1.call-update) | async-done | bytes 4194320 | tf_op jit(solution)/shard_map/reduce_scatter | solution.py:27
  (1 shorter events, 0.0 us)
Async XLA Ops:
  6.5 60.2 %all-gather.3.cloned.1.call-start = ((), (), s32[]{:S(2)}) async-start(), calls=%async_computation.1 | async-start | bytes 6291456 | tf_op jit(solution)/shard_map/all_gather | solution.py:16
  7.3 203.9 %all-gather.5.cloned.1.call-start = ((), (), s32[]{:S(2)}) async-start(), calls=%async_computation.2 | async-start | bytes 12582912 | tf_op jit(solution)/shard_map/all_gather | solution.py:26
  107.0 452.5 %reduce-scatter.2.cloned.1.call-start = ((), (), s32[]{:S(2)}) async-start(), calls=%async_computation.3 | async-start | bytes 37748736 | tf_op jit(solution)/shard_map/reduce_scatter | solution.py:27
Sparse Core Ops, SparseCore 0:
  8.9 57.7 all-gather.2
  107.1 103.9 all-gather.4
  236.5 322.9 reduce-scatter.1
where the time goes:
time: 571 us; the launch traced here: 566 us
  waiting for transfers between devices  486 us (85%)
  matrix products  44.9 us (8%)
  local copies, waits for them, and re-layouts  20.7 us (4%)
  between operations  13.1 us (2%)
    reduce_scatter x1, waiting for transfers between devices, shards(): lax.psum_scatter(jnp.einsum('pli,pni->ln', every_row, transformed, prefer...  323 us
    all_gather x1, waiting for transfers between devices, shards(): every_row = lax.all_gather(transformed, 'orb', axis=1, tiled=True)  104 us
    all_gather x1, waiting for transfers between devices, shards(): whole_coeff = lax.all_gather(coefficients, 'orb', axis=0, tiled=True)  57.9 us
    dot_general x1, matrix products, shards(): jnp.einsum('pli,pni->ln', every_row, transformed, preferred_element_type=...  25.2 us
    dot_general x1, matrix products, transform_padded(): jnp.einsum('pmsrc,msci->pmri', masked, picked, preferred_element_type=jnp...  19.7 us
    gather x1, local copies, waits for them, and re-layouts, transform_padded(): picked = coeff_blocks[columns]  16.1 us
  transfers between devices with their start and end apart: 3, of which 3 were waited for; matrix products, arithmetic and copies ran while one was open for 0% of the time, Pallas kernels for 0%

commit v1 on v0

v1 whole, which is shorter than its diff:
```python
import functools

import jax
import jax.numpy as jnp
from jax import lax
from jax.experimental import pallas as pl
from jax.experimental.pallas import tpu as pltpu
from jax.sharding import PartitionSpec as P

GROUP = 4
VMEM_LIMIT = 40 * 1024 * 1024


def transform_kernel(columns, counts, x_ref, *refs, parts):
    coeff_refs = refs[:parts]
    out_ref, coeff_vmem, total, sems = refs[parts:]
    functions, together, slots, side, _ = x_ref.shape
    width = coeff_vmem.shape[1]

    @pl.when(pl.program_id(0) == 0)
    def _():
        copies = []
        for part, ref in enumerate(coeff_refs):
            rows = ref.shape[0]
            copy = pltpu.make_async_copy(ref, coeff_vmem.at[pl.ds(part * rows, rows)], sems.at[part])
            copy.start()
            copies.append(copy)
        for copy in copies:
            copy.wait()

    for inner in range(together):
        block = pl.program_id(0) * together + inner
        count = counts[block]

        def product(first, inner=inner, block=block, count=count):
            left = jnp.concatenate(
                [
                    jnp.concatenate([x_ref[p, inner, first + t] for t in range(GROUP)], axis=1)
                    for p in range(functions)
                ],
                axis=0,
            )
            lane = lax.broadcasted_iota(jnp.int32, left.shape, 1)
            left = jnp.where(lane < (count - first) * side, left, jnp.zeros_like(left))
            right = jnp.concatenate(
                [
                    coeff_vmem[pl.ds(pl.multiple_of(columns[block, first + t] * side, side), side), :]
                    for t in range(GROUP)
                ],
                axis=0,
            )
            return jnp.dot(left, right, preferred_element_type=jnp.float32)

        total[inner] = product(0)
        for first in range(GROUP, slots, GROUP):

            @pl.when(count > first)
            def _(first=first, inner=inner, product=product):
                total[inner] += product(first)

        for p in range(functions):
            out_ref[inner * side : (inner + 1) * side, p * width : (p + 1) * width] = total[
                inner, p * side : (p + 1) * side, :
            ].astype(out_ref.dtype)


def transform(three_index, columns, counts, coeff_parts):
    functions, blocks, slots, side, _ = three_index.shape
    part_rows, width = coeff_parts[0].shape
    parts = len(coeff_parts)
    together = next(t for t in (4, 2, 1) if blocks % t == 0)
    flops = 2 * functions * blocks * slots * side * side * width
    return pl.pallas_call(
        functools.partial(transform_kernel, parts=parts),
        grid_spec=pltpu.PrefetchScalarGridSpec(
            num_scalar_prefetch=2,
            grid=(blocks // together,),
            in_specs=[
                pl.BlockSpec((functions, together, slots, side, side), lambda m, *_: (0, m, 0, 0, 0))
            ]
            + [pl.BlockSpec(memory_space=pl.ANY)] * parts,
            out_specs=pl.BlockSpec((together * side, functions * width), lambda m, *_: (m, 0)),
            scratch_shapes=[
                pltpu.VMEM((parts * part_rows, width), jnp.bfloat16),
                pltpu.VMEM((together, functions * side, width), jnp.float32),
                pltpu.SemaphoreType.DMA((parts,)),
            ],
        ),
        out_shape=jax.ShapeDtypeStruct((blocks * side, functions * width), jnp.bfloat16),
        compiler_params=pltpu.CompilerParams(vmem_limit_bytes=VMEM_LIMIT),
        cost_estimate=pl.CostEstimate(flops=flops, bytes_accessed=three_index.size * 2, transcendentals=0),
    )(columns, counts, three_index, *coeff_parts)


def product_kernel(index, *refs, parts):
    out_ref = refs[-1]
    total = None
    for rows_ref, cols_ref in zip(refs[:parts], refs[parts:-1]):
        term = lax.dot_general(
            rows_ref[0], cols_ref[...], (((1,), (1,)), ((), ())), preferred_element_type=jnp.float32
        )
        total = term if total is None else total + term
    out_ref[...] = total


def row_product(index, rows, cols):
    parts = len(rows)
    height, depth = rows[0].shape[1:]
    length = cols[0].shape[0]
    tile = min(length, 512)
    return pl.pallas_call(
        functools.partial(product_kernel, parts=parts),
        grid_spec=pltpu.PrefetchScalarGridSpec(
            num_scalar_prefetch=1,
            grid=(length // tile,),
            in_specs=[pl.BlockSpec((1, height, depth), lambda c, index: (index[0], 0, 0))] * parts
            + [pl.BlockSpec((tile, depth), lambda c, index: (c, 0))] * parts,
            out_specs=pl.BlockSpec((height, tile), lambda c, index: (0, c)),
        ),
        out_shape=jax.ShapeDtypeStruct((height, length), jnp.float32),
        compiler_params=pltpu.CompilerParams(vmem_limit_bytes=VMEM_LIMIT),
        cost_estimate=pl.CostEstimate(
            flops=2 * height * length * depth * parts,
            bytes_accessed=parts * 2 * depth * (height + length) + 4 * height * length,
            transcendentals=0,
        ),
    )(index, *rows, *cols)


class Line:
    def __init__(self, aux, orb):
        self.aux, self.orb, self.owned = aux, orb, aux // orb

    def targets(self, phase, o):
        first = ((o + phase) % self.orb) * self.owned
        return list(range(first, first + self.owned))

    def chains(self, phase, o, direction):
        head = 0 if direction > 0 else self.aux - 1
        found = sorted((t for t in self.targets(phase, o) if t != head), key=lambda t: -t * direction)
        late = self.owned - len(found) if phase else 0
        return {t: place + late for place, t in enumerate(found)}

    def first_use(self, phase, o, z, target):
        if target == z:
            return 10 * self.aux
        direction = 1 if target > z else -1
        return self.chains(phase, o, direction)[target] + (z if direction > 0 else self.aux - 1 - z)

    def order(self, phase, o, z):
        return sorted(self.targets(phase, o), key=lambda d: (self.first_use(phase, o, z, d), d))

    def hop(self, phase, rank, step):
        pairs, position, final = [], {}, {}
        for o in range(self.orb):
            for direction in (1, -1):
                z = step if direction > 0 else self.aux - 1 - step
                for target, place in self.chains(phase, o, direction).items():
                    if place != rank or (target - z) * direction <= 0:
                        continue
                    pairs.append((z * self.orb + o, (z + direction) * self.orb + o))
                    position[z * self.orb + o] = self.order(phase, o, z).index(target)
                    if z + direction == target:
                        final[target * self.orb + o] = True
        return pairs, position, final


def lookup(table, place):
    return jnp.asarray(table, jnp.int32)[place]


def after(value, earlier):
    return value if earlier is None else lax.optimization_barrier((value, earlier))[0]


def shards(mesh, three_index, block_cols, live_count, coefficients):
    aux, orb, sub = mesh.shape["aux"], mesh.shape["orb"], mesh.shape["sub"]
    z, o, s = lax.axis_index("aux"), lax.axis_index("orb"), lax.axis_index("sub")
    place = z * orb + o
    line = Line(aux, orb)
    owned = line.owned
    blocks = three_index.shape[1]

    coeff_parts = [coefficients]
    for k in range(1, orb):
        coeff_parts.append(lax.ppermute(coefficients, "orb", [((t + k) % orb, t) for t in range(orb)]))
    all_blocks = blocks * orb
    columns = lax.rem(block_cols[0] - o * blocks + all_blocks, all_blocks)
    own = transform(three_index, columns, live_count[0], coeff_parts)
    length, depth = own.shape
    height = length // (owned * sub)
    chunks = max(1, height // 256)
    piece = height // chunks

    cols = [own]
    for t in range(1, sub):
        cols.append(lax.ppermute(own, "sub", [((u + t) % sub, u) for u in range(sub)]))
    views = [c.reshape(owned * sub, height, depth) for c in cols]

    came_rows, last = {}, None
    for k in range(1, orb):
        for q in range(owned):
            table = [line.order(k, (b - k) % orb, a)[q] % owned for a in range(aux) for b in range(orb)]
            mine = after(lookup(table, place), last)
            came_rows[k, q] = []
            for t in range(sub):
                sent = lax.dynamic_slice_in_dim(views[0], mine * sub + lax.rem(s - t + sub, sub), 1, 0)
                pairs = [
                    (((b + k) % orb) * sub + (c + t) % sub, b * sub + c) for b in range(orb) for c in range(sub)
                ]
                came_rows[k, q].append(lax.ppermute(sent, ("orb", "sub"), pairs))
                last = sent

    squares = jnp.sum(jnp.square(after(own, last).astype(jnp.float32)), axis=1)
    diagonal = jnp.sum(lax.all_gather(squares, ("aux", "sub")), axis=0)

    events = []
    for k in range(orb):
        base = owned * k - 1 if k else 0
        for q in range(owned):
            events.append((((base + q) * chunks - 0.5) if k or q else -1.0, 0, "product", k, q, 0, 0))
        finals = {c: [] for c in range(chunks)}
        for rank in range(owned):
            for step in range(aux - 1):
                pairs, _, final = line.hop(k, rank, step)
                if not pairs:
                    continue
                for c in range(chunks):
                    when = (base + rank) * chunks + c + step
                    events.append((when, step, "hop", k, rank, step, c))
                    if final:
                        finals[c].append((when + 1.5, rank, step))
        for c in range(chunks):
            events.append((max(f[0] for f in finals[c]), 0, "fold", k, c, [f[1:] for f in finals[c]], 0))
    events.sort(key=lambda e: e[:2])

    sums, came, result, last = {}, {}, None, squares
    for _, _, kind, k, a1, a2, c in events:
        if kind == "product":
            q = a1
            if k == 0:
                table = [line.order(k, b, a)[q] % owned for a in range(aux) for b in range(orb)]
                index = (lookup(table, place) * sub + s)[None]
                rows = views
            else:
                index = jnp.zeros((1,), jnp.int32)
                rows = came_rows[k, q]
            sums[k, q] = row_product(after(index, last), rows, cols)
            last = sums[k, q]
        elif kind == "hop":
            rank, step = a1, a2
            pairs, position, final = line.hop(k, rank, step)
            used = sorted(set(position.values()))
            arrived = came.get((k, rank, step - 1, c))
            if arrived is not None:
                arrived = after(arrived, last)
            value = sums[k, used[0]][c * piece : (c + 1) * piece]
            for q in used[1:]:
                flag = lookup([position.get(i) == q for i in range(aux * orb)], place)
                value = jnp.where(flag > 0, sums[k, q][c * piece : (c + 1) * piece], value)
            if arrived is not None:
                value = value + arrived.astype(jnp.float32)
            last = value.astype(jnp.bfloat16)
            came[k, rank, step, c] = lax.ppermute(last, ("aux", "orb"), pairs)
        else:
            at, terms = a1, a2
            if result is None:
                result = jnp.zeros((height, length), jnp.float32)
            flag = lookup([z_ in line.targets(k, o_) for z_ in range(aux) for o_ in range(orb)], place)
            rows = slice(at * piece, (at + 1) * piece)
            total = jnp.where(flag > 0, after(sums[k, owned - 1], last)[rows], 0.0)
            if k:
                total = total + result[rows]
            for rank, step in terms:
                final = line.hop(k, rank, step)[2]
                flag = lookup([i in final for i in range(aux * orb)], place)
                total = total + jnp.where(flag > 0, came[k, rank, step, at].astype(jnp.float32), 0.0)
            if k == orb - 1:
                start = lax.rem(z, owned) * sub * height + s * height + at * piece
                local = lax.div(z, owned) == o
                row = lax.broadcasted_iota(jnp.int32, total.shape, 0) + start
                col = lax.broadcasted_iota(jnp.int32, total.shape, 1)
                exact = lax.dynamic_slice_in_dim(diagonal, start, piece)
                total = jnp.where((row == col) & local, exact[:, None], total)
            result = lax.dynamic_update_slice(result, total, (at * piece, 0))
            last = result
    return result


def solution(mesh):
    return jax.shard_map(
        functools.partial(shards, mesh),
        mesh=mesh,
        in_specs=(
            P(("groups", "aux"), "orb", None, None, None),
            P(("groups", "aux"), "orb", None),
            P(("groups", "aux"), "orb"),
            P(("groups", "orb"), "sub"),
        ),
        out_specs=P(("groups", "aux", "sub"), "orb"),
        check_vma=False,
    )
```

time: 571 us -> 348 us (0.61)
  waiting for transfers between devices: 486 us -> 151 us
  starting transfers between devices: 0.08 us -> 55.3 us
  matrix products: 44.9 us -> 0 us
  Pallas kernels: 0 us -> 42.5 us
  other arithmetic: 1.44 us -> 40.3 us
  blocking collectives: 0 us -> 29.5 us
  between operations: 13.1 us -> 6.48 us
    reduce_scatter x1 -> x0, waiting for transfers between devices: 323 us -> none  [shards(): lax.psum_scatter(jnp.einsum('pli,pni->ln', every_row, transformed, prefer...]
    all_gather x2 -> x0, waiting for transfers between devices: 162 us -> none  [the longest x1 104 us: shards(): every_row = lax.all_gather(transformed, 'orb', axis=1, tiled=True)]
    ppermute x0 -> x26, waiting for transfers between devices: none -> 151 us  [the longest x20 69.7 us: shards(): came[k, rank, step, c] = lax.ppermute(last, ('aux', 'orb'), pairs)]
    ppermute x0 -> x26, starting transfers between devices: none -> 55.3 us  [the longest x20 49.9 us: shards(): came[k, rank, step, c] = lax.ppermute(last, ('aux', 'orb'), pairs)]
    dot_general x2 -> x0, matrix products: 44.9 us -> none  [the longest x1 25.2 us: shards(): jnp.einsum('pli,pni->ln', every_row, transformed, preferred_element_type=...]
    pallas_call x0 -> x5, Pallas kernels: none -> 42.5 us  [the longest x4 30.6 us: row_product(): pl.pallas_call(functools.partial(product_kernel, parts=parts), grid_spec=...]
    all_gather x0 -> x1, blocking collectives: none -> 29.5 us  [shards(): diagonal = jnp.sum(lax.all_gather(squares, ('aux', 'sub')), axis=0)]
    convert_element_type x0 -> x11, other arithmetic: none -> 22.8 us  [shards(): last = value.astype(jnp.bfloat16)]
  transfers between devices with their start and end apart: 3 -> 26, of which waited for: 3 -> 9; matrix products, arithmetic and copies ran while one was open for 0% -> 13% of each run, Pallas kernels for 0% -> 6%
where the time goes in v1:
time: 348 us; the launch traced here: 344 us
  waiting for transfers between devices  151 us (43%)
  starting transfers between devices  55.3 us (16%)
  Pallas kernels  42.5 us (12%)
  other arithmetic  40.3 us (12%)
  blocking collectives  29.5 us (8%)
  local copies, waits for them, and re-layouts  19.7 us (6%)
  between operations  6.48 us (2%)
    ppermute x20, waiting for transfers between devices, shards(): came[k, rank, step, c] = lax.ppermute(last, ('aux', 'orb'), pairs)  69.7 us
    ppermute x20, starting transfers between devices, shards(): came[k, rank, step, c] = lax.ppermute(last, ('aux', 'orb'), pairs)  49.9 us
    ppermute x1, waiting for transfers between devices, shards(): lax.ppermute(coefficients, 'orb', [((t + k) % orb, t) for t in range(orb)])  45.4 us
    ppermute x4, waiting for transfers between devices, shards(): came_rows[k, q].append(lax.ppermute(sent, ('orb', 'sub'), pairs))  35.5 us
    pallas_call x4, Pallas kernels, row_product(): pl.pallas_call(functools.partial(product_kernel, parts=parts), grid_spec=...  30.6 us
    all_gather x1, blocking collectives, shards(): diagonal = jnp.sum(lax.all_gather(squares, ('aux', 'sub')), axis=0)  29.5 us
    convert_element_type x11, other arithmetic, shards(): last = value.astype(jnp.bfloat16)  22.8 us
    dynamic_update_slice x3, other arithmetic, shards(): result = lax.dynamic_update_slice(result, total, (at * piece, 0))  12.2 us
  transfers between devices with their start and end apart: 26, of which 9 were waited for; matrix products, arithmetic and copies ran while one was open for 13% of the time, Pallas kernels for 6%

profile of v1, /device:TPU:20, one launch (start us, length us, event | category | flops | bytes accessed | tf_op | source)
XLA Modules:
  0.0 344.4 jit_solution(1324435587752147630)
XLA Ops:
  0.0 1.5 collective-permute-start
  2.2 45.4 %collective-permute-done.refs_1_ = bf16[2048,512]{1,0:T(8,128)(2,1)S(1)} collective-permute-done((bf16[2048,512]{1,0:T(8,128)(2,1)}, bf16[2048,512]{1,0:T(8,128)(2,1)S(1)}, u32[]{:S(2)}, u32[]{:S(2)}) %collective-permute-start) | collective-permute-done | bytes 2097184 | tf_op jit(solution)/shard_map/ppermute | solution.py:186
  47.6 1.6 copy-done.9
  49.8 12.0 %shard_map.244.refs_2_ = bf16[2048,1024]{1,0:T(8,128)(2,1)} custom-call(s32[16,16]{1,0:T(8,128)S(1)} %negate_select_fusion.columns, s32[16]{0:T(128)S(1)} %bitcast.16, bf16[2,16,16,128,128]{4,3,2,1,0:T(8,128)(2,1)} %x_ref.1, bf16[2048,512]{1,0:T(8,128)(2,1)S(1)} %copy-done.9, bf16[2048,512]{1,0:T(8,128)(2,1)S(1)} %collective-permute-done.refs_1_), custom_call_target="tpu_custom_call" | custom-call | flops 8589934592 | bytes 16777216 | tf_op jit(solution)/shard_map/pallas_call | solution.py:73
  63.9 1.3 constant_dynamic-slice_fusion.3
  65.9 3.6 %constant_dynamic-slice_fusion = (bf16[1,512,1024]{2,1,0:T(8,128)(2,1)}, bf16[1,512,1024]{2,1,0:T(8,128)(2,1)}, bf16[1,512,1024]{2,1,0:T(8,128)(2,1)}) fusion(bf16[4,512,1024]{2,1,0:T(8,128)(2,1)} %bitcast.7.refs_0_, s32[]{:T(128)S(6)} %select_n.167, s32[]{:T(128)S(6)} %select_n.165, s32[]{:T(128)S(6)} %select_n.164), kind=kLoop, calls=%fused_computation.38 | loop fusion | bytes 6291468 | tf_op jit(solution)/shard_map/dynamic_slice | solution.py:207
  69.5 3.1 multiply_reduce_fusion
  72.6 8.4 %shard_map.245 = f32[512,2048]{1,0:T(8,128)S(1)} custom-call(s32[1]{0:T(128)} %bitcast.4.index, bf16[4,512,1024]{2,1,0:T(8,128)(2,1)} %bitcast.7.refs_0_, bf16[4,512,1024]{2,1,0:T(8,128)(2,1)} %bitcast.9.refs_1_, bf16[2048,1024]{1,0:T(8,128)(2,1)} %shard_map.244.refs_2_, bf16[2048,1024]{1,0:T(8,128)(2,1)} %collective-permute-done.1.refs_3_), custom_call_target="tpu_custom_call" | custom-call | flops 4294967296 | bytes 14680064 | tf_op jit(solution)/shard_map/pallas_call | solution.py:111
  81.0 1.5 fusion.10
  83.2 1.3 collective-permute-start.2
  88.7 1.5 collective-permute-start.12
  90.2 19.9 %collective-permute-done.2 = bf16[256,2048]{1,0:T(8,128)(2,1)S(1)} collective-permute-done((bf16[256,2048]{1,0:T(8,128)(2,1)S(1)}, bf16[256,2048]{1,0:T(8,128)(2,1)S(1)}, u32[]{:S(2)}, u32[]{:S(2)}) %collective-permute-start.2) | collective-permute-done | bytes 1048608 | tf_op jit(solution)/shard_map/ppermute | solution.py:264
  110.1 1.3 collective-permute-start.10
  111.4 1.9 add_convert_fusion.11
  113.3 7.9 %shard_map.246 = f32[512,2048]{1,0:T(8,128)S(1)} custom-call(s32[1]{0:T(128)} %bitcast.2.index, bf16[4,512,1024]{2,1,0:T(8,128)(2,1)} %bitcast.7.refs_0_, bf16[4,512,1024]{2,1,0:T(8,128)(2,1)} %bitcast.9.refs_1_, bf16[2048,1024]{1,0:T(8,128)(2,1)} %shard_map.244.refs_2_, bf16[2048,1024]{1,0:T(8,128)(2,1)} %collective-permute-done.1.refs_3_), custom_call_target="tpu_custom_call" | custom-call | flops 4294967296 | bytes 14680064 | tf_op jit(solution)/shard_map/pallas_call | solution.py:111
  121.5 35.5 %collective-permute-done.3.refs_0_ = bf16[1,512,1024]{2,1,0:T(8,128)(2,1)S(1)} collective-permute-done((bf16[1,512,1024]{2,1,0:T(8,128)(2,1)}, bf16[1,512,1024]{2,1,0:T(8,128)(2,1)S(1)}, u32[]{:S(2)}, u32[]{:S(2)}) %collective-permute-start.3) | collective-permute-done | bytes 1048608 | tf_op jit(solution)/shard_map/ppermute | solution.py:211
  157.0 13.0 %collective-permute-start.14 = (bf16[256,2048]{1,0:T(8,128)(2,1)S(1)}, bf16[256,2048]{1,0:T(8,128)(2,1)}, u32[]{:S(2)}, u32[]{:S(2)}) collective-permute-start(bf16[256,2048]{1,0:T(8,128)(2,1)S(1)} %add_convert_fusion.11), channel_id=1, source_target_pairs={{8,4},{6,10},{9,5},{7,11},{24,20},{22,26},{25,21},{23,27}} | collective-permute-start | bytes 3145736 | tf_op jit(solution)/shard_map/ppermute | solution.py:264
  170.0 1.3 collective-permute-start.6
  171.3 7.2 %shard_map.247 = f32[512,2048]{1,0:T(8,128)S(1)} custom-call(s32[1]{0:T(128)} %constant.78.clone.1.index, bf16[1,512,1024]{2,1,0:T(8,128)(2,1)S(1)} %collective-permute-done.3.refs_0_, bf16[1,512,1024]{2,1,0:T(8,128)(2,1)S(1)} %collective-permute-done.4.refs_1_, bf16[2048,1024]{1,0:T(8,128)(2,1)} %shard_map.244.refs_2_, ...), custom_call_target="tpu_custom_call" | custom-call | flops 4294967296 | bytes 14680064 | tf_op jit(solution)/shard_map/pallas_call | solution.py:111
  179.7 2.5 copy-done.1
  182.5 8.9 %collective-permute-done.14 = bf16[256,2048]{1,0:T(8,128)(2,1)} collective-permute-done((bf16[256,2048]{1,0:T(8,128)(2,1)S(1)}, bf16[256,2048]{1,0:T(8,128)(2,1)}, u32[]{:S(2)}, u32[]{:S(2)}) %collective-permute-start.14) | collective-permute-done | bytes 1048608 | tf_op jit(solution)/shard_map/ppermute | solution.py:264
  191.4 4.5 %collective-permute-start.11 = (bf16[256,2048]{1,0:T(8,128)(2,1)S(1)}, bf16[256,2048]{1,0:T(8,128)(2,1)S(1)}, u32[]{:S(2)}, u32[]{:S(2)}) collective-permute-start(bf16[256,2048]{1,0:T(8,128)(2,1)S(1)} %add_convert_fusion.8), channel_id=1, source_target_pairs={{8,4},{6,10},{9,5},{7,11},{24,20},{22,26},{25,21},{23,27}} | collective-permute-start | bytes 3145736 | tf_op jit(solution)/shard_map/ppermute | solution.py:264
  196.6 1.6 collective-permute-start.8
  198.2 1.3 add_convert_fusion.10
  199.5 1.3 collective-permute-start.9
  202.0 15.4 %collective-permute-done.11 = bf16[256,2048]{1,0:T(8,128)(2,1)S(1)} collective-permute-done((bf16[256,2048]{1,0:T(8,128)(2,1)S(1)}, bf16[256,2048]{1,0:T(8,128)(2,1)S(1)}, u32[]{:S(2)}, u32[]{:S(2)}) %collective-permute-start.11) | collective-permute-done | bytes 1048608 | tf_op jit(solution)/shard_map/ppermute | solution.py:264
  217.5 1.5 collective-permute-start.7
  218.9 3.3 add_convert_fusion.3
  222.2 7.2 %shard_map.248 = f32[512,2048]{1,0:T(8,128)S(1)} custom-call(s32[1]{0:T(128)} %constant.78.clone.1.index, bf16[1,512,1024]{2,1,0:T(8,128)(2,1)S(1)} %collective-permute-done.12.refs_0_, bf16[1,512,1024]{2,1,0:T(8,128)(2,1)S(1)} %collective-permute-done.13.refs_1_, bf16[2048,1024]{1,0:T(8,128)(2,1)} %shard_map.244.refs_2_, ...), custom_call_target="tpu_custom_call" | custom-call | flops 4294967296 | bytes 14680064 | tf_op jit(solution)/shard_map/pallas_call | solution.py:111
  229.4 1.6 select_convert_fusion
  233.0 2.5 add_convert_fusion.6
  235.6 2.5 add_convert_fusion.5
  246.0 6.4 %collective-permute-start.20 = (bf16[256,2048]{1,0:T(8,128)(2,1)}, bf16[256,2048]{1,0:T(8,128)(2,1)S(1)}, u32[]{:S(2)}, u32[]{:S(2)}) collective-permute-start(bf16[256,2048]{1,0:T(8,128)(2,1)} %add_convert_fusion.6), channel_id=1, source_target_pairs={{8,4},{6,10},{9,5},{7,11},{24,20},{22,26},{25,21},{23,27}} | collective-permute-start | bytes 3145736 | tf_op jit(solution)/shard_map/ppermute | solution.py:264
  253.1 4.0 %collective-permute-start.16 = (bf16[256,2048]{1,0:T(8,128)(2,1)}, bf16[256,2048]{1,0:T(8,128)(2,1)S(1)}, u32[]{:S(2)}, u32[]{:S(2)}) collective-permute-start(bf16[256,2048]{1,0:T(8,128)(2,1)} %add_convert_fusion.10), channel_id=1, source_target_pairs={{8,4},{6,10},{9,5},{7,11},{24,20},{22,26},{25,21},{23,27}} | collective-permute-start | bytes 3145736 | tf_op jit(solution)/shard_map/ppermute | solution.py:264
  257.2 1.6 collective-permute-start.21
  258.8 2.9 add_convert_fusion.2
  261.7 3.8 %collective-permute-done.17 = bf16[256,2048]{1,0:T(8,128)(2,1)} collective-permute-done((bf16[256,2048]{1,0:T(8,128)(2,1)}, bf16[256,2048]{1,0:T(8,128)(2,1)}, u32[]{:S(2)}, u32[]{:S(2)}) %collective-permute-start.17) | collective-permute-done | bytes 1048608 | tf_op jit(solution)/shard_map/ppermute | solution.py:264
  266.4 4.0 %add_convert_fusion.4 = (bf16[256,2048]{1,0:T(8,128)(2,1)}, bf16[256,2048]{1,0:T(8,128)(2,1)}) fusion(bf16[256,2048]{1,0:T(8,128)(2,1)} %collective-permute-done.7, f32[512,2048]{1,0:T(8,128)S(1)} %copy-done.5, bf16[256,2048]{1,0:T(8,128)(2,1)} %collective-permute-done.17), kind=kLoop, calls=%fused_computation.18 | loop fusion | flops 3145728 | bytes 8388608 | tf_op jit(solution)/shard_map/convert_element_type | solution.py:263
  270.3 5.9 %collective-permute-done.20 = bf16[256,2048]{1,0:T(8,128)(2,1)S(1)} collective-permute-done((bf16[256,2048]{1,0:T(8,128)(2,1)}, bf16[256,2048]{1,0:T(8,128)(2,1)S(1)}, u32[]{:S(2)}, u32[]{:S(2)}) %collective-permute-start.20) | collective-permute-done | bytes 1048608 | tf_op jit(solution)/shard_map/ppermute | solution.py:264
  277.5 2.3 collective-permute-start.22
  280.5 15.1 %collective-permute-done.16 = bf16[256,2048]{1,0:T(8,128)(2,1)S(1)} collective-permute-done((bf16[256,2048]{1,0:T(8,128)(2,1)}, bf16[256,2048]{1,0:T(8,128)(2,1)S(1)}, u32[]{:S(2)}, u32[]{:S(2)}) %collective-permute-start.16) | collective-permute-done | bytes 1048608 | tf_op jit(solution)/shard_map/ppermute | solution.py:264
  295.7 2.3 collective-permute-start.24
  298.7 2.5 pad_maximum_fusion
  302.4 1.4 add_convert_fusion
  303.8 1.3 collective-permute-start.25
  305.1 29.5 %all-gather = f32[16384]{0:T(1024)S(1)} all-gather(f32[2048]{0:T(1024)S(1)} %multiply_reduce_fusion), channel_id=2, replica_groups=mesh['groups'=2,'aux'=4,'orb'=2,'sub'=2] {'aux','sub'}, dimensions={0}, use_global_device_ids=true | all-gather | bytes 73728 | tf_op jit(solution)/shard_map/all_gather | solution.py:215
  334.7 4.9 %select_dynamic-update-slice_fusion = f32[512,2048]{1,0:T(8,128)} fusion(f32[512,2048]{1,0:T(8,128)} %pad_maximum_fusion, bf16[256,2048]{1,0:T(8,128)(2,1)} %collective-permute-done.23, bf16[256,2048]{1,0:T(8,128)(2,1)S(1)} %collective-permute-done.18, bf16[256,2048]{1,0:T(8,128)(2,1)} %collective-permute-done.22, f32[256,2048]{1,0:T(8,128)S(1)} %select_add_fusion.1, ...), kind=kLoop, calls=%fused_computation.9 | loop fusion | flops 7340032 | bytes 9440769 | tf_op jit(solution)/shard_map/dynamic_update_slice | solution.py:285
  339.7 4.8 %fusion.4 = f32[512,2048]{1,0:T(8,128)} fusion(f32[512,2048]{1,0:T(8,128)} %select_dynamic-update-slice_fusion, bf16[256,2048]{1,0:T(8,128)(2,1)} %collective-permute-done.25, bf16[256,2048]{1,0:T(8,128)(2,1)S(1)} %copy-done.12, bf16[256,2048]{1,0:T(8,128)(2,1)} %collective-permute-done.24, f32[512,2048]{1,0:T(8,128)S(1)} %copy-done.8, ...), kind=kLoop, calls=%fused_computation.7 | loop fusion | flops 7340032 | bytes 9440769 | tf_op jit(solution)/shard_map/dynamic_update_slice | solution.py:285
  (92 shorter events, 22.2 us)
Async XLA Ops:
  0.0 47.6 %collective-permute-start = (bf16[2048,512]{1,0:T(8,128)(2,1)}, bf16[2048,512]{1,0:T(8,128)(2,1)S(1)}, u32[]{:S(2)}, u32[]{:S(2)}) collective-permute-start(bf16[2048,512]{1,0:T(8,128)(2,1)} %refs_0_.1), channel_id=1, source_target_pairs={{2,0},{0,2},{3,1},{1,3},{6,4},{4,6},{7,5},{5,7},{10,8},{8,10},{11,... | collective-permute-start | bytes 6291464 | tf_op jit(solution)/shard_map/ppermute | solution.py:186
  47.6 1.6 copy-start.9
  49.8 12.1 %copy-start.22 = (s32[8]{0:T(128)S(1)}, s32[8]{0:T(128)}, u32[]{:S(2)}) copy-start(s32[8]{0:T(128)} %constant.91.clone) | copy-start | bytes 100
  49.8 13.4 %copy-start.21 = (s32[8]{0:T(128)S(1)}, s32[8]{0:T(128)}, u32[]{:S(2)}) copy-start(s32[8]{0:T(128)} %constant.92.clone) | copy-start | bytes 100
  61.8 10.8 %collective-permute-start.1 = (bf16[2048,1024]{1,0:T(8,128)(2,1)}, bf16[2048,1024]{1,0:T(8,128)(2,1)}, u32[]{:S(2)}, u32[]{:S(2)}) collective-permute-start(bf16[2048,1024]{1,0:T(8,128)(2,1)} %shard_map.244.refs_2_), channel_id=1, source_target_pairs={{1,0},{0,1},{3,2},{2,3},{5,4},{4,5},{7,6},{6,7},{9,8},{8,9},{11,10... | collective-permute-start | bytes 12582920 | tf_op jit(solution)/shard_map/ppermute | solution.py:197
  80.9 2.3 copy-start
  81.0 4.2 %copy-start.20 = (s32[8]{0:T(128)S(1)}, s32[8]{0:T(128)}, u32[]{:S(2)}) copy-start(s32[8]{0:T(128)} %constant.93.clone) | copy-start | bytes 100
  83.2 26.9 %collective-permute-start.2 = (bf16[256,2048]{1,0:T(8,128)(2,1)S(1)}, bf16[256,2048]{1,0:T(8,128)(2,1)S(1)}, u32[]{:S(2)}, u32[]{:S(2)}) collective-permute-start(bf16[256,2048]{1,0:T(8,128)(2,1)S(1)} %get-tuple-element.63), channel_id=1, source_target_pairs={{0,4},{12,8},{2,6},{14,10},{1,5},{13,9},{3,7},{15,11},{16,20},{28,... | collective-permute-start | bytes 3145736 | tf_op jit(solution)/shard_map/ppermute | solution.py:264
  86.4 83.6 %collective-permute-start.4 = (bf16[1,512,1024]{2,1,0:T(8,128)(2,1)S(1)}, bf16[1,512,1024]{2,1,0:T(8,128)(2,1)S(1)}, u32[]{:S(2)}, u32[]{:S(2)}) collective-permute-start(bf16[1,512,1024]{2,1,0:T(8,128)(2,1)S(1)} %constant_dynamic-slice_fusion.3), channel_id=1, source_target_pairs={{3,0},{2,1},{1,2},{0,3},{7,4},{6,5},{5,6},{4,7},{11,8},{10,9},{9,1... | collective-permute-start | bytes 3145736 | tf_op jit(solution)/shard_map/ppermute | solution.py:211
  87.0 135.2 %collective-permute-start.13 = (bf16[1,512,1024]{2,1,0:T(8,128)(2,1)}, bf16[1,512,1024]{2,1,0:T(8,128)(2,1)S(1)}, u32[]{:S(2)}, u32[]{:S(2)}) collective-permute-start(bf16[1,512,1024]{2,1,0:T(8,128)(2,1)} %get-tuple-element.57), channel_id=1, source_target_pairs={{3,0},{2,1},{1,2},{0,3},{7,4},{6,5},{5,6},{4,7},{11,8},{10,9},{9,1... | collective-permute-start | bytes 3145736 | tf_op jit(solution)/shard_map/ppermute | solution.py:211
  88.2 68.8 %collective-permute-start.3 = (bf16[1,512,1024]{2,1,0:T(8,128)(2,1)}, bf16[1,512,1024]{2,1,0:T(8,128)(2,1)S(1)}, u32[]{:S(2)}, u32[]{:S(2)}) collective-permute-start(bf16[1,512,1024]{2,1,0:T(8,128)(2,1)} %get-tuple-element.56), channel_id=1, source_target_pairs={{2,0},{3,1},{0,2},{1,3},{6,4},{7,5},{4,6},{5,7},{10,8},{11,9},{8,1... | collective-permute-start | bytes 3145736 | tf_op jit(solution)/shard_map/ppermute | solution.py:211
  88.7 133.5 %collective-permute-start.12 = (bf16[1,512,1024]{2,1,0:T(8,128)(2,1)}, bf16[1,512,1024]{2,1,0:T(8,128)(2,1)S(1)}, u32[]{:S(2)}, u32[]{:S(2)}) collective-permute-start(bf16[1,512,1024]{2,1,0:T(8,128)(2,1)} %get-tuple-element.55), channel_id=1, source_target_pairs={{2,0},{3,1},{0,2},{1,3},{6,4},{7,5},{4,6},{5,7},{10,8},{11,9},{8,1... | collective-permute-start | bytes 3145736 | tf_op jit(solution)/shard_map/ppermute | solution.py:211
  110.1 3.2 copy-start.13
  110.1 68.7 %collective-permute-start.10 = (bf16[256,2048]{1,0:T(8,128)(2,1)}, bf16[256,2048]{1,0:T(8,128)(2,1)S(1)}, u32[]{:S(2)}, u32[]{:S(2)}) collective-permute-start(bf16[256,2048]{1,0:T(8,128)(2,1)} %get-tuple-element.62), channel_id=1, source_target_pairs={{0,4},{12,8},{2,6},{14,10},{1,5},{13,9},{3,7},{15,11},{16,20},{28,... | collective-permute-start | bytes 3145736 | tf_op jit(solution)/shard_map/ppermute | solution.py:264
  121.1 111.9 %copy-start.2 = (f32[512,2048]{1,0:T(8,128)}, f32[512,2048]{1,0:T(8,128)S(1)}, u32[]{:S(2)}) copy-start(f32[512,2048]{1,0:T(8,128)S(1)} %shard_map.246) | copy-start | bytes 12582916
  157.0 34.4 %collective-permute-start.14 = (bf16[256,2048]{1,0:T(8,128)(2,1)S(1)}, bf16[256,2048]{1,0:T(8,128)(2,1)}, u32[]{:S(2)}, u32[]{:S(2)}) collective-permute-start(bf16[256,2048]{1,0:T(8,128)(2,1)S(1)} %add_convert_fusion.11), channel_id=1, source_target_pairs={{8,4},{6,10},{9,5},{7,11},{24,20},{22,26},{25,21},{23,27}} | collective-permute-start | bytes 3145736 | tf_op jit(solution)/shard_map/ppermute | solution.py:264
  170.0 26.5 %collective-permute-start.6 = (bf16[256,2048]{1,0:T(8,128)(2,1)S(1)}, bf16[256,2048]{1,0:T(8,128)(2,1)S(1)}, u32[]{:S(2)}, u32[]{:S(2)}) collective-permute-start(bf16[256,2048]{1,0:T(8,128)(2,1)S(1)} %get-tuple-element.60), channel_id=1, source_target_pairs={{12,8},{2,6},{13,9},{3,7},{28,24},{18,22},{29,25},{19,23}} | collective-permute-start | bytes 3145736 | tf_op jit(solution)/shard_map/ppermute | solution.py:264
  178.5 57.1 %copy-start.4 = (f32[512,2048]{1,0:T(8,128)}, f32[512,2048]{1,0:T(8,128)S(1)}, u32[]{:S(2)}) copy-start(f32[512,2048]{1,0:T(8,128)S(1)} %shard_map.247) | copy-start | bytes 12582916
  178.5 3.7 %copy-start.1 = (f32[512,2048]{1,0:T(8,128)S(1)}, f32[512,2048]{1,0:T(8,128)}, u32[]{:S(2)}) copy-start(f32[512,2048]{1,0:T(8,128)} %copy-done) | copy-start | bytes 12582916
  178.9 20.6 %collective-permute-start.5 = (bf16[256,2048]{1,0:T(8,128)(2,1)S(1)}, bf16[256,2048]{1,0:T(8,128)(2,1)S(1)}, u32[]{:S(2)}, u32[]{:S(2)}) collective-permute-start(bf16[256,2048]{1,0:T(8,128)(2,1)S(1)} %get-tuple-element.59), channel_id=1, source_target_pairs={{0,4},{14,10},{1,5},{15,11},{16,20},{30,26},{17,21},{31,27}} | collective-permute-start | bytes 3145736 | tf_op jit(solution)/shard_map/ppermute | solution.py:264
  191.4 26.0 %collective-permute-start.11 = (bf16[256,2048]{1,0:T(8,128)(2,1)S(1)}, bf16[256,2048]{1,0:T(8,128)(2,1)S(1)}, u32[]{:S(2)}, u32[]{:S(2)}) collective-permute-start(bf16[256,2048]{1,0:T(8,128)(2,1)S(1)} %add_convert_fusion.8), channel_id=1, source_target_pairs={{8,4},{6,10},{9,5},{7,11},{24,20},{22,26},{25,21},{23,27}} | collective-permute-start | bytes 3145736 | tf_op jit(solution)/shard_map/ppermute | solution.py:264
  196.6 39.0 %collective-permute-start.8 = (bf16[256,2048]{1,0:T(8,128)(2,1)S(1)}, bf16[256,2048]{1,0:T(8,128)(2,1)}, u32[]{:S(2)}, u32[]{:S(2)}) collective-permute-start(bf16[256,2048]{1,0:T(8,128)(2,1)S(1)} %get-tuple-element.58), channel_id=1, source_target_pairs={{0,4},{14,10},{1,5},{15,11},{16,20},{30,26},{17,21},{31,27}} | collective-permute-start | bytes 3145736 | tf_op jit(solution)/shard_map/ppermute | solution.py:264
  199.5 33.5 %collective-permute-start.9 = (bf16[256,2048]{1,0:T(8,128)(2,1)S(1)}, bf16[256,2048]{1,0:T(8,128)(2,1)}, u32[]{:S(2)}, u32[]{:S(2)}) collective-permute-start(bf16[256,2048]{1,0:T(8,128)(2,1)S(1)} %get-tuple-element.61), channel_id=1, source_target_pairs={{12,8},{2,6},{13,9},{3,7},{28,24},{18,22},{29,25},{19,23}} | collective-permute-start | bytes 3145736 | tf_op jit(solution)/shard_map/ppermute | solution.py:264
  217.5 35.7 %collective-permute-start.7 = (bf16[256,2048]{1,0:T(8,128)(2,1)}, bf16[256,2048]{1,0:T(8,128)(2,1)}, u32[]{:S(2)}, u32[]{:S(2)}) collective-permute-start(bf16[256,2048]{1,0:T(8,128)(2,1)} %add_convert_fusion.9), channel_id=1, source_target_pairs={{4,8},{10,6},{5,9},{11,7},{20,24},{26,22},{21,25},{27,23}} | collective-permute-start | bytes 3145736 | tf_op jit(solution)/shard_map/ppermute | solution.py:264
  229.4 2.4 copy-start.6
  231.7 25.4 %collective-permute-start.18 = (bf16[256,2048]{1,0:T(8,128)(2,1)S(1)}, bf16[256,2048]{1,0:T(8,128)(2,1)S(1)}, u32[]{:S(2)}, u32[]{:S(2)}) collective-permute-start(bf16[256,2048]{1,0:T(8,128)(2,1)S(1)} %get-tuple-element.50), channel_id=1, source_target_pairs={{0,4},{12,8},{2,6},{14,10},{1,5},{13,9},{3,7},{15,11},{16,20},{28,... | collective-permute-start | bytes 3145736 | tf_op jit(solution)/shard_map/ppermute | solution.py:264
  235.5 3.9 %copy-start.19 = (s32[8]{0:T(128)S(1)}, s32[8]{0:T(128)}, u32[]{:S(2)}) copy-start(s32[8]{0:T(128)} %constant.95.clone) | copy-start | bytes 100
  235.5 5.2 %copy-start.18 = (s32[8]{0:T(128)S(1)}, s32[8]{0:T(128)}, u32[]{:S(2)}) copy-start(s32[8]{0:T(128)} %constant.94.clone) | copy-start | bytes 100
  235.5 6.6 %copy-start.17 = (s32[8]{0:T(128)S(1)}, s32[8]{0:T(128)}, u32[]{:S(2)}) copy-start(s32[8]{0:T(128)} %constant.98.clone) | copy-start | bytes 100
  235.5 8.0 %copy-start.16 = (s32[8]{0:T(128)S(1)}, s32[8]{0:T(128)}, u32[]{:S(2)}) copy-start(s32[8]{0:T(128)} %constant.97.clone) | copy-start | bytes 100
  235.5 9.3 %copy-start.15 = (s32[8]{0:T(128)S(1)}, s32[8]{0:T(128)}, u32[]{:S(2)}) copy-start(s32[8]{0:T(128)} %constant.96.clone) | copy-start | bytes 100
  238.1 27.4 %collective-permute-start.17 = (bf16[256,2048]{1,0:T(8,128)(2,1)}, bf16[256,2048]{1,0:T(8,128)(2,1)}, u32[]{:S(2)}, u32[]{:S(2)}) collective-permute-start(bf16[256,2048]{1,0:T(8,128)(2,1)} %add_convert_fusion.5), channel_id=1, source_target_pairs={{4,8},{10,6},{5,9},{11,7},{20,24},{26,22},{21,25},{27,23}} | collective-permute-start | bytes 3145736 | tf_op jit(solution)/shard_map/ppermute | solution.py:264
  246.0 30.2 %collective-permute-start.20 = (bf16[256,2048]{1,0:T(8,128)(2,1)}, bf16[256,2048]{1,0:T(8,128)(2,1)S(1)}, u32[]{:S(2)}, u32[]{:S(2)}) collective-permute-start(bf16[256,2048]{1,0:T(8,128)(2,1)} %add_convert_fusion.6), channel_id=1, source_target_pairs={{8,4},{6,10},{9,5},{7,11},{24,20},{22,26},{25,21},{23,27}} | collective-permute-start | bytes 3145736 | tf_op jit(solution)/shard_map/ppermute | solution.py:264
  252.4 25.1 %collective-permute-start.19 = (bf16[256,2048]{1,0:T(8,128)(2,1)}, bf16[256,2048]{1,0:T(8,128)(2,1)S(1)}, u32[]{:S(2)}, u32[]{:S(2)}) collective-permute-start(bf16[256,2048]{1,0:T(8,128)(2,1)} %get-tuple-element.54), channel_id=1, source_target_pairs={{4,0},{10,14},{5,1},{11,15},{20,16},{26,30},{21,17},{27,31}} | collective-permute-start | bytes 3145736 | tf_op jit(solution)/shard_map/ppermute | solution.py:264
  253.1 42.6 %collective-permute-start.16 = (bf16[256,2048]{1,0:T(8,128)(2,1)}, bf16[256,2048]{1,0:T(8,128)(2,1)S(1)}, u32[]{:S(2)}, u32[]{:S(2)}) collective-permute-start(bf16[256,2048]{1,0:T(8,128)(2,1)} %add_convert_fusion.10), channel_id=1, source_target_pairs={{8,4},{6,10},{9,5},{7,11},{24,20},{22,26},{25,21},{23,27}} | collective-permute-start | bytes 3145736 | tf_op jit(solution)/shard_map/ppermute | solution.py:264
  257.2 9.2 %copy-start.5 = (f32[512,2048]{1,0:T(8,128)S(1)}, f32[512,2048]{1,0:T(8,128)}, u32[]{:S(2)}) copy-start(f32[512,2048]{1,0:T(8,128)} %copy-done.4) | copy-start | bytes 12582916
  257.2 44.0 %collective-permute-start.21 = (bf16[256,2048]{1,0:T(8,128)(2,1)}, bf16[256,2048]{1,0:T(8,128)(2,1)S(1)}, u32[]{:S(2)}, u32[]{:S(2)}) collective-permute-start(bf16[256,2048]{1,0:T(8,128)(2,1)} %get-tuple-element.49), channel_id=1, source_target_pairs={{0,4},{12,8},{2,6},{14,10},{1,5},{13,9},{3,7},{15,11},{16,20},{28,... | collective-permute-start | bytes 3145736 | tf_op jit(solution)/shard_map/ppermute | solution.py:264
  265.5 14.3 %copy-start.3 = (f32[512,2048]{1,0:T(8,128)S(1)}, f32[512,2048]{1,0:T(8,128)}, u32[]{:S(2)}) copy-start(f32[512,2048]{1,0:T(8,128)} %copy-done.2) | copy-start | bytes 12582916
  265.5 32.5 %collective-permute-start.15 = (bf16[256,2048]{1,0:T(8,128)(2,1)}, bf16[256,2048]{1,0:T(8,128)(2,1)S(1)}, u32[]{:S(2)}, u32[]{:S(2)}) collective-permute-start(bf16[256,2048]{1,0:T(8,128)(2,1)} %get-tuple-element.53), channel_id=1, source_target_pairs={{4,0},{10,14},{5,1},{11,15},{20,16},{26,30},{21,17},{27,31}} | collective-permute-start | bytes 3145736 | tf_op jit(solution)/shard_map/ppermute | solution.py:264
  276.2 58.5 %collective-permute-start.23 = (bf16[256,2048]{1,0:T(8,128)(2,1)}, bf16[256,2048]{1,0:T(8,128)(2,1)}, u32[]{:S(2)}, u32[]{:S(2)}) collective-permute-start(bf16[256,2048]{1,0:T(8,128)(2,1)} %add_convert_fusion.2), channel_id=1, source_target_pairs={{4,8},{10,6},{5,9},{11,7},{20,24},{26,22},{21,25},{27,23}} | collective-permute-start | bytes 3145736 | tf_op jit(solution)/shard_map/ppermute | solution.py:264
  277.5 57.2 %collective-permute-start.22 = (bf16[256,2048]{1,0:T(8,128)(2,1)}, bf16[256,2048]{1,0:T(8,128)(2,1)}, u32[]{:S(2)}, u32[]{:S(2)}) collective-permute-start(bf16[256,2048]{1,0:T(8,128)(2,1)} %get-tuple-element.51), channel_id=1, source_target_pairs={{8,12},{6,2},{9,13},{7,3},{24,28},{22,18},{25,29},{23,19}} | collective-permute-start | bytes 3145736 | tf_op jit(solution)/shard_map/ppermute | solution.py:264
  279.8 18.1 %copy-start.14 = (bf16[256,2048]{1,0:T(8,128)(2,1)S(1)}, bf16[256,2048]{1,0:T(8,128)(2,1)}, u32[]{:S(2)}) copy-start(bf16[256,2048]{1,0:T(8,128)(2,1)} %copy-done.13) | copy-start | bytes 3145732
  295.7 44.0 %collective-permute-start.24 = (bf16[256,2048]{1,0:T(8,128)(2,1)}, bf16[256,2048]{1,0:T(8,128)(2,1)}, u32[]{:S(2)}, u32[]{:S(2)}) collective-permute-start(bf16[256,2048]{1,0:T(8,128)(2,1)} %get-tuple-element.52), channel_id=1, source_target_pairs={{8,12},{6,2},{9,13},{7,3},{24,28},{22,18},{25,29},{23,19}} | collective-permute-start | bytes 3145736 | tf_op jit(solution)/shard_map/ppermute | solution.py:264
  298.7 3.7 %copy-start.7 = (f32[512,2048]{1,0:T(8,128)S(1)}, f32[512,2048]{1,0:T(8,128)}, u32[]{:S(2)}) copy-start(f32[512,2048]{1,0:T(8,128)} %copy-done.6) | copy-start | bytes 12582916
  302.4 1.4 copy-start.11
  303.8 35.9 %collective-permute-start.25 = (bf16[256,2048]{1,0:T(8,128)(2,1)}, bf16[256,2048]{1,0:T(8,128)(2,1)}, u32[]{:S(2)}, u32[]{:S(2)}) collective-permute-start(bf16[256,2048]{1,0:T(8,128)(2,1)} %add_convert_fusion), channel_id=1, source_target_pairs={{4,8},{10,6},{5,9},{11,7},{20,24},{26,22},{21,25},{27,23}} | collective-permute-start | bytes 3145736 | tf_op jit(solution)/shard_map/ppermute | solution.py:264
  334.7 4.9 %copy-start.8 = (f32[512,2048]{1,0:T(8,128)S(1)}, f32[512,2048]{1,0:T(8,128)}, u32[]{:S(2)}) copy-start(f32[512,2048]{1,0:T(8,128)} %copy-done.6) | copy-start | bytes 12582916
  334.7 4.9 %copy-start.12 = (bf16[256,2048]{1,0:T(8,128)(2,1)S(1)}, bf16[256,2048]{1,0:T(8,128)(2,1)}, u32[]{:S(2)}) copy-start(bf16[256,2048]{1,0:T(8,128)(2,1)} %copy-done.11) | copy-start | bytes 3145732
  (1 other events, 0.7 us)

commit v2 on v1

--- a/solution.py
+++ b/solution.py
@@ -9,6 +9,7 @@
 
 GROUP = 4
 VMEM_LIMIT = 40 * 1024 * 1024
+COST = 1024
 
 
 def transform_kernel(columns, counts, x_ref, *refs, parts):
@@ -69,7 +70,6 @@
     part_rows, width = coeff_parts[0].shape
     parts = len(coeff_parts)
     together = next(t for t in (4, 2, 1) if blocks % t == 0)
-    flops = 2 * functions * blocks * slots * side * side * width
     return pl.pallas_call(
         functools.partial(transform_kernel, parts=parts),
         grid_spec=pltpu.PrefetchScalarGridSpec(
@@ -88,42 +88,44 @@
         ),
         out_shape=jax.ShapeDtypeStruct((blocks * side, functions * width), jnp.bfloat16),
         compiler_params=pltpu.CompilerParams(vmem_limit_bytes=VMEM_LIMIT),
-        cost_estimate=pl.CostEstimate(flops=flops, bytes_accessed=three_index.size * 2, transcendentals=0),
+        cost_estimate=pl.CostEstimate(flops=COST, bytes_accessed=COST, transcendentals=0),
     )(columns, counts, three_index, *coeff_parts)
 
 
-def product_kernel(index, *refs, parts):
-    out_ref = refs[-1]
+def product_kernel(index, *refs, parts, pieces):
+    out_ref, piece_refs = refs[2 * parts], refs[2 * parts + 1 :]
     total = None
-    for rows_ref, cols_ref in zip(refs[:parts], refs[parts:-1]):
+    for rows_ref, cols_ref in zip(refs[:parts], refs[parts : 2 * parts]):
         term = lax.dot_general(
             rows_ref[0], cols_ref[...], (((1,), (1,)), ((), ())), preferred_element_type=jnp.float32
         )
         total = term if total is None else total + term
     out_ref[...] = total
-
-
-def row_product(index, rows, cols):
+    for c, ref in enumerate(piece_refs):
+        ref[...] = total[c * ref.shape[0] : (c + 1) * ref.shape[0]].astype(ref.dtype)
+
+
+def row_product(index, rows, cols, pieces):
     parts = len(rows)
     height, depth = rows[0].shape[1:]
     length = cols[0].shape[0]
     tile = min(length, 512)
     return pl.pallas_call(
-        functools.partial(product_kernel, parts=parts),
+        functools.partial(product_kernel, parts=parts, pieces=pieces),
         grid_spec=pltpu.PrefetchScalarGridSpec(
             num_scalar_prefetch=1,
             grid=(length // tile,),
-            in_specs=[pl.BlockSpec((1, height, depth), lambda c, index: (index[0], 0, 0))] * parts
+            in_specs=[
+                pl.BlockSpec((1, height, depth), lambda c, index, t=t: (index[t], 0, 0)) for t in range(parts)
+            ]
             + [pl.BlockSpec((tile, depth), lambda c, index: (c, 0))] * parts,
-            out_specs=pl.BlockSpec((height, tile), lambda c, index: (0, c)),
+            out_specs=[pl.BlockSpec((height, tile), lambda c, index: (0, c))]
+            + [pl.BlockSpec((height // pieces, tile), lambda c, index: (0, c))] * pieces,
         ),
-        out_shape=jax.ShapeDtypeStruct((height, length), jnp.float32),
+        out_shape=[jax.ShapeDtypeStruct((height, length), jnp.float32)]
+        + [jax.ShapeDtypeStruct((height // pieces, length), jnp.bfloat16)] * pieces,
         compiler_params=pltpu.CompilerParams(vmem_limit_bytes=VMEM_LIMIT),
-        cost_estimate=pl.CostEstimate(
-            flops=2 * height * length * depth * parts,
-            bytes_accessed=parts * 2 * depth * (height + length) + 4 * height * length,
-            transcendentals=0,
-        ),
+        cost_estimate=pl.CostEstimate(flops=COST, bytes_accessed=COST, transcendentals=0),
     )(index, *rows, *cols)
 
 
@@ -173,6 +175,20 @@
     return value if earlier is None else lax.optimization_barrier((value, earlier))[0]
 
 
+def total_over(axis, size, value):
+    if size & (size - 1):
+        return lax.psum(value, axis)
+    if size <= 4:
+        return value + sum(
+            lax.ppermute(value, axis, [(i, (i + shift) % size) for i in range(size)]) for shift in range(1, size)
+        )
+    shift = 1
+    while shift < size:
+        value = value + lax.ppermute(value, axis, [(i, (i + shift) % size) for i in range(size)])
+        shift *= 2
+    return value
+
+
 def shards(mesh, three_index, block_cols, live_count, coefficients):
     aux, orb, sub = mesh.shape["aux"], mesh.shape["orb"], mesh.shape["sub"]
     z, o, s = lax.axis_index("aux"), lax.axis_index("orb"), lax.axis_index("sub")
@@ -189,100 +205,96 @@
     own = transform(three_index, columns, live_count[0], coeff_parts)
     length, depth = own.shape
     height = length // (owned * sub)
-    chunks = max(1, height // 256)
-    piece = height // chunks
+    pieces = [1] + [max(1, height // 256)] * (orb - 1)
+    beats = pieces[-1]
 
     cols = [own]
     for t in range(1, sub):
         cols.append(lax.ppermute(own, "sub", [((u + t) % sub, u) for u in range(sub)]))
     views = [c.reshape(owned * sub, height, depth) for c in cols]
-
-    came_rows, last = {}, None
+    halves = total_over("aux", aux, jnp.sum(jnp.square(own.astype(jnp.float32)), axis=1))
+    diagonal = total_over("sub", sub, halves)
+
+    came_rows = {}
     for k in range(1, orb):
         for q in range(owned):
             table = [line.order(k, (b - k) % orb, a)[q] % owned for a in range(aux) for b in range(orb)]
-            mine = after(lookup(table, place), last)
-            came_rows[k, q] = []
-            for t in range(sub):
-                sent = lax.dynamic_slice_in_dim(views[0], mine * sub + lax.rem(s - t + sub, sub), 1, 0)
-                pairs = [
-                    (((b + k) % orb) * sub + (c + t) % sub, b * sub + c) for b in range(orb) for c in range(sub)
-                ]
-                came_rows[k, q].append(lax.ppermute(sent, ("orb", "sub"), pairs))
-                last = sent
-
-    squares = jnp.sum(jnp.square(after(own, last).astype(jnp.float32)), axis=1)
-    diagonal = jnp.sum(lax.all_gather(squares, ("aux", "sub")), axis=0)
+            block = lookup(table, place) * sub + s
+            message = jnp.concatenate([lax.dynamic_slice_in_dim(view, block, 1, 0) for view in views])
+            pairs = [((b + k) % orb, b) for b in range(orb)]
+            came_rows[k, q] = lax.ppermute(message, "orb", pairs)
 
     events = []
     for k in range(orb):
-        base = owned * k - 1 if k else 0
+        base = (owned * k - 1 if k else 0) * beats
+        wide = beats // pieces[k]
+        ready = [base + q * beats - 0.5 if k else 0.25 * q - 1 for q in range(owned)]
         for q in range(owned):
-            events.append((((base + q) * chunks - 0.5) if k or q else -1.0, 0, "product", k, q, 0, 0))
-        finals = {c: [] for c in range(chunks)}
+            events.append((ready[q], 0, "product", k, q, 0, 0))
+        finals = {c: [] for c in range(pieces[k])}
         for rank in range(owned):
             for step in range(aux - 1):
                 pairs, _, final = line.hop(k, rank, step)
                 if not pairs:
                     continue
-                for c in range(chunks):
-                    when = (base + rank) * chunks + c + step
-                    events.append((when, step, "hop", k, rank, step, c))
+                for c in range(pieces[k]):
+                    when = base + rank * beats + (c + step) * wide
+                    events.append((when if step else ready[rank] + 0.1, step, "hop", k, rank, step, c))
                     if final:
-                        finals[c].append((when + 1.5, rank, step))
-        for c in range(chunks):
+                        finals[c].append((when + wide + 0.5, rank, step))
+        for c in range(pieces[k]):
             events.append((max(f[0] for f in finals[c]), 0, "fold", k, c, [f[1:] for f in finals[c]], 0))
     events.sort(key=lambda e: e[:2])
 
-    sums, came, result, last = {}, {}, None, squares
+    sums, heads, came, result, last = {}, {}, {}, None, halves
     for _, _, kind, k, a1, a2, c in events:
+        piece = height // pieces[k]
         if kind == "product":
             q = a1
             if k == 0:
                 table = [line.order(k, b, a)[q] % owned for a in range(aux) for b in range(orb)]
-                index = (lookup(table, place) * sub + s)[None]
+                index = jnp.broadcast_to(lookup(table, place) * sub + s, (sub,))
                 rows = views
             else:
-                index = jnp.zeros((1,), jnp.int32)
-                rows = came_rows[k, q]
-            sums[k, q] = row_product(after(index, last), rows, cols)
+                index = jnp.arange(sub, dtype=jnp.int32)
+                rows = [came_rows[k, q]] * sub
+            sums[k, q], *heads[k, q] = row_product(after(index, last), rows, cols, pieces[k])
             last = sums[k, q]
         elif kind == "hop":
             rank, step = a1, a2
             pairs, position, final = line.hop(k, rank, step)
             used = sorted(set(position.values()))
-            arrived = came.get((k, rank, step - 1, c))
-            if arrived is not None:
-                arrived = after(arrived, last)
-            value = sums[k, used[0]][c * piece : (c + 1) * piece]
-            for q in used[1:]:
-                flag = lookup([position.get(i) == q for i in range(aux * orb)], place)
-                value = jnp.where(flag > 0, sums[k, q][c * piece : (c + 1) * piece], value)
-            if arrived is not None:
-                value = value + arrived.astype(jnp.float32)
-            last = value.astype(jnp.bfloat16)
-            came[k, rank, step, c] = lax.ppermute(last, ("aux", "orb"), pairs)
+            if step == 0 and len(used) == 1:
+                value = heads[k, used[0]][c]
+            else:
+                value = sums[k, used[0]][c * piece : (c + 1) * piece]
+                for q in used[1:]:
+                    flag = lookup([position.get(i) == q for i in range(aux * orb)], place)
+                    value = jnp.where(flag > 0, sums[k, q][c * piece : (c + 1) * piece], value)
+                if step:
+                    value = value + after(came[k, rank, step - 1, c], last).astype(jnp.float32)
+                value = value.astype(jnp.bfloat16)
+                last = value
+            came[k, rank, step, c] = lax.ppermute(value, ("aux", "orb"), pairs)
         else:
             at, terms = a1, a2
-            if result is None:
-                result = jnp.zeros((height, length), jnp.float32)
             flag = lookup([z_ in line.targets(k, o_) for z_ in range(aux) for o_ in range(orb)], place)
             rows = slice(at * piece, (at + 1) * piece)
             total = jnp.where(flag > 0, after(sums[k, owned - 1], last)[rows], 0.0)
-            if k:
-                total = total + result[rows]
             for rank, step in terms:
                 final = line.hop(k, rank, step)[2]
                 flag = lookup([i in final for i in range(aux * orb)], place)
                 total = total + jnp.where(flag > 0, came[k, rank, step, at].astype(jnp.float32), 0.0)
-            if k == orb - 1:
-                start = lax.rem(z, owned) * sub * height + s * height + at * piece
+            if k == 0:
+                start = lax.rem(z, owned) * sub * height + s * height
                 local = lax.div(z, owned) == o
                 row = lax.broadcasted_iota(jnp.int32, total.shape, 0) + start
                 col = lax.broadcasted_iota(jnp.int32, total.shape, 1)
-                exact = lax.dynamic_slice_in_dim(diagonal, start, piece)
+                exact = lax.dynamic_slice_in_dim(diagonal, start, height)
                 total = jnp.where((row == col) & local, exact[:, None], total)
-            result = lax.dynamic_update_slice(result, total, (at * piece, 0))
+                result = total
+            else:
+                result = lax.dynamic_update_slice(result, result[rows] + total, (at * piece, 0))
             last = result
     return result
 

time: 348 us -> 292 us (0.84)
  blocking collectives: 29.5 us -> 0 us
  starting transfers between devices: 55.3 us -> 37.1 us
  other arithmetic: 40.3 us -> 28.3 us
  Pallas kernels: 42.5 us -> 48.7 us
  local copies, waits for them, and re-layouts: 19.7 us -> 14.9 us
    all_gather x1 -> x0, blocking collectives: 29.5 us -> none  [shards(): diagonal = jnp.sum(lax.all_gather(squares, ('aux', 'sub')), axis=0)]
    ppermute x24 -> x21, starting transfers between devices: 53.7 us -> 35.5 us  [the longest x15 22.5 us: shards(): came[k, rank, step, c] = lax.ppermute(value, ('aux', 'orb'), pairs)]
    convert_element_type x11 -> x10, other arithmetic: 22.8 us -> 13.7 us  [shards(): value = value.astype(jnp.bfloat16)]
    dynamic_update_slice x3 -> x2, other arithmetic: 12.2 us -> 5.16 us  [shards(): lax.dynamic_update_slice(result, result[rows] + total, (at * piece, 0))]
    pallas_call x4, Pallas kernels: 30.6 us -> 37 us  [row_product(): pl.pallas_call(functools.partial(product_kernel, parts=parts, pieces=piec...]
    select_n x0 -> x1, other arithmetic: none -> 3.8 us  [shards(): total = jnp.where((row == col) & local, exact[:, None], total)]
    unnamed x46 -> x34, local copies, waits for them, and re-layouts: 7.44 us -> 6.26 us
    ppermute x24 -> x21, waiting for transfers between devices: 105 us -> 106 us  [the longest x15 96.3 us: shards(): came[k, rank, step, c] = lax.ppermute(value, ('aux', 'orb'), pairs)]
  transfers between devices with their start and end apart: 26 -> 23, of which waited for: 9 -> 12; matrix products, arithmetic and copies ran while one was open for 13% -> 11% of each run, Pallas kernels for 6% -> 13%
where the time goes in v2:
time: 292 us; the launch traced here: 289 us
  waiting for transfers between devices  154 us (53%)
  Pallas kernels  48.7 us (17%)
  starting transfers between devices  37.1 us (13%)
  other arithmetic  28.3 us (10%)
  local copies, waits for them, and re-layouts  14.9 us (5%)
  between operations  5.73 us (2%)
    ppermute x15, waiting for transfers between devices, shards(): came[k, rank, step, c] = lax.ppermute(value, ('aux', 'orb'), pairs)  96.3 us
    ppermute x1, waiting for transfers between devices, shards(): lax.ppermute(coefficients, 'orb', [((t + k) % orb, t) for t in range(orb)])  45.4 us
    pallas_call x4, Pallas kernels, row_product(): pl.pallas_call(functools.partial(product_kernel, parts=parts, pieces=piec...  37 us
    ppermute x15, starting transfers between devices, shards(): came[k, rank, step, c] = lax.ppermute(value, ('aux', 'orb'), pairs)  22.5 us
    convert_element_type x10, other arithmetic, shards(): value = value.astype(jnp.bfloat16)  13.7 us
    pallas_call x1, Pallas kernels, transform(): pl.pallas_call(functools.partial(transform_kernel, parts=parts), grid_spe...  11.7 us
    ppermute x4, starting transfers between devices, total_over(): lax.ppermute(value, axis, [(i, (i + shift) % size) for i in range(size)])  10.7 us
    ppermute x2, waiting for transfers between devices, shards(): came_rows[k, q] = lax.ppermute(message, 'orb', pairs)  6.42 us
  transfers between devices with their start and end apart: 23, of which 12 were waited for; matrix products, arithmetic and copies ran while one was open for 11% of the time, Pallas kernels for 13%

profile of v2, /device:TPU:20, one launch (start us, length us, event | category | flops | bytes accessed | tf_op | source)
XLA Modules:
  0.0 288.8 jit_solution(13513315134058327749)
XLA Ops:
  0.0 1.5 collective-permute-start
  2.2 45.4 %collective-permute-done.refs_1_ = bf16[2048,512]{1,0:T(8,128)(2,1)S(1)} collective-permute-done((bf16[2048,512]{1,0:T(8,128)(2,1)}, bf16[2048,512]{1,0:T(8,128)(2,1)S(1)}, u32[]{:S(2)}, u32[]{:S(2)}) %collective-permute-start) | collective-permute-done | bytes 2097184 | tf_op jit(solution)/shard_map/ppermute | solution.py:202
  47.6 1.6 copy-done.6
  49.8 11.7 %shard_map.208.refs_2_ = bf16[2048,1024]{1,0:T(8,128)(2,1)} custom-call(s32[16,16]{1,0:T(8,128)S(1)} %negate_select_fusion.columns, s32[16]{0:T(128)S(1)} %bitcast.13, bf16[2,16,16,128,128]{4,3,2,1,0:T(8,128)(2,1)} %x_ref.1, bf16[2048,512]{1,0:T(8,128)(2,1)S(1)} %copy-done.6, bf16[2048,512]{1,0:T(8,128)(2,1)S(1)} %collective-permute-done.refs_1_), custom_call_target="tpu_custom_call" | custom-call | flops 1024 | bytes 1024 | tf_op jit(solution)/shard_map/pallas_call | solution.py:73
  64.4 1.7 constant_dynamic-slice_fusion.1
  66.2 3.0 %collective-permute-done.5.refs_3_ = bf16[2048,1024]{1,0:T(8,128)(2,1)} collective-permute-done((bf16[2048,1024]{1,0:T(8,128)(2,1)}, bf16[2048,1024]{1,0:T(8,128)(2,1)}, u32[]{:S(2)}, u32[]{:S(2)}) %collective-permute-start.5) | collective-permute-done | bytes 4194336 | tf_op jit(solution)/shard_map/ppermute | solution.py:213
  69.1 1.7 constant_dynamic-slice_fusion
  71.1 1.7 collective-permute-start.6
  72.7 3.1 %multiply_reduce_fusion = f32[2048]{0:T(1024)S(1)} fusion(bf16[2048,1024]{1,0:T(8,128)(2,1)} %shard_map.208.refs_2_), kind=kLoop, calls=%fused_computation | loop fusion | flops 6289408 | bytes 4202496 | tf_op jit(solution)/shard_map/reduce_sum | solution.py:215
  75.8 9.0 %collective-permute-start.3 = (f32[2048]{0:T(1024)S(1)}, f32[2048]{0:T(1024)S(1)}, u32[]{:S(2)}, u32[]{:S(2)}) collective-permute-start(f32[2048]{0:T(1024)S(1)} %multiply_reduce_fusion), channel_id=1, source_target_pairs={{0,12},{4,0},{8,4},{12,8},{1,13},{5,1},{9,5},{13,9},{2,14},{6,2},{... | collective-permute-start | bytes 24584 | tf_op jit(solution)/shard_map/ppermute | solution.py:183
  84.9 1.5 collective-permute-start.1
  86.4 3.0 %collective-permute-done.2 = f32[2048]{0:T(1024)S(1)} collective-permute-done((f32[2048]{0:T(1024)S(1)}, f32[2048]{0:T(1024)S(1)}, u32[]{:S(2)}, u32[]{:S(2)}) %collective-permute-start.2) | collective-permute-done | bytes 8224 | tf_op jit(solution)/shard_map/ppermute | solution.py:183
  89.4 10.0 %shard_map.209 = (f32[512,2048]{1,0:T(8,128)S(1)}, bf16[512,2048]{1,0:T(8,128)(2,1)}) custom-call(s32[2]{0:T(128)S(1)} %broadcast_in_dim.35.index, bf16[4,512,1024]{2,1,0:T(8,128)(2,1)} %bitcast.5.refs_0_, bf16[4,512,1024]{2,1,0:T(8,128)(2,1)} %bitcast.6.refs_1_, bf16[2048,1024]{1,0:T(8,128)(2,1)} %shard_map.208.refs_2_, ...), custom_call_target="tpu_custom_call" | custom-call | flops 1024 | bytes 1024 | tf_op jit(solution)/shard_map/pallas_call | solution.py:113
  99.4 1.3 collective-permute-start.8
  100.7 1.6 pad_maximum_fusion.1
  102.9 9.5 %shard_map.210 = (f32[512,2048]{1,0:T(8,128)S(1)}, bf16[512,2048]{1,0:T(8,128)(2,1)}) custom-call(s32[2]{0:T(128)S(1)} %broadcast_in_dim.34.index, bf16[4,512,1024]{2,1,0:T(8,128)(2,1)} %bitcast.5.refs_0_, bf16[4,512,1024]{2,1,0:T(8,128)(2,1)} %bitcast.6.refs_1_, bf16[2048,1024]{1,0:T(8,128)(2,1)} %shard_map.208.refs_2_, ...), custom_call_target="tpu_custom_call" | custom-call | flops 1024 | bytes 1024 | tf_op jit(solution)/shard_map/pallas_call | solution.py:113
  112.4 2.0 copy-done.2
  114.5 5.1 %collective-permute-done.6.refs_0_.refs_1_ = bf16[2,512,1024]{2,1,0:T(8,128)(2,1)S(1)} collective-permute-done((bf16[2,512,1024]{2,1,0:T(8,128)(2,1)S(1)}, bf16[2,512,1024]{2,1,0:T(8,128)(2,1)S(1)}, u32[]{:S(2)}, u32[]{:S(2)}) %collective-permute-start.6) | collective-permute-done | bytes 2097184 | tf_op jit(solution)/shard_map/ppermute | solution.py:225
  119.6 8.7 %shard_map.211 = (f32[512,2048]{1,0:T(8,128)S(1)}, bf16[256,2048]{1,0:T(8,128)(2,1)}, bf16[256,2048]{1,0:T(8,128)(2,1)S(1)}) custom-call(s32[2]{0:T(128)S(1)} %iota.21.index, bf16[2,512,1024]{2,1,0:T(8,128)(2,1)S(1)} %collective-permute-done.6.refs_0_.refs_1_, bf16[2,512,1024]{2,1,0:T(8,128)(2,1)S(1)} %collective-permute-done.6.refs_0_.refs_1_, ...), custom_call_target="tpu_custom_call" | custom-call | flops 1024 | bytes 1024 | tf_op jit(solution)/shard_map/pallas_call | solution.py:113
  128.3 1.9 copy-done
  130.2 1.6 collective-permute-start.7
  131.8 1.3 collective-permute-start.12
  141.0 9.1 %collective-permute-done.8 = bf16[512,2048]{1,0:T(8,128)(2,1)} collective-permute-done((bf16[512,2048]{1,0:T(8,128)(2,1)}, bf16[512,2048]{1,0:T(8,128)(2,1)}, u32[]{:S(2)}, u32[]{:S(2)}) %collective-permute-start.8) | collective-permute-done | bytes 2097184 | tf_op jit(solution)/shard_map/ppermute | solution.py:278
  150.2 1.8 collective-permute-start.11
  151.9 3.6 %add_convert_fusion.2 = bf16[512,2048]{1,0:T(8,128)(2,1)S(1)} fusion(f32[512,2048]{1,0:T(8,128)} %copy-done.4, bf16[512,2048]{1,0:T(8,128)(2,1)} %collective-permute-done.8), kind=kLoop, calls=%fused_computation.4 | loop fusion | flops 3145728 | bytes 8388608 | tf_op jit(solution)/shard_map/convert_element_type | solution.py:276
  155.5 3.1 %collective-permute-start.16 = (bf16[512,2048]{1,0:T(8,128)(2,1)S(1)}, bf16[512,2048]{1,0:T(8,128)(2,1)S(1)}, u32[]{:S(2)}, u32[]{:S(2)}) collective-permute-start(bf16[512,2048]{1,0:T(8,128)(2,1)S(1)} %add_convert_fusion.2), channel_id=1, source_target_pairs={{8,4},{6,10},{9,5},{7,11},{24,20},{22,26},{25,21},{23,27}} | collective-permute-start | bytes 6291464 | tf_op jit(solution)/shard_map/ppermute | solution.py:278
  158.6 2.5 add_convert_fusion.8
  162.5 1.3 collective-permute-done.9.refs_0_.refs_1_
  163.7 8.9 %shard_map.212 = (f32[512,2048]{1,0:T(8,128)S(1)}, bf16[256,2048]{1,0:T(8,128)(2,1)}, bf16[256,2048]{1,0:T(8,128)(2,1)}) custom-call(s32[2]{0:T(128)S(1)} %iota.20.index, bf16[2,512,1024]{2,1,0:T(8,128)(2,1)S(1)} %collective-permute-done.9.refs_0_.refs_1_, bf16[2,512,1024]{2,1,0:T(8,128)(2,1)S(1)} %collective-permute-done.9.refs_0_.refs_1_, ...), custom_call_target="tpu_custom_call" | custom-call | flops 1024 | bytes 1024 | tf_op jit(solution)/shard_map/pallas_call | solution.py:113
  173.0 1.7 collective-permute-start.10
  174.7 20.4 %collective-permute-done.12 = bf16[512,2048]{1,0:T(8,128)(2,1)} collective-permute-done((bf16[512,2048]{1,0:T(8,128)(2,1)}, bf16[512,2048]{1,0:T(8,128)(2,1)}, u32[]{:S(2)}, u32[]{:S(2)}) %collective-permute-start.12) | collective-permute-done | bytes 2097184 | tf_op jit(solution)/shard_map/ppermute | solution.py:278
  195.1 2.4 add_convert_fusion.1
  197.5 1.7 collective-permute-start.18
  199.2 1.6 add_convert_fusion.7
  200.8 1.3 collective-permute-start.13
  202.1 2.4 collective-permute-done.16
  207.3 1.6 add_convert_fusion.6
  208.9 27.9 %collective-permute-done.14 = bf16[256,2048]{1,0:T(8,128)(2,1)S(1)} collective-permute-done((bf16[256,2048]{1,0:T(8,128)(2,1)S(1)}, bf16[256,2048]{1,0:T(8,128)(2,1)S(1)}, u32[]{:S(2)}, u32[]{:S(2)}) %collective-permute-start.14) | collective-permute-done | bytes 1048608 | tf_op jit(solution)/shard_map/ppermute | solution.py:278
  236.8 1.5 collective-permute-start.19
  238.7 1.3 collective-permute-start.20
  240.6 1.3 collective-permute-start.22
  241.9 6.7 %collective-permute-done.18 = bf16[512,2048]{1,0:T(8,128)(2,1)S(1)} collective-permute-done((bf16[512,2048]{1,0:T(8,128)(2,1)S(1)}, bf16[512,2048]{1,0:T(8,128)(2,1)S(1)}, u32[]{:S(2)}, u32[]{:S(2)}) %collective-permute-start.18) | collective-permute-done | bytes 2097184 | tf_op jit(solution)/shard_map/ppermute | solution.py:278
  248.6 1.3 collective-permute-start.21
  250.0 3.8 %add_select_fusion = f32[512,2048]{1,0:T(8,128)S(1)} fusion(bf16[512,2048]{1,0:T(8,128)(2,1)S(1)} %collective-permute-done.18, bf16[512,2048]{1,0:T(8,128)(2,1)S(1)} %collective-permute-done.17, bf16[512,2048]{1,0:T(8,128)(2,1)} %collective-permute-done.8, f32[512,2048]{1,0:T(8,128)S(1)} %copy-done.3, f32[512]{0:T(512)S(1)} %dynamic-slice_add_fusion, ...), kind=kLoop, calls=%fused_computation.1 | loop fusion | flops 13631488 | bytes 14684164 | tf_op jit(solution)/shard_map/jit(_where)/select_n | solution.py:294
  253.8 12.9 %collective-permute-done.20 = bf16[256,2048]{1,0:T(8,128)(2,1)S(1)} collective-permute-done((bf16[256,2048]{1,0:T(8,128)(2,1)S(1)}, bf16[256,2048]{1,0:T(8,128)(2,1)S(1)}, u32[]{:S(2)}, u32[]{:S(2)}) %collective-permute-start.20) | collective-permute-done | bytes 1048608 | tf_op jit(solution)/shard_map/ppermute | solution.py:278
  266.7 1.3 fusion.2
  268.0 16.9 %collective-permute-done.22 = bf16[256,2048]{1,0:T(8,128)(2,1)S(1)} collective-permute-done((bf16[256,2048]{1,0:T(8,128)(2,1)S(1)}, bf16[256,2048]{1,0:T(8,128)(2,1)S(1)}, u32[]{:S(2)}, u32[]{:S(2)}) %collective-permute-start.22) | collective-permute-done | bytes 1048608 | tf_op jit(solution)/shard_map/ppermute | solution.py:278
  285.0 3.8 %fusion.1 = f32[512,2048]{1,0:T(8,128)} fusion(f32[512,2048]{1,0:T(8,128)} %copy-done.8, bf16[256,2048]{1,0:T(8,128)(2,1)S(1)} %collective-permute-done.22, bf16[256,2048]{1,0:T(8,128)(2,1)S(1)} %collective-permute-done.10, bf16[256,2048]{1,0:T(8,128)(2,1)S(1)} %collective-permute-done.21, f32[512,2048]{1,0:T(8,128)S(1)} %get-tuple-element.52, pred[]{:T(512)} %bitcast.11, ...), kind=kLoop, calls=%fused_computation.8 | loop fusion | flops 5767168 | bytes 9438720 | tf_op jit(solution)/shard_map/dynamic_update_slice | solution.py:297
  (71 shorter events, 13.1 us)
Async XLA Ops:
  0.0 47.6 %collective-permute-start = (bf16[2048,512]{1,0:T(8,128)(2,1)}, bf16[2048,512]{1,0:T(8,128)(2,1)S(1)}, u32[]{:S(2)}, u32[]{:S(2)}) collective-permute-start(bf16[2048,512]{1,0:T(8,128)(2,1)} %refs_0_.1), channel_id=1, source_target_pairs={{2,0},{0,2},{3,1},{1,3},{6,4},{4,6},{7,5},{5,7},{10,8},{8,10},{11,... | collective-permute-start | bytes 6291464 | tf_op jit(solution)/shard_map/ppermute | solution.py:202
  47.6 1.6 copy-start.6
  49.2 0.7 copy-start.7
  49.8 11.8 %copy-start.16 = (s32[8]{0:T(128)S(1)}, s32[8]{0:T(128)}, u32[]{:S(2)}) copy-start(s32[8]{0:T(128)} %constant.78.clone) | copy-start | bytes 100
  49.8 13.2 %copy-start.15 = (s32[8]{0:T(128)S(1)}, s32[8]{0:T(128)}, u32[]{:S(2)}) copy-start(s32[8]{0:T(128)} %constant.77.clone) | copy-start | bytes 100
  61.6 7.6 %collective-permute-start.5 = (bf16[2048,1024]{1,0:T(8,128)(2,1)}, bf16[2048,1024]{1,0:T(8,128)(2,1)}, u32[]{:S(2)}, u32[]{:S(2)}) collective-permute-start(bf16[2048,1024]{1,0:T(8,128)(2,1)} %shard_map.208.refs_2_), channel_id=1, source_target_pairs={{1,0},{0,1},{3,2},{2,3},{5,4},{4,5},{7,6},{6,7},{9,8},{8,9},{11,10... | collective-permute-start | bytes 12582920 | tf_op jit(solution)/shard_map/ppermute | solution.py:213
  71.1 48.5 %collective-permute-start.6 = (bf16[2,512,1024]{2,1,0:T(8,128)(2,1)S(1)}, bf16[2,512,1024]{2,1,0:T(8,128)(2,1)S(1)}, u32[]{:S(2)}, u32[]{:S(2)}) collective-permute-start(bf16[2,512,1024]{2,1,0:T(8,128)(2,1)S(1)} %pad_maximum_fusion), channel_id=1, source_target_pairs={{2,0},{0,2},{3,1},{1,3},{6,4},{4,6},{7,5},{5,7},{10,8},{8,10},{11,... | collective-permute-start | bytes 6291464 | tf_op jit(solution)/shard_map/ppermute | solution.py:225
  75.8 10.6 %collective-permute-start.3 = (f32[2048]{0:T(1024)S(1)}, f32[2048]{0:T(1024)S(1)}, u32[]{:S(2)}, u32[]{:S(2)}) collective-permute-start(f32[2048]{0:T(1024)S(1)} %multiply_reduce_fusion), channel_id=1, source_target_pairs={{0,12},{4,0},{8,4},{12,8},{1,13},{5,1},{9,5},{13,9},{2,14},{6,2},{... | collective-permute-start | bytes 24584 | tf_op jit(solution)/shard_map/ppermute | solution.py:183
  84.9 4.5 %collective-permute-start.2 = (f32[2048]{0:T(1024)S(1)}, f32[2048]{0:T(1024)S(1)}, u32[]{:S(2)}, u32[]{:S(2)}) collective-permute-start(f32[2048]{0:T(1024)S(1)} %multiply_reduce_fusion), channel_id=1, source_target_pairs={{0,8},{4,12},{8,0},{12,4},{1,9},{5,13},{9,1},{13,5},{2,10},{6,14},... | collective-permute-start | bytes 24584 | tf_op jit(solution)/shard_map/ppermute | solution.py:183
  84.9 4.5 %collective-permute-start.1 = (f32[2048]{0:T(1024)S(1)}, f32[2048]{0:T(1024)S(1)}, u32[]{:S(2)}, u32[]{:S(2)}) collective-permute-start(f32[2048]{0:T(1024)S(1)} %multiply_reduce_fusion), channel_id=1, source_target_pairs={{0,4},{4,8},{8,12},{12,0},{1,5},{5,9},{9,13},{13,1},{2,6},{6,10},{... | collective-permute-start | bytes 24584 | tf_op jit(solution)/shard_map/ppermute | solution.py:183
  99.4 2.9 copy-start.4
  99.4 50.8 %collective-permute-start.8 = (bf16[512,2048]{1,0:T(8,128)(2,1)}, bf16[512,2048]{1,0:T(8,128)(2,1)}, u32[]{:S(2)}, u32[]{:S(2)}) collective-permute-start(bf16[512,2048]{1,0:T(8,128)(2,1)} %get-tuple-element.36), channel_id=1, source_target_pairs={{0,4},{12,8},{2,6},{14,10},{1,5},{13,9},{3,7},{15,11},{16,20},{28,... | collective-permute-start | bytes 6291464 | tf_op jit(solution)/shard_map/ppermute | solution.py:278
  102.3 61.5 %collective-permute-start.9 = (bf16[2,512,1024]{2,1,0:T(8,128)(2,1)}, bf16[2,512,1024]{2,1,0:T(8,128)(2,1)S(1)}, u32[]{:S(2)}, u32[]{:S(2)}) collective-permute-start(bf16[2,512,1024]{2,1,0:T(8,128)(2,1)} %pad_maximum_fusion.1), channel_id=1, source_target_pairs={{2,0},{0,2},{3,1},{1,3},{6,4},{4,6},{7,5},{5,7},{10,8},{8,10},{11,... | collective-permute-start | bytes 6291464 | tf_op jit(solution)/shard_map/ppermute | solution.py:225
  112.4 2.0 copy-start.2
  114.4 18.8 %copy-start.14 = (s32[8]{0:T(128)S(1)}, s32[8]{0:T(128)}, u32[]{:S(2)}) copy-start(s32[8]{0:T(128)} %constant.84.clone) | copy-start | bytes 100
  114.4 19.5 %copy-start.13 = (s32[8]{0:T(128)S(1)}, s32[8]{0:T(128)}, u32[]{:S(2)}) copy-start(s32[8]{0:T(128)} %constant.83.clone) | copy-start | bytes 100
  114.4 21.5 %copy-start.12 = (s32[8]{0:T(128)S(1)}, s32[8]{0:T(128)}, u32[]{:S(2)}) copy-start(s32[8]{0:T(128)} %constant.82.clone) | copy-start | bytes 100
  114.4 22.6 %copy-start.11 = (s32[8]{0:T(128)S(1)}, s32[8]{0:T(128)}, u32[]{:S(2)}) copy-start(s32[8]{0:T(128)} %constant.81.clone) | copy-start | bytes 100
  114.5 23.9 %copy-start.10 = (s32[8]{0:T(128)S(1)}, s32[8]{0:T(128)}, u32[]{:S(2)}) copy-start(s32[8]{0:T(128)} %constant.80.clone) | copy-start | bytes 100
  114.5 25.2 %copy-start.9 = (s32[8]{0:T(128)S(1)}, s32[8]{0:T(128)}, u32[]{:S(2)}) copy-start(s32[8]{0:T(128)} %constant.79.clone) | copy-start | bytes 100
  128.3 1.9 copy-start
  130.2 28.4 %collective-permute-start.7 = (bf16[256,2048]{1,0:T(8,128)(2,1)}, bf16[256,2048]{1,0:T(8,128)(2,1)}, u32[]{:S(2)}, u32[]{:S(2)}) collective-permute-start(bf16[256,2048]{1,0:T(8,128)(2,1)} %get-tuple-element.35), channel_id=1, source_target_pairs={{0,4},{14,10},{1,5},{15,11},{16,20},{30,26},{17,21},{31,27}} | collective-permute-start | bytes 3145736 | tf_op jit(solution)/shard_map/ppermute | solution.py:278
  131.8 63.3 %collective-permute-start.12 = (bf16[512,2048]{1,0:T(8,128)(2,1)}, bf16[512,2048]{1,0:T(8,128)(2,1)}, u32[]{:S(2)}, u32[]{:S(2)}) collective-permute-start(bf16[512,2048]{1,0:T(8,128)(2,1)} %get-tuple-element.42), channel_id=1, source_target_pairs={{12,8},{2,6},{13,9},{3,7},{28,24},{18,22},{29,25},{19,23}} | collective-permute-start | bytes 6291464 | tf_op jit(solution)/shard_map/ppermute | solution.py:278
  133.1 7.8 %collective-permute-start.4 = (f32[2048]{0:T(1024)S(1)}, f32[2048]{0:T(1024)S(1)}, u32[]{:S(2)}, u32[]{:S(2)}) collective-permute-start(f32[2048]{0:T(1024)S(1)} %add_add_fusion), channel_id=1, source_target_pairs={{0,1},{1,0},{2,3},{3,2},{4,5},{5,4},{6,7},{7,6},{8,9},{9,8},{10,11... | collective-permute-start | bytes 24584 | tf_op jit(solution)/shard_map/ppermute | solution.py:183
  150.2 8.5 %copy-start.1 = (f32[512,2048]{1,0:T(8,128)S(1)}, f32[512,2048]{1,0:T(8,128)}, u32[]{:S(2)}) copy-start(f32[512,2048]{1,0:T(8,128)} %copy-done) | copy-start | bytes 12582916
  150.2 49.0 %collective-permute-start.11 = (bf16[256,2048]{1,0:T(8,128)(2,1)S(1)}, bf16[256,2048]{1,0:T(8,128)(2,1)}, u32[]{:S(2)}, u32[]{:S(2)}) collective-permute-start(bf16[256,2048]{1,0:T(8,128)(2,1)S(1)} %get-tuple-element.41), channel_id=1, source_target_pairs={{0,4},{14,10},{1,5},{15,11},{16,20},{30,26},{17,21},{31,27}} | collective-permute-start | bytes 3145736 | tf_op jit(solution)/shard_map/ppermute | solution.py:278
  155.5 48.9 %collective-permute-start.16 = (bf16[512,2048]{1,0:T(8,128)(2,1)S(1)}, bf16[512,2048]{1,0:T(8,128)(2,1)S(1)}, u32[]{:S(2)}, u32[]{:S(2)}) collective-permute-start(bf16[512,2048]{1,0:T(8,128)(2,1)S(1)} %add_convert_fusion.2), channel_id=1, source_target_pairs={{8,4},{6,10},{9,5},{7,11},{24,20},{22,26},{25,21},{23,27}} | collective-permute-start | bytes 6291464 | tf_op jit(solution)/shard_map/ppermute | solution.py:278
  161.2 45.4 %collective-permute-start.15 = (bf16[256,2048]{1,0:T(8,128)(2,1)}, bf16[256,2048]{1,0:T(8,128)(2,1)}, u32[]{:S(2)}, u32[]{:S(2)}) collective-permute-start(bf16[256,2048]{1,0:T(8,128)(2,1)} %add_convert_fusion.8), channel_id=1, source_target_pairs={{4,8},{10,6},{5,9},{11,7},{20,24},{26,22},{21,25},{27,23}} | collective-permute-start | bytes 3145736 | tf_op jit(solution)/shard_map/ppermute | solution.py:278
  172.6 22.5 %copy-start.3 = (f32[512,2048]{1,0:T(8,128)S(1)}, f32[512,2048]{1,0:T(8,128)}, u32[]{:S(2)}) copy-start(f32[512,2048]{1,0:T(8,128)} %copy-done.2) | copy-start | bytes 12582916
  173.0 67.3 %collective-permute-start.10 = (bf16[256,2048]{1,0:T(8,128)(2,1)S(1)}, bf16[256,2048]{1,0:T(8,128)(2,1)S(1)}, u32[]{:S(2)}, u32[]{:S(2)}) collective-permute-start(bf16[256,2048]{1,0:T(8,128)(2,1)S(1)} %get-tuple-element.54), channel_id=1, source_target_pairs={{0,4},{12,8},{2,6},{14,10},{1,5},{13,9},{3,7},{15,11},{16,20},{28,... | collective-permute-start | bytes 3145736 | tf_op jit(solution)/shard_map/ppermute | solution.py:278
  197.5 8.2 %copy-start.5 = (f32[512,2048]{1,0:T(8,128)S(1)}, f32[512,2048]{1,0:T(8,128)}, u32[]{:S(2)}) copy-start(f32[512,2048]{1,0:T(8,128)} %copy-done.4) | copy-start | bytes 12582916
  197.5 51.1 %collective-permute-start.18 = (bf16[512,2048]{1,0:T(8,128)(2,1)S(1)}, bf16[512,2048]{1,0:T(8,128)(2,1)S(1)}, u32[]{:S(2)}, u32[]{:S(2)}) collective-permute-start(bf16[512,2048]{1,0:T(8,128)(2,1)S(1)} %add_convert_fusion.1), channel_id=1, source_target_pairs={{8,4},{6,10},{9,5},{7,11},{24,20},{22,26},{25,21},{23,27}} | collective-permute-start | bytes 6291464 | tf_op jit(solution)/shard_map/ppermute | solution.py:278
  200.8 37.9 %collective-permute-start.13 = (bf16[256,2048]{1,0:T(8,128)(2,1)S(1)}, bf16[256,2048]{1,0:T(8,128)(2,1)S(1)}, u32[]{:S(2)}, u32[]{:S(2)}) collective-permute-start(bf16[256,2048]{1,0:T(8,128)(2,1)S(1)} %add_convert_fusion.7), channel_id=1, source_target_pairs={{4,8},{10,6},{5,9},{11,7},{20,24},{26,22},{21,25},{27,23}} | collective-permute-start | bytes 3145736 | tf_op jit(solution)/shard_map/ppermute | solution.py:278
  204.4 32.4 %collective-permute-start.14 = (bf16[256,2048]{1,0:T(8,128)(2,1)S(1)}, bf16[256,2048]{1,0:T(8,128)(2,1)S(1)}, u32[]{:S(2)}, u32[]{:S(2)}) collective-permute-start(bf16[256,2048]{1,0:T(8,128)(2,1)S(1)} %get-tuple-element.53), channel_id=1, source_target_pairs={{0,4},{12,8},{2,6},{14,10},{1,5},{13,9},{3,7},{15,11},{16,20},{28,... | collective-permute-start | bytes 3145736 | tf_op jit(solution)/shard_map/ppermute | solution.py:278
  206.5 43.4 %collective-permute-start.17 = (bf16[512,2048]{1,0:T(8,128)(2,1)S(1)}, bf16[512,2048]{1,0:T(8,128)(2,1)S(1)}, u32[]{:S(2)}, u32[]{:S(2)}) collective-permute-start(bf16[512,2048]{1,0:T(8,128)(2,1)S(1)} %add_convert_fusion), channel_id=1, source_target_pairs={{4,0},{10,14},{5,1},{11,15},{20,16},{26,30},{21,17},{27,31}} | collective-permute-start | bytes 6291464 | tf_op jit(solution)/shard_map/ppermute | solution.py:278
  236.8 29.8 %collective-permute-start.19 = (bf16[256,2048]{1,0:T(8,128)(2,1)S(1)}, bf16[256,2048]{1,0:T(8,128)(2,1)S(1)}, u32[]{:S(2)}, u32[]{:S(2)}) collective-permute-start(bf16[256,2048]{1,0:T(8,128)(2,1)S(1)} %add_convert_fusion.6), channel_id=1, source_target_pairs={{8,12},{6,2},{9,13},{7,3},{24,28},{22,18},{25,29},{23,19}} | collective-permute-start | bytes 3145736 | tf_op jit(solution)/shard_map/ppermute | solution.py:278
  238.7 28.0 %collective-permute-start.20 = (bf16[256,2048]{1,0:T(8,128)(2,1)S(1)}, bf16[256,2048]{1,0:T(8,128)(2,1)S(1)}, u32[]{:S(2)}, u32[]{:S(2)}) collective-permute-start(bf16[256,2048]{1,0:T(8,128)(2,1)S(1)} %add_convert_fusion.5), channel_id=1, source_target_pairs={{4,8},{10,6},{5,9},{11,7},{20,24},{26,22},{21,25},{27,23}} | collective-permute-start | bytes 3145736 | tf_op jit(solution)/shard_map/ppermute | solution.py:278
  240.6 44.3 %collective-permute-start.22 = (bf16[256,2048]{1,0:T(8,128)(2,1)S(1)}, bf16[256,2048]{1,0:T(8,128)(2,1)S(1)}, u32[]{:S(2)}, u32[]{:S(2)}) collective-permute-start(bf16[256,2048]{1,0:T(8,128)(2,1)S(1)} %add_convert_fusion.3), channel_id=1, source_target_pairs={{4,8},{10,6},{5,9},{11,7},{20,24},{26,22},{21,25},{27,23}} | collective-permute-start | bytes 3145736 | tf_op jit(solution)/shard_map/ppermute | solution.py:278
  248.6 36.3 %collective-permute-start.21 = (bf16[256,2048]{1,0:T(8,128)(2,1)S(1)}, bf16[256,2048]{1,0:T(8,128)(2,1)S(1)}, u32[]{:S(2)}, u32[]{:S(2)}) collective-permute-start(bf16[256,2048]{1,0:T(8,128)(2,1)S(1)} %add_convert_fusion.4), channel_id=1, source_target_pairs={{8,12},{6,2},{9,13},{7,3},{24,28},{22,18},{25,29},{23,19}} | collective-permute-start | bytes 3145736 | tf_op jit(solution)/shard_map/ppermute | solution.py:278
  268.0 16.9 %copy-start.8 = (f32[512,2048]{1,0:T(8,128)}, f32[512,2048]{1,0:T(8,128)S(1)}, u32[]{:S(2)}) copy-start(f32[512,2048]{1,0:T(8,128)S(1)} %fusion.2) | copy-start | bytes 12582916

commit v3 on v2

v3 whole, which is shorter than its diff:
```python
import functools

import jax
import jax.numpy as jnp
from jax import lax
from jax.experimental import pallas as pl
from jax.experimental.pallas import tpu as pltpu
from jax.sharding import PartitionSpec as P

GROUP = 4
VMEM_LIMIT = 40 * 1024 * 1024
COST = 1024
EXTRA = 16


def transform_kernel(order, columns, bounds, x_ref, *refs, parts, last, together):
    coeff_refs, refs = refs[:parts], refs[parts:]
    if last:
        early_ref, out_ref, x_vmem, coeff_vmem, total, sems, x_sems = refs
    else:
        out_ref, x_vmem, coeff_vmem, total, sems, x_sems = refs
    functions, blocks, slots, side, _ = x_ref.shape
    width = coeff_vmem.shape[1]
    top = coeff_vmem.shape[0] // side - 1

    def x_copy(block, i):
        return pltpu.make_async_copy(
            x_ref.at[:, block, order[block, i]], x_vmem.at[block, i], x_sems.at[block, i]
        )

    @pl.when(pl.program_id(0) == 0)
    def _():
        copies, done = [], 0
        for part, ref in enumerate(coeff_refs):
            rows = ref.shape[0]
            copy = pltpu.make_async_copy(ref, coeff_vmem.at[pl.ds(done, rows)], sems.at[part])
            copy.start()
            copies.append(copy)
            done += rows

        @pl.loop(0, blocks)
        def _(block):
            @pl.loop(bounds[block, 0], bounds[block, 1])
            def _(i):
                x_copy(block, i).start()

        for copy in copies:
            copy.wait()

    @pl.loop(0, together)
    def _(inner):
        block = pl.program_id(0) * together + inner
        start = bounds[block, 0]
        count = bounds[block, 1] - start

        @pl.loop(start, bounds[block, 1])
        def _(i):
            x_copy(block, i).wait()

        def product(first, group, masked):
            slot = [jnp.minimum(start + first + t, slots - 1) for t in range(group)]
            left = jnp.concatenate(
                [jnp.concatenate([x_vmem[block, i, p] for i in slot], axis=1) for p in range(functions)],
                axis=0,
            )
            if masked:
                lane = lax.broadcasted_iota(jnp.int32, left.shape, 1)
                left = jnp.where(lane < (count - first) * side, left, jnp.zeros_like(left))
            right = jnp.concatenate(
                [
                    coeff_vmem[pl.ds(pl.multiple_of(jnp.minimum(columns[block, i], top) * side, side), side), :]
                    for i in slot
                ],
                axis=0,
            )
            return jnp.dot(left, right, preferred_element_type=jnp.float32)

        total[...] = early_ref[inner] if last else jnp.zeros_like(total)
        full = lax.div(count, GROUP)
        rest = count - full * GROUP

        @pl.loop(0, full)
        def _(g):
            total[...] += product(g * GROUP, GROUP, False)

        @pl.when(rest > GROUP // 2)
        def _():
            total[...] += product(full * GROUP, GROUP, True)

        @pl.when((rest > 0) & (rest <= GROUP // 2))
        def _():
            total[...] += product(full * GROUP, GROUP // 2, True)

        if last:
            rows = pl.ds(pl.multiple_of(inner * side, side), side)
            for p in range(functions):
                out_ref[rows, p * width : (p + 1) * width] = total[p * side : (p + 1) * side, :].astype(
                    out_ref.dtype
                )
        else:
            out_ref[inner] = total[...]


def transform(three_index, order, columns, bounds, coeff_parts, early=None):
    functions, blocks, slots, side, _ = three_index.shape
    width = coeff_parts[0].shape[1]
    parts = len(coeff_parts)
    together = next(t for t in (2, 1) if blocks % t == 0)
    sums = pl.BlockSpec((together, functions * side, width), lambda m, *_: (m, 0, 0))
    last = early is not None
    return pl.pallas_call(
        functools.partial(transform_kernel, parts=parts, last=last, together=together),
        grid_spec=pltpu.PrefetchScalarGridSpec(
            num_scalar_prefetch=3,
            grid=(blocks // together,),
            in_specs=[pl.BlockSpec(memory_space=pl.ANY)] * (parts + 1) + [sums] * last,
            out_specs=pl.BlockSpec((together * side, functions * width), lambda m, *_: (m, 0)) if last else sums,
            scratch_shapes=[
                pltpu.VMEM((blocks, slots, functions, side, side), jnp.bfloat16),
                pltpu.VMEM((sum(c.shape[0] for c in coeff_parts), width), jnp.bfloat16),
                pltpu.VMEM((functions * side, width), jnp.float32),
                pltpu.SemaphoreType.DMA((parts,)),
                pltpu.SemaphoreType.DMA((blocks, slots)),
            ],
        ),
        out_shape=jax.ShapeDtypeStruct((blocks * side, functions * width), jnp.bfloat16)
        if last
        else jax.ShapeDtypeStruct((blocks, functions * side, width), jnp.float32),
        compiler_params=pltpu.CompilerParams(vmem_limit_bytes=VMEM_LIMIT),
        cost_estimate=pl.CostEstimate(flops=COST, bytes_accessed=COST, transcendentals=0),
    )(order, columns, bounds, three_index, *coeff_parts, *([early] * last))


def collect_kernel(index, *refs, parts):
    view_refs, out_refs, sems = refs[:parts], refs[parts:-1], refs[-1]
    copies = []
    for q, out_ref in enumerate(out_refs):
        for t, ref in enumerate(view_refs):
            copies.append(pltpu.make_async_copy(ref.at[index[q]], out_ref.at[t], sems.at[q, t]))
            copies[-1].start()
    for copy in copies:
        copy.wait()


def collect(index, views, count):
    parts = len(views)
    shape = (parts,) + views[0].shape[1:]
    return pl.pallas_call(
        functools.partial(collect_kernel, parts=parts),
        grid_spec=pltpu.PrefetchScalarGridSpec(
            num_scalar_prefetch=1,
            grid=(1,),
            in_specs=[pl.BlockSpec(memory_space=pl.ANY)] * parts,
            out_specs=[pl.BlockSpec(memory_space=pl.ANY)] * count,
            scratch_shapes=[pltpu.SemaphoreType.DMA((count, parts))],
        ),
        out_shape=[jax.ShapeDtypeStruct(shape, views[0].dtype)] * count,
        cost_estimate=pl.CostEstimate(flops=COST, bytes_accessed=COST, transcendentals=0),
    )(index, *views)


def store_rounded(out_ref, total, first_diagonal, carried):
    rows, tile = total.shape
    rounded = total.astype(out_ref.dtype)
    out_ref[:rows] = rounded
    if out_ref.shape[0] == rows:
        return
    row = lax.broadcasted_iota(jnp.int32, total.shape, 0) + first_diagonal
    col = lax.broadcasted_iota(jnp.int32, total.shape, 1) + pl.program_id(0) * tile
    lost = jnp.where(row == col, total - rounded.astype(jnp.float32), 0.0)
    lost = jnp.sum(lost, axis=0, keepdims=True)
    if carried is not None:
        lost = lost + carried
    extra = lax.broadcasted_iota(jnp.int32, (EXTRA, tile), 0)
    out_ref[rows:] = jnp.where(extra == 0, lost, 0.0).astype(out_ref.dtype)


def forward_kernel(index, sums_ref, came_ref, out_ref, *, first):
    rows = sums_ref.shape[0]
    total = sums_ref[...] + came_ref[:rows].astype(jnp.float32)
    carried = came_ref[rows : rows + 1].astype(jnp.float32)
    store_rounded(out_ref, total, index[0] + first, carried)


def forward(index, sums, came, piece, c):
    length = sums.shape[1]
    tile = min(length, 1024)
    return pl.pallas_call(
        functools.partial(forward_kernel, first=c * piece),
        grid_spec=pltpu.PrefetchScalarGridSpec(
            num_scalar_prefetch=1,
            grid=(length // tile,),
            in_specs=[
                pl.BlockSpec((piece, tile), lambda j, index: (c, j)),
                pl.BlockSpec((piece + EXTRA, tile), lambda j, index: (0, j)),
            ],
            out_specs=pl.BlockSpec((piece + EXTRA, tile), lambda j, index: (0, j)),
        ),
        out_shape=jax.ShapeDtypeStruct(came.shape, came.dtype),
        compiler_params=pltpu.CompilerParams(vmem_limit_bytes=VMEM_LIMIT),
        cost_estimate=pl.CostEstimate(flops=COST, bytes_accessed=COST, transcendentals=0),
    )(index, sums, came)


def product_kernel(index, *refs, parts, extra):
    out_ref, piece_refs = refs[2 * parts], refs[2 * parts + 1 :]
    total = None
    for rows_ref, cols_ref in zip(refs[:parts], refs[parts : 2 * parts]):
        term = lax.dot_general(
            rows_ref[0], cols_ref[...], (((1,), (1,)), ((), ())), preferred_element_type=jnp.float32
        )
        total = term if total is None else total + term
    out_ref[...] = total
    for c, ref in enumerate(piece_refs):
        rows = ref.shape[0] - extra
        store_rounded(ref, total[c * rows : (c + 1) * rows], index[0] * total.shape[0] + c * rows, None)


def row_product(index, rows, cols, pieces, extra):
    parts = len(rows)
    height, depth = rows[0].shape[1:]
    length = cols[0].shape[0]
    tile = min(length, 512)
    taller = height // max(pieces, 1) + extra
    return pl.pallas_call(
        functools.partial(product_kernel, parts=parts, extra=extra),
        grid_spec=pltpu.PrefetchScalarGridSpec(
            num_scalar_prefetch=1,
            grid=(length // tile,),
            in_specs=[
                pl.BlockSpec((1, height, depth), lambda c, index, t=t: (index[t], 0, 0)) for t in range(parts)
            ]
            + [pl.BlockSpec((tile, depth), lambda c, index: (c, 0))] * parts,
            out_specs=[pl.BlockSpec((height, tile), lambda c, index: (0, c))]
            + [pl.BlockSpec((taller, tile), lambda c, index: (0, c))] * pieces,
        ),
        out_shape=[jax.ShapeDtypeStruct((height, length), jnp.float32)]
        + [jax.ShapeDtypeStruct((taller, length), jnp.bfloat16)] * pieces,
        compiler_params=pltpu.CompilerParams(vmem_limit_bytes=VMEM_LIMIT),
        cost_estimate=pl.CostEstimate(flops=COST, bytes_accessed=COST, transcendentals=0),
    )(index, *rows, *cols)


class Line:
    def __init__(self, aux, orb):
        self.aux, self.orb, self.owned = aux, orb, aux // orb

    def targets(self, phase, o):
        first = ((o + phase) % self.orb) * self.owned
        return list(range(first, first + self.owned))

    def chains(self, phase, o, direction):
        head = 0 if direction > 0 else self.aux - 1
        found = sorted((t for t in self.targets(phase, o) if t != head), key=lambda t: -t * direction)
        late = self.owned - len(found) if phase else 0
        return {t: place + late for place, t in enumerate(found)}

    def first_use(self, phase, o, z, target):
        if target == z:
            return 10 * self.aux
        direction = 1 if target > z else -1
        return self.chains(phase, o, direction)[target] + (z if direction > 0 else self.aux - 1 - z)

    def order(self, phase, o, z):
        return sorted(self.targets(phase, o), key=lambda d: (self.first_use(phase, o, z, d), d))

    def hop(self, phase, rank, step):
        pairs, position, final = [], {}, {}
        for o in range(self.orb):
            for direction in (1, -1):
                z = step if direction > 0 else self.aux - 1 - step
                for target, place in self.chains(phase, o, direction).items():
                    if place != rank or (target - z) * direction <= 0:
                        continue
                    pairs.append((z * self.orb + o, (z + direction) * self.orb + o))
                    position[z * self.orb + o] = self.order(phase, o, z).index(target)
                    if z + direction == target:
                        final[target * self.orb + o] = True
        return pairs, position, final


def lookup(table, place):
    return jnp.asarray(table, jnp.int32)[place]


def after(value, earlier):
    return value if earlier is None else lax.optimization_barrier((value, earlier))[0]


def shards(mesh, three_index, block_cols, live_count, coefficients):
    aux, orb, sub = mesh.shape["aux"], mesh.shape["orb"], mesh.shape["sub"]
    z, o, s = lax.axis_index("aux"), lax.axis_index("orb"), lax.axis_index("sub")
    place = z * orb + o
    line = Line(aux, orb)
    owned = line.owned
    blocks = three_index.shape[1]

    side = three_index.shape[3]
    share = blocks // 3 if aux % 2 == 0 else 0
    parity = lax.rem(z, 2)
    firsts, rests = [], []
    for k in range(1, orb):
        pairs = [((t + k) % orb, t) for t in range(orb)]
        if share:
            first = lax.dynamic_slice_in_dim(coefficients, parity * share * side, share * side)
            firsts.append(lax.ppermute(first, "orb", pairs))
        rests.append(lax.ppermute(coefficients[2 * share * side :], "orb", pairs))

    slots = three_index.shape[2]
    all_blocks = blocks * orb
    columns = lax.rem(block_cols[0] - o * blocks + all_blocks, all_blocks)
    slot = lax.broadcasted_iota(jnp.int32, columns.shape, 1)
    alive = slot < live_count[0][:, None]
    mine = columns < blocks
    rank_key = jnp.where(alive, jnp.where(mine, 0, slots), 2 * slots) + slot
    rank = jnp.sum((rank_key[:, None, :] < rank_key[:, :, None]).astype(jnp.int32), axis=2)
    within = lax.rem(columns, blocks)
    half = lax.div(within, max(share, 1))
    moved = jnp.where(
        within >= 2 * share,
        within - share,
        jnp.where(half == parity, within - half * share, within - half * share + blocks - share),
    )
    placed = jnp.where(mine, columns, columns - within - blocks + moved)
    at_rank = rank[:, None, :] == lax.broadcasted_iota(jnp.int32, (1, slots, 1), 1)
    order = jnp.sum(jnp.where(at_rank, slot[:, None, :], 0), axis=2)
    columns = jnp.sum(jnp.where(at_rank, placed[:, None, :], 0), axis=2)
    live = jnp.sum(alive.astype(jnp.int32), axis=1)
    near = jnp.sum((alive & mine).astype(jnp.int32), axis=1)
    bounds = jnp.stack([jnp.zeros_like(near), near], axis=1)
    early = transform(three_index, order, columns, bounds, [coefficients])
    coeff_parts = []
    for k in range(1, orb):
        if not share:
            coeff_parts.append(rests[k - 1])
            continue
        handed = lax.ppermute(after(firsts[k - 1], early), "aux", [(i, i ^ 1) for i in range(aux)])
        coeff_parts += [firsts[k - 1], rests[k - 1], handed]
    if coeff_parts:
        bounds = jnp.stack([near, live], axis=1)
        own = transform(three_index, order, columns, bounds, coeff_parts, early)
    else:
        functions, width = three_index.shape[0], coefficients.shape[1]
        own = early.reshape(blocks, functions, side, width).transpose(0, 2, 1, 3)
        own = own.reshape(blocks * side, functions * width).astype(jnp.bfloat16)
    length, depth = own.shape
    height = length // (owned * sub)
    halves = 2 if height % 256 == 0 else 1

    def pieces(k, rank):
        return 2 * halves if k == orb - 1 and rank == owned - 1 and k else halves

    cols = [own]
    for t in range(1, sub):
        cols.append(lax.ppermute(own, "sub", [((u + t) % sub, u) for u in range(sub)]))
    views = [c.reshape(owned * sub, height, depth) for c in cols]

    blocks_sent = []
    for k in range(1, orb):
        for q in range(owned):
            table = [line.order(k, (b - k) % orb, a)[q] % owned for a in range(aux) for b in range(orb)]
            blocks_sent.append(lookup(table, place) * sub + s)
    came_rows = {}
    if blocks_sent:
        messages = collect(jnp.stack(blocks_sent), views, len(blocks_sent))
        for k in range(1, orb):
            for q in range(owned):
                pairs = [((b + k) % orb, b) for b in range(orb)]
                came_rows[k, q] = lax.ppermute(messages[(k - 1) * owned + q], "orb", pairs)
    own_blocks = [
        lookup([line.order(0, b, a)[q] % owned for a in range(aux) for b in range(orb)], place) * sub + s
        for q in range(owned)
    ]

    events, finals = [], []
    for k in range(orb):
        base = (owned * k - 1 if k else 0) * halves
        ready = [base + q * halves - 0.4 if k else 0.25 * q - 1 for q in range(owned)]
        for q in range(owned):
            events.append((ready[q], 0, "product", k, q, 0, 0))
        arrivals = [0]
        for rank in range(owned):
            wide = halves / pieces(k, rank)
            for step in range(aux - 1):
                pairs, _, final = line.hop(k, rank, step)
                if not pairs:
                    continue
                for c in range(pieces(k, rank)):
                    when = base + rank * halves + (c + step) * wide
                    events.append((when if step or c else ready[rank] + 0.1, step, "hop", k, rank, step, c))
                    arrivals.append(when + wide)
                if final:
                    finals.append((k, rank, step))
        if k < orb - 1:
            for c in range(halves):
                events.append((max(arrivals) + 0.6, 0, "fold", k, c, halves, 0))
        else:
            count = max(pieces(k, rank) for rank in range(owned))
            for c in range(count):
                late = max(arrivals) - (count - 1 - c) * halves / count
                events.append((late + 0.6, 0, "fold", k, c, count, 0))
    events.sort(key=lambda e: e[:2])

    sums, heads, came, result, last = {}, {}, {}, None, None
    for _, _, kind, k, a1, a2, c in events:
        extra = 0 if k else EXTRA
        if kind == "product":
            q = a1
            if k == 0:
                index = jnp.broadcast_to(own_blocks[q], (sub,))
                rows = views
            else:
                index = jnp.arange(sub, dtype=jnp.int32)
                rows = [came_rows[k, q]] * sub
            sums[k, q], *heads[k, q] = row_product(after(index, last), rows, cols, halves, extra)
            last = sums[k, q]
        elif kind == "hop":
            rank, step = a1, a2
            pairs, position, final = line.hop(k, rank, step)
            used = sorted(set(position.values()))
            flags = [lookup([position.get(i) == q for i in range(aux * orb)], place) for q in used]
            piece = height // pieces(k, rank)
            if step == 0 and len(used) == 1 and pieces(k, rank) == halves:
                value = heads[k, used[0]][c]
                value = after(value, last) if c else value
            elif k == 0:
                index, value = own_blocks[used[0]], sums[k, used[0]]
                head = heads[k, used[0]][c]
                for q, flag in zip(used[1:], flags[1:]):
                    index = jnp.where(flag > 0, own_blocks[q], index)
                    if step:
                        value = jnp.where(flag > 0, sums[k, q], value)
                    else:
                        head = jnp.where(flag > 0, heads[k, q][c], head)
                if step:
                    index = after((index * height)[None], last)
                    value = forward(index, value, came[k, rank, step - 1, c], piece, c)
                else:
                    value = after(head, last)
                last = value
            else:
                value = sums[k, used[0]] if step else after(sums[k, used[0]], last)
                value = value[c * piece : (c + 1) * piece]
                for q, flag in zip(used[1:], flags[1:]):
                    value = jnp.where(flag > 0, sums[k, q][c * piece : (c + 1) * piece], value)
                if step:
                    value = value + after(came[k, rank, step - 1, c], last).astype(jnp.float32)
                value = value.astype(jnp.bfloat16)
                last = value
            came[k, rank, step, c] = lax.ppermute(value, ("aux", "orb"), pairs)
        else:
            at, count = a1, a2
            piece = height // count
            rows = slice(at * piece, (at + 1) * piece)
            flag = lookup([z_ in line.targets(k, o_) for z_ in range(aux) for o_ in range(orb)], place)
            total = jnp.where(flag > 0, after(sums[k, owned - 1], last)[rows], 0.0)
            for k_, rank, step in finals:
                if k_ != k:
                    continue
                final = line.hop(k, rank, step)[2]
                flag = lookup([i in final for i in range(aux * orb)], place)
                sent = height // pieces(k, rank)
                first = at * piece % sent
                message = came[k, rank, step, at * piece // sent]
                term = message[first : first + piece].astype(jnp.float32)
                if extra:
                    start = (lax.rem(z, owned) * sub + s) * height + at * piece
                    row = lax.broadcasted_iota(jnp.int32, total.shape, 0) + start
                    col = lax.broadcasted_iota(jnp.int32, total.shape, 1)
                    term = term + jnp.where(row == col, message[sent : sent + 1].astype(jnp.float32), 0.0)
                total = total + jnp.where(flag > 0, term, 0.0)
            if result is None:
                result = jnp.zeros((height, length), jnp.float32)
            if k:
                total = total + result[rows]
            result = lax.dynamic_update_slice(result, total, (at * piece, 0))
            last = result
    return result


def solution(mesh):
    return jax.shard_map(
        functools.partial(shards, mesh),
        mesh=mesh,
        in_specs=(
            P(("groups", "aux"), "orb", None, None, None),
            P(("groups", "aux"), "orb", None),
            P(("groups", "aux"), "orb"),
            P(("groups", "orb"), "sub"),
        ),
        out_specs=P(("groups", "aux", "sub"), "orb"),
        check_vma=False,
    )
```

time: 292 us -> 410 us (1.40)
  Pallas kernels: 48.7 us -> 203 us
  waiting for transfers between devices: 154 us -> 91.8 us
  starting transfers between devices: 37.1 us -> 58.4 us
  local copies, waits for them, and re-layouts: 14.9 us -> 26 us
  other arithmetic: 28.3 us -> 22.7 us
    pallas_call x5 -> x13, Pallas kernels: 48.7 us -> 203 us  [the longest x1 129 us: collect(): pl.pallas_call(functools.partial(collect_kernel, parts=parts), grid_spec=...]
    ppermute x7 -> x5, waiting for transfers between devices: 54.8 us -> 14.1 us  [the longest x1 8.9 us: shards(): lax.ppermute(after(firsts[k - 1], early), 'aux', [(i, i ^ 1) for i in ran...]
    ppermute x15 -> x24, starting transfers between devices: 22.5 us -> 46.7 us  [shards(): came[k, rank, step, c] = lax.ppermute(value, ('aux', 'orb'), pairs)]
    ppermute x15 -> x24, waiting for transfers between devices: 96.3 us -> 73.4 us  [shards(): came[k, rank, step, c] = lax.ppermute(value, ('aux', 'orb'), pairs)]
    unnamed x34 -> x56, local copies, waits for them, and re-layouts: 6.26 us -> 16.5 us
    convert_element_type x10 -> x12, other arithmetic: 13.7 us -> 7.01 us  [shards(): value = value.astype(jnp.bfloat16)]
    add x2 -> x3, other arithmetic: 0.08 us -> 5.72 us  [the longest x2 5.1 us: shards(): total = total + jnp.where(flag > 0, term, 0.0)]
    ppermute x7 -> x5, starting transfers between devices: 14.5 us -> 11.6 us  [the longest x1 7.79 us: shards(): lax.ppermute(after(firsts[k - 1], early), 'aux', [(i, i ^ 1) for i in ran...]
  transfers between devices with their start and end apart: 23 -> 30, of which waited for: 12 -> 14; matrix products, arithmetic and copies ran while one was open for 11% -> 7% of each run, Pallas kernels for 13% -> 15%
where the time goes in v3:
time: 410 us; the launch traced here: 407 us
  Pallas kernels  203 us (50%)
  waiting for transfers between devices  91.8 us (22%)
  starting transfers between devices  58.4 us (14%)
  local copies, waits for them, and re-layouts  26 us (6%)
  other arithmetic  22.7 us (6%)
  between operations  5.84 us (1%)
    pallas_call x1, Pallas kernels, collect(): pl.pallas_call(functools.partial(collect_kernel, parts=parts), grid_spec=...  129 us
    ppermute x24, waiting for transfers between devices, shards(): came[k, rank, step, c] = lax.ppermute(value, ('aux', 'orb'), pairs)  73.4 us
    ppermute x24, starting transfers between devices, shards(): came[k, rank, step, c] = lax.ppermute(value, ('aux', 'orb'), pairs)  46.7 us
    pallas_call x4, Pallas kernels, row_product(): pl.pallas_call(functools.partial(product_kernel, parts=parts, extra=extra...  38.2 us
    pallas_call x2, Pallas kernels, transform(): pl.pallas_call(functools.partial(transform_kernel, parts=parts, last=last...  23.3 us
    unnamed x56, local copies, waits for them, and re-layouts  16.5 us
    pallas_call x6, Pallas kernels, forward(): pl.pallas_call(functools.partial(forward_kernel, first=c * piece), grid_s...  12.3 us
    ppermute x1, waiting for transfers between devices, shards(): lax.ppermute(after(firsts[k - 1], early), 'aux', [(i, i ^ 1) for i in ran...  8.9 us
  transfers between devices with their start and end apart: 30, of which 14 were waited for; matrix products, arithmetic and copies ran while one was open for 7% of the time, Pallas kernels for 15%

profile of v3, /device:TPU:20, one launch (start us, length us, event | category | flops | bytes accessed | tf_op | source)
XLA Modules:
  0.0 407.4 jit_solution(17800742439626381874)
XLA Ops:
  0.0 2.1 constant_dynamic-slice_fusion
  3.6 2.1 slice.118
  10.1 9.2 %shard_map.334.refs_3_ = f32[16,256,512]{2,1,0:T(8,128)S(1)} custom-call(s32[16,16]{1,0:T(8,128)S(1)} %get-tuple-element.90.order, s32[16,16]{1,0:T(8,128)S(1)} %get-tuple-element.89.columns, s32[16,2]{1,0:T(8,128)S(1)} %stack.25.bounds, bf16[2,16,16,128,128]{4,3,2,1,0:T(8,128)(2,1)} %x_ref.3, bf16[2048,512]{1,0:T(8,128)(2,1)S(1)} %copy-done.11), custom_call_target="tpu_custom_call" | custom-call | flops 1024 | bytes 1024 | tf_op jit(solution)/shard_map/pallas_call | solution.py:111
  19.3 3.3 copy-done.6
  22.6 7.8 %collective-permute-start.2 = (bf16[640,512]{1,0:T(8,128)(2,1)S(1)}, bf16[640,512]{1,0:T(8,128)(2,1)S(1)}, u32[]{:S(2)}, u32[]{:S(2)}) collective-permute-start(bf16[640,512]{1,0:T(8,128)(2,1)S(1)} %collective-permute-done.refs_0_), channel_id=1, source_target_pairs={{0,4},{4,0},{8,12},{12,8},{1,5},{5,1},{9,13},{13,9},{2,6},{6,2},{1... | collective-permute-start | bytes 1966088 | tf_op jit(solution)/shard_map/ppermute | solution.py:337
  30.5 5.2 %collective-permute-done.1.refs_1_ = bf16[768,512]{1,0:T(8,128)(2,1)S(1)} collective-permute-done((bf16[768,512]{1,0:T(8,128)(2,1)}, bf16[768,512]{1,0:T(8,128)(2,1)S(1)}, u32[]{:S(2)}, u32[]{:S(2)}) %collective-permute-start.1) | collective-permute-done | bytes 786464 | tf_op jit(solution)/shard_map/ppermute | solution.py:307
  35.7 8.9 %collective-permute-done.2.refs_2_ = bf16[640,512]{1,0:T(8,128)(2,1)S(1)} collective-permute-done((bf16[640,512]{1,0:T(8,128)(2,1)S(1)}, bf16[640,512]{1,0:T(8,128)(2,1)S(1)}, u32[]{:S(2)}, u32[]{:S(2)}) %collective-permute-start.2) | collective-permute-done | bytes 655392 | tf_op jit(solution)/shard_map/ppermute | solution.py:337
  44.6 14.1 %shard_map.335.refs_2_ = bf16[2048,1024]{1,0:T(8,128)(2,1)} custom-call(s32[16,16]{1,0:T(8,128)S(1)} %get-tuple-element.90.order, s32[16,16]{1,0:T(8,128)S(1)} %get-tuple-element.89.columns, s32[16,2]{1,0:T(8,128)S(1)} %copy.43.bounds, bf16[2,16,16,128,128]{4,3,2,1,0:T(8,128)(2,1)} %x_ref.3, bf16[640,512]{1,0:T(8,128)(2,1)S(1)} %collective-permute-done.refs_0_, ...), custom_call_target="tpu_custom_call" | custom-call | flops 1024 | bytes 1024 | tf_op jit(solution)/shard_map/pallas_call | solution.py:111
  61.9 4.4 %collective-permute-done.3.refs_3_ = bf16[2048,1024]{1,0:T(8,128)(2,1)} collective-permute-done((bf16[2048,1024]{1,0:T(8,128)(2,1)}, bf16[2048,1024]{1,0:T(8,128)(2,1)}, u32[]{:S(2)}, u32[]{:S(2)}) %collective-permute-start.3) | collective-permute-done | bytes 4194336 | tf_op jit(solution)/shard_map/ppermute | solution.py:355
  66.3 128.9 %shard_map.339 = (bf16[2,512,1024]{2,1,0:T(8,128)(2,1)}, bf16[2,512,1024]{2,1,0:T(8,128)(2,1)}) custom-call(s32[2]{0:T(128)} %pad_add_fusion.1.index, bf16[4,512,1024]{2,1,0:T(8,128)(2,1)} %bitcast.7.refs_0_, bf16[4,512,1024]{2,1,0:T(8,128)(2,1)} %bitcast.8.refs_1_), custom_call_target="tpu_custom_call" | custom-call | flops 1024 | bytes 1024 | tf_op jit(solution)/shard_map/pallas_call | solution.py:148
  195.6 10.1 %shard_map.336 = (f32[512,2048]{1,0:T(8,128)S(1)}, bf16[272,2048]{1,0:T(8,128)(2,1)S(1)}, bf16[272,2048]{1,0:T(8,128)(2,1)}) custom-call(s32[2]{0:T(128)S(1)} %broadcast_in_dim.147.index, bf16[4,512,1024]{2,1,0:T(8,128)(2,1)} %bitcast.7.refs_0_, bf16[4,512,1024]{2,1,0:T(8,128)(2,1)} %bitcast.8.refs_1_, bf16[2048,1024]{1,0:T(8,128)(2,1)} %shard_map.335.refs_2_, ...), custom_call_target="tpu_custom_call" | custom-call | flops 1024 | bytes 1024 | tf_op jit(solution)/shard_map/pallas_call | solution.py:225
  205.7 2.0 copy-done
  209.0 9.8 %shard_map.337 = (f32[512,2048]{1,0:T(8,128)S(1)}, bf16[272,2048]{1,0:T(8,128)(2,1)}, bf16[272,2048]{1,0:T(8,128)(2,1)}) custom-call(s32[2]{0:T(128)S(1)} %broadcast_in_dim.146.index, bf16[4,512,1024]{2,1,0:T(8,128)(2,1)} %bitcast.7.refs_0_, bf16[4,512,1024]{2,1,0:T(8,128)(2,1)} %bitcast.8.refs_1_, bf16[2048,1024]{1,0:T(8,128)(2,1)} %shard_map.335.refs_2_, ...), custom_call_target="tpu_custom_call" | custom-call | flops 1024 | bytes 1024 | tf_op jit(solution)/shard_map/pallas_call | solution.py:225
  218.8 2.1 copy-done.4
  222.1 18.3 %collective-permute-done.4.came_ref = bf16[272,2048]{1,0:T(8,128)(2,1)S(1)} collective-permute-done((bf16[272,2048]{1,0:T(8,128)(2,1)S(1)}, bf16[272,2048]{1,0:T(8,128)(2,1)S(1)}, u32[]{:S(2)}, u32[]{:S(2)}) %collective-permute-start.4) | collective-permute-done | bytes 1114144 | tf_op jit(solution)/shard_map/ppermute | solution.py:450
  240.4 2.2 copy-done.1
  242.6 1.7 shard_map.338
  244.3 2.4 collective-permute-start.8
  249.4 9.5 %shard_map.340 = (f32[512,2048]{1,0:T(8,128)S(1)}, bf16[256,2048]{1,0:T(8,128)(2,1)}, bf16[256,2048]{1,0:T(8,128)(2,1)}) custom-call(s32[2]{0:T(128)S(1)} %iota.65.index, bf16[2,512,1024]{2,1,0:T(8,128)(2,1)} %collective-permute-done.5.refs_0_.refs_1_, bf16[2,512,1024]{2,1,0:T(8,128)(2,1)} %collective-permute-done.5.refs_0_.refs_1_, ...), custom_call_target="tpu_custom_call" | custom-call | flops 1024 | bytes 1024 | tf_op jit(solution)/shard_map/pallas_call | solution.py:225
  258.9 1.9 copy-done.7
  260.8 1.7 collective-permute-start.6
  270.3 2.2 copy-done.2
  272.5 1.8 shard_map.341
  274.3 5.0 %collective-permute-start.10 = (bf16[272,2048]{1,0:T(8,128)(2,1)S(1)}, bf16[272,2048]{1,0:T(8,128)(2,1)S(1)}, u32[]{:S(2)}, u32[]{:S(2)}) collective-permute-start(bf16[272,2048]{1,0:T(8,128)(2,1)S(1)} %shard_map.341), channel_id=1, source_target_pairs={{8,4},{6,10},{9,5},{7,11},{24,20},{22,26},{25,21},{23,27}} | collective-permute-start | bytes 3342344 | tf_op jit(solution)/shard_map/ppermute | solution.py:450
  279.3 2.7 shard_map.342
  282.0 5.2 %collective-permute-done.9.came_ref = bf16[272,2048]{1,0:T(8,128)(2,1)} collective-permute-done((bf16[272,2048]{1,0:T(8,128)(2,1)}, bf16[272,2048]{1,0:T(8,128)(2,1)}, u32[]{:S(2)}, u32[]{:S(2)}) %collective-permute-start.9) | collective-permute-done | bytes 1114144 | tf_op jit(solution)/shard_map/ppermute | solution.py:450
  287.2 2.6 shard_map.343
  291.9 1.6 collective-permute-start.14
  295.1 2.6 add_convert_fusion.3
  297.6 6.6 %collective-permute-done.10.came_ref = bf16[272,2048]{1,0:T(8,128)(2,1)S(1)} collective-permute-done((bf16[272,2048]{1,0:T(8,128)(2,1)S(1)}, bf16[272,2048]{1,0:T(8,128)(2,1)S(1)}, u32[]{:S(2)}, u32[]{:S(2)}) %collective-permute-start.10) | collective-permute-done | bytes 1114144 | tf_op jit(solution)/shard_map/ppermute | solution.py:450
  304.2 1.7 collective-permute-start.19
  305.9 1.7 shard_map.344
  309.0 8.8 %shard_map.345 = (f32[512,2048]{1,0:T(8,128)S(1)}, bf16[256,2048]{1,0:T(8,128)(2,1)}, bf16[256,2048]{1,0:T(8,128)(2,1)}) custom-call(s32[2]{0:T(128)S(1)} %iota.64.index, bf16[2,512,1024]{2,1,0:T(8,128)(2,1)S(1)} %collective-permute-done.11.refs_0_.refs_1_, bf16[2,512,1024]{2,1,0:T(8,128)(2,1)S(1)} %collective-permute-done.11.refs_0_.refs_1_, ...), custom_call_target="tpu_custom_call" | custom-call | flops 1024 | bytes 1024 | tf_op jit(solution)/shard_map/pallas_call | solution.py:225
  317.9 2.0 copy-done.9
  320.0 4.0 collective-permute-done.20
  326.1 1.8 shard_map.346
  327.9 8.3 %collective-permute-start.22 = (bf16[272,2048]{1,0:T(8,128)(2,1)S(1)}, bf16[272,2048]{1,0:T(8,128)(2,1)S(1)}, u32[]{:S(2)}, u32[]{:S(2)}) collective-permute-start(bf16[272,2048]{1,0:T(8,128)(2,1)S(1)} %shard_map.346), channel_id=1, source_target_pairs={{8,4},{6,10},{9,5},{7,11},{24,20},{22,26},{25,21},{23,27}} | collective-permute-start | bytes 3342344 | tf_op jit(solution)/shard_map/ppermute | solution.py:450
  339.8 1.7 add_convert_fusion.1
  345.3 4.0 collective-permute-start.23
  349.4 6.1 %collective-permute-done.22 = bf16[272,2048]{1,0:T(8,128)(2,1)S(1)} collective-permute-done((bf16[272,2048]{1,0:T(8,128)(2,1)S(1)}, bf16[272,2048]{1,0:T(8,128)(2,1)S(1)}, u32[]{:S(2)}, u32[]{:S(2)}) %collective-permute-start.22) | collective-permute-done | bytes 1114144 | tf_op jit(solution)/shard_map/ppermute | solution.py:450
  356.7 2.6 fusion.2
  360.7 5.0 %collective-permute-done.17 = bf16[256,2048]{1,0:T(8,128)(2,1)S(1)} collective-permute-done((bf16[256,2048]{1,0:T(8,128)(2,1)S(1)}, bf16[256,2048]{1,0:T(8,128)(2,1)S(1)}, u32[]{:S(2)}, u32[]{:S(2)}) %collective-permute-start.17) | collective-permute-done | bytes 1048608 | tf_op jit(solution)/shard_map/ppermute | solution.py:450
  367.6 3.8 collective-permute-done.16
  372.9 2.5 select_add_fusion
  380.2 8.0 %collective-permute-done.26 = bf16[128,2048]{1,0:T(8,128)(2,1)S(1)} collective-permute-done((bf16[128,2048]{1,0:T(8,128)(2,1)S(1)}, bf16[128,2048]{1,0:T(8,128)(2,1)S(1)}, u32[]{:S(2)}, u32[]{:S(2)}) %collective-permute-start.26) | collective-permute-done | bytes 524320 | tf_op jit(solution)/shard_map/ppermute | solution.py:450
  388.9 10.2 %collective-permute-done.28 = bf16[128,2048]{1,0:T(8,128)(2,1)S(1)} collective-permute-done((bf16[128,2048]{1,0:T(8,128)(2,1)S(1)}, bf16[128,2048]{1,0:T(8,128)(2,1)S(1)}, u32[]{:S(2)}, u32[]{:S(2)}) %collective-permute-start.28) | collective-permute-done | bytes 524320 | tf_op jit(solution)/shard_map/ppermute | solution.py:450
  399.8 4.9 %collective-permute-done.29 = bf16[128,2048]{1,0:T(8,128)(2,1)S(1)} collective-permute-done((bf16[128,2048]{1,0:T(8,128)(2,1)S(1)}, bf16[128,2048]{1,0:T(8,128)(2,1)S(1)}, u32[]{:S(2)}, u32[]{:S(2)}) %collective-permute-start.29) | collective-permute-done | bytes 524320 | tf_op jit(solution)/shard_map/ppermute | solution.py:450
  404.8 2.6 fusion.3
  (131 shorter events, 44.1 us)
Async XLA Ops:
  0.0 10.1 %copy-start.11 = (bf16[2048,512]{1,0:T(8,128)(2,1)S(1)}, bf16[2048,512]{1,0:T(8,128)(2,1)}, u32[]{:S(2)}) copy-start(bf16[2048,512]{1,0:T(8,128)(2,1)} %refs_0_.1) | copy-start | bytes 6291460
  0.0 6.2 %copy-start.18 = (s32[1,16]{1,0:T(1,128)S(1)}, s32[1,16]{1,0:T(1,128)}, u32[]{:S(2)}) copy-start(s32[1,16]{1,0:T(1,128)} %param.38) | copy-start | bytes 196
  0.0 6.2 %copy-start.15 = (s32[1,16,16]{2,1,0:T(8,128)S(1)}, s32[1,16,16]{2,1,0:T(8,128)}, u32[]{:S(2)}) copy-start(s32[1,16,16]{2,1,0:T(8,128)} %param.37) | copy-start | bytes 3076
  2.2 20.5 %collective-permute-start = (bf16[640,512]{1,0:T(8,128)(2,1)}, bf16[640,512]{1,0:T(8,128)(2,1)S(1)}, u32[]{:S(2)}, u32[]{:S(2)}) collective-permute-start(bf16[640,512]{1,0:T(8,128)(2,1)} %constant_dynamic-slice_fusion), channel_id=1, source_target_pairs={{2,0},{0,2},{3,1},{1,3},{6,4},{4,6},{7,5},{5,7},{10,8},{8,10},{11,... | collective-permute-start | bytes 1966088 | tf_op jit(solution)/shard_map/ppermute | solution.py:306
  5.7 30.0 %collective-permute-start.1 = (bf16[768,512]{1,0:T(8,128)(2,1)}, bf16[768,512]{1,0:T(8,128)(2,1)S(1)}, u32[]{:S(2)}, u32[]{:S(2)}) collective-permute-start(bf16[768,512]{1,0:T(8,128)(2,1)} %slice.118), channel_id=1, source_target_pairs={{2,0},{0,2},{3,1},{1,3},{6,4},{4,6},{7,5},{5,7},{10,8},{8,10},{11,... | collective-permute-start | bytes 2359304 | tf_op jit(solution)/shard_map/ppermute | solution.py:307
  10.1 20.3 %copy-start.17 = (s32[16]{0:T(128)S(1)}, s32[16]{0:T(128)}, u32[]{:S(2)}) copy-start(s32[16]{0:T(128)} %copy-done.16) | copy-start | bytes 196
  10.1 20.3 %copy-start.19 = (s32[16]{0:T(128)S(1)}, s32[16]{0:T(128)}, u32[]{:S(2)}) copy-start(s32[16]{0:T(128)} %get-tuple-element.92) | copy-start | bytes 196
  22.6 22.0 %collective-permute-start.2 = (bf16[640,512]{1,0:T(8,128)(2,1)S(1)}, bf16[640,512]{1,0:T(8,128)(2,1)S(1)}, u32[]{:S(2)}, u32[]{:S(2)}) collective-permute-start(bf16[640,512]{1,0:T(8,128)(2,1)S(1)} %collective-permute-done.refs_0_), channel_id=1, source_target_pairs={{0,4},{4,0},{8,12},{12,8},{1,5},{5,1},{9,13},{13,9},{2,6},{6,2},{1... | collective-permute-start | bytes 1966088 | tf_op jit(solution)/shard_map/ppermute | solution.py:337
  30.5 28.3 %copy-start.27 = (s32[8]{0:T(128)S(1)}, s32[8]{0:T(128)}, u32[]{:S(2)}) copy-start(s32[8]{0:T(128)} %constant.110.clone) | copy-start | bytes 100
  30.5 28.9 %copy-start.26 = (s32[8]{0:T(128)S(1)}, s32[8]{0:T(128)}, u32[]{:S(2)}) copy-start(s32[8]{0:T(128)} %constant.111.clone) | copy-start | bytes 100
  58.7 7.6 %collective-permute-start.3 = (bf16[2048,1024]{1,0:T(8,128)(2,1)}, bf16[2048,1024]{1,0:T(8,128)(2,1)}, u32[]{:S(2)}, u32[]{:S(2)}) collective-permute-start(bf16[2048,1024]{1,0:T(8,128)(2,1)} %shard_map.335.refs_2_), channel_id=1, source_target_pairs={{1,0},{0,1},{3,2},{2,3},{5,4},{4,5},{7,6},{6,7},{9,8},{8,9},{11,10... | collective-permute-start | bytes 12582920 | tf_op jit(solution)/shard_map/ppermute | solution.py:355
  195.1 54.2 %collective-permute-start.5 = (bf16[2,512,1024]{2,1,0:T(8,128)(2,1)}, bf16[2,512,1024]{2,1,0:T(8,128)(2,1)}, u32[]{:S(2)}, u32[]{:S(2)}) collective-permute-start(bf16[2,512,1024]{2,1,0:T(8,128)(2,1)} %get-tuple-element.54), channel_id=1, source_target_pairs={{2,0},{0,2},{3,1},{1,3},{6,4},{4,6},{7,5},{5,7},{10,8},{8,10},{11,... | collective-permute-start | bytes 6291464 | tf_op jit(solution)/shard_map/ppermute | solution.py:369
  207.7 32.7 %collective-permute-start.4 = (bf16[272,2048]{1,0:T(8,128)(2,1)S(1)}, bf16[272,2048]{1,0:T(8,128)(2,1)S(1)}, u32[]{:S(2)}, u32[]{:S(2)}) collective-permute-start(bf16[272,2048]{1,0:T(8,128)(2,1)S(1)} %get-tuple-element.52), channel_id=1, source_target_pairs={{0,4},{12,8},{2,6},{14,10},{1,5},{13,9},{3,7},{15,11},{16,20},{28,... | collective-permute-start | bytes 3342344 | tf_op jit(solution)/shard_map/ppermute | solution.py:450
  220.8 49.4 %collective-permute-start.7 = (bf16[272,2048]{1,0:T(8,128)(2,1)}, bf16[272,2048]{1,0:T(8,128)(2,1)}, u32[]{:S(2)}, u32[]{:S(2)}) collective-permute-start(bf16[272,2048]{1,0:T(8,128)(2,1)} %get-tuple-element.59), channel_id=1, source_target_pairs={{0,4},{12,8},{2,6},{14,10},{1,5},{13,9},{3,7},{15,11},{16,20},{28,... | collective-permute-start | bytes 3342344 | tf_op jit(solution)/shard_map/ppermute | solution.py:450
  244.3 35.0 %collective-permute-start.8 = (bf16[272,2048]{1,0:T(8,128)(2,1)}, bf16[272,2048]{1,0:T(8,128)(2,1)}, u32[]{:S(2)}, u32[]{:S(2)}) collective-permute-start(bf16[272,2048]{1,0:T(8,128)(2,1)} %shard_map.338), channel_id=1, source_target_pairs={{8,4},{6,10},{9,5},{7,11},{24,20},{22,26},{25,21},{23,27}} | collective-permute-start | bytes 3342344 | tf_op jit(solution)/shard_map/ppermute | solution.py:450
  246.7 40.5 %collective-permute-start.9 = (bf16[272,2048]{1,0:T(8,128)(2,1)}, bf16[272,2048]{1,0:T(8,128)(2,1)}, u32[]{:S(2)}, u32[]{:S(2)}) collective-permute-start(bf16[272,2048]{1,0:T(8,128)(2,1)} %get-tuple-element.62), channel_id=1, source_target_pairs={{12,8},{2,6},{13,9},{3,7},{28,24},{18,22},{29,25},{19,23}} | collective-permute-start | bytes 3342344 | tf_op jit(solution)/shard_map/ppermute | solution.py:450
  247.9 59.6 %collective-permute-start.11 = (bf16[2,512,1024]{2,1,0:T(8,128)(2,1)}, bf16[2,512,1024]{2,1,0:T(8,128)(2,1)S(1)}, u32[]{:S(2)}, u32[]{:S(2)}) collective-permute-start(bf16[2,512,1024]{2,1,0:T(8,128)(2,1)} %get-tuple-element.66), channel_id=1, source_target_pairs={{2,0},{0,2},{3,1},{1,3},{6,4},{4,6},{7,5},{5,7},{10,8},{8,10},{11,... | collective-permute-start | bytes 6291464 | tf_op jit(solution)/shard_map/ppermute | solution.py:369
  249.3 13.2 %copy-start.25 = (s32[8]{0:T(128)S(1)}, s32[8]{0:T(128)}, u32[]{:S(2)}) copy-start(s32[8]{0:T(128)} %constant.112.clone) | copy-start | bytes 100
  249.3 13.8 %copy-start.24 = (s32[8]{0:T(128)S(1)}, s32[8]{0:T(128)}, u32[]{:S(2)}) copy-start(s32[8]{0:T(128)} %constant.113.clone) | copy-start | bytes 100
  249.3 15.8 %copy-start.23 = (s32[8]{0:T(128)S(1)}, s32[8]{0:T(128)}, u32[]{:S(2)}) copy-start(s32[8]{0:T(128)} %constant.114.clone) | copy-start | bytes 100
  249.3 17.0 %copy-start.22 = (s32[8]{0:T(128)S(1)}, s32[8]{0:T(128)}, u32[]{:S(2)}) copy-start(s32[8]{0:T(128)} %constant.115.clone) | copy-start | bytes 100
  249.3 18.3 %copy-start.21 = (s32[8]{0:T(128)S(1)}, s32[8]{0:T(128)}, u32[]{:S(2)}) copy-start(s32[8]{0:T(128)} %constant.116.clone) | copy-start | bytes 100
  249.3 19.6 %copy-start.20 = (s32[8]{0:T(128)S(1)}, s32[8]{0:T(128)}, u32[]{:S(2)}) copy-start(s32[8]{0:T(128)} %constant.117.clone) | copy-start | bytes 100
  260.8 32.7 %collective-permute-start.6 = (bf16[256,2048]{1,0:T(8,128)(2,1)}, bf16[256,2048]{1,0:T(8,128)(2,1)}, u32[]{:S(2)}, u32[]{:S(2)}) collective-permute-start(bf16[256,2048]{1,0:T(8,128)(2,1)} %get-tuple-element.56), channel_id=1, source_target_pairs={{0,4},{14,10},{1,5},{15,11},{16,20},{30,26},{17,21},{31,27}} | collective-permute-start | bytes 3145736 | tf_op jit(solution)/shard_map/ppermute | solution.py:450
  274.3 29.9 %collective-permute-start.10 = (bf16[272,2048]{1,0:T(8,128)(2,1)S(1)}, bf16[272,2048]{1,0:T(8,128)(2,1)S(1)}, u32[]{:S(2)}, u32[]{:S(2)}) collective-permute-start(bf16[272,2048]{1,0:T(8,128)(2,1)S(1)} %shard_map.341), channel_id=1, source_target_pairs={{8,4},{6,10},{9,5},{7,11},{24,20},{22,26},{25,21},{23,27}} | collective-permute-start | bytes 3342344 | tf_op jit(solution)/shard_map/ppermute | solution.py:450
  279.3 7.9 %copy-start.5 = (f32[512,2048]{1,0:T(8,128)S(1)}, f32[512,2048]{1,0:T(8,128)}, u32[]{:S(2)}) copy-start(f32[512,2048]{1,0:T(8,128)} %copy-done.4) | copy-start | bytes 12582916
  282.0 13.0 %copy-start.8 = (f32[512,2048]{1,0:T(8,128)S(1)}, f32[512,2048]{1,0:T(8,128)}, u32[]{:S(2)}) copy-start(f32[512,2048]{1,0:T(8,128)} %copy-done.7) | copy-start | bytes 12582916
  289.8 34.2 %collective-permute-start.20 = (bf16[272,2048]{1,0:T(8,128)(2,1)}, bf16[272,2048]{1,0:T(8,128)(2,1)S(1)}, u32[]{:S(2)}, u32[]{:S(2)}) collective-permute-start(bf16[272,2048]{1,0:T(8,128)(2,1)} %shard_map.343), channel_id=1, source_target_pairs={{8,4},{6,10},{9,5},{7,11},{24,20},{22,26},{25,21},{23,27}} | collective-permute-start | bytes 3342344 | tf_op jit(solution)/shard_map/ppermute | solution.py:450
  291.9 36.0 %collective-permute-start.14 = (bf16[256,2048]{1,0:T(8,128)(2,1)}, bf16[256,2048]{1,0:T(8,128)(2,1)}, u32[]{:S(2)}, u32[]{:S(2)}) collective-permute-start(bf16[256,2048]{1,0:T(8,128)(2,1)} %get-tuple-element.70), channel_id=1, source_target_pairs={{0,4},{14,10},{1,5},{15,11},{16,20},{30,26},{17,21},{31,27}} | collective-permute-start | bytes 3145736 | tf_op jit(solution)/shard_map/ppermute | solution.py:450
  293.5 12.4 %copy-start.3 = (f32[512,2048]{1,0:T(8,128)S(1)}, f32[512,2048]{1,0:T(8,128)}, u32[]{:S(2)}) copy-start(f32[512,2048]{1,0:T(8,128)} %copy-done) | copy-start | bytes 12582916
  293.5 31.8 %collective-permute-start.15 = (bf16[272,2048]{1,0:T(8,128)(2,1)}, bf16[272,2048]{1,0:T(8,128)(2,1)}, u32[]{:S(2)}, u32[]{:S(2)}) collective-permute-start(bf16[272,2048]{1,0:T(8,128)(2,1)} %get-tuple-element.73), channel_id=1, source_target_pairs={{12,8},{2,6},{13,9},{3,7},{28,24},{18,22},{29,25},{19,23}} | collective-permute-start | bytes 3342344 | tf_op jit(solution)/shard_map/ppermute | solution.py:450
  304.2 33.6 %collective-permute-start.19 = (bf16[272,2048]{1,0:T(8,128)(2,1)}, bf16[272,2048]{1,0:T(8,128)(2,1)}, u32[]{:S(2)}, u32[]{:S(2)}) collective-permute-start(bf16[272,2048]{1,0:T(8,128)(2,1)} %shard_map.342), channel_id=1, source_target_pairs={{4,0},{10,14},{5,1},{11,15},{20,16},{26,30},{21,17},{27,31}} | collective-permute-start | bytes 3342344 | tf_op jit(solution)/shard_map/ppermute | solution.py:450
  307.6 32.3 %collective-permute-start.13 = (bf16[256,2048]{1,0:T(8,128)(2,1)}, bf16[256,2048]{1,0:T(8,128)(2,1)}, u32[]{:S(2)}, u32[]{:S(2)}) collective-permute-start(bf16[256,2048]{1,0:T(8,128)(2,1)} %add_convert_fusion.3), channel_id=1, source_target_pairs={{4,8},{10,6},{5,9},{11,7},{20,24},{26,22},{21,25},{27,23}} | collective-permute-start | bytes 3145736 | tf_op jit(solution)/shard_map/ppermute | solution.py:450
  324.0 19.7 %collective-permute-start.12 = (bf16[128,2048]{1,0:T(8,128)(2,1)S(1)}, bf16[128,2048]{1,0:T(8,128)(2,1)S(1)}, u32[]{:S(2)}, u32[]{:S(2)}) collective-permute-start(bf16[128,2048]{1,0:T(8,128)(2,1)S(1)} %select_convert_fusion.3), channel_id=1, source_target_pairs={{0,4},{12,8},{2,6},{14,10},{1,5},{13,9},{3,7},{15,11},{16,20},{28,... | collective-permute-start | bytes 1572872 | tf_op jit(solution)/shard_map/ppermute | solution.py:450
  325.3 20.0 %collective-permute-start.21 = (bf16[272,2048]{1,0:T(8,128)(2,1)}, bf16[272,2048]{1,0:T(8,128)(2,1)S(1)}, u32[]{:S(2)}, u32[]{:S(2)}) collective-permute-start(bf16[272,2048]{1,0:T(8,128)(2,1)} %shard_map.344), channel_id=1, source_target_pairs={{4,0},{10,14},{5,1},{11,15},{20,16},{26,30},{21,17},{27,31}} | collective-permute-start | bytes 3342344 | tf_op jit(solution)/shard_map/ppermute | solution.py:450
  327.9 27.5 %collective-permute-start.22 = (bf16[272,2048]{1,0:T(8,128)(2,1)S(1)}, bf16[272,2048]{1,0:T(8,128)(2,1)S(1)}, u32[]{:S(2)}, u32[]{:S(2)}) collective-permute-start(bf16[272,2048]{1,0:T(8,128)(2,1)S(1)} %shard_map.346), channel_id=1, source_target_pairs={{8,4},{6,10},{9,5},{7,11},{24,20},{22,26},{25,21},{23,27}} | collective-permute-start | bytes 3342344 | tf_op jit(solution)/shard_map/ppermute | solution.py:450
  337.8 28.0 %collective-permute-start.17 = (bf16[256,2048]{1,0:T(8,128)(2,1)S(1)}, bf16[256,2048]{1,0:T(8,128)(2,1)S(1)}, u32[]{:S(2)}, u32[]{:S(2)}) collective-permute-start(bf16[256,2048]{1,0:T(8,128)(2,1)S(1)} %add_convert_fusion.2), channel_id=1, source_target_pairs={{4,8},{10,6},{5,9},{11,7},{20,24},{26,22},{21,25},{27,23}} | collective-permute-start | bytes 3145736 | tf_op jit(solution)/shard_map/ppermute | solution.py:450
  342.4 16.9 %collective-permute-start.18 = (bf16[128,2048]{1,0:T(8,128)(2,1)S(1)}, bf16[128,2048]{1,0:T(8,128)(2,1)S(1)}, u32[]{:S(2)}, u32[]{:S(2)}) collective-permute-start(bf16[128,2048]{1,0:T(8,128)(2,1)S(1)} %select_convert_fusion.2), channel_id=1, source_target_pairs={{0,4},{12,8},{2,6},{14,10},{1,5},{13,9},{3,7},{15,11},{16,20},{28,... | collective-permute-start | bytes 1572872 | tf_op jit(solution)/shard_map/ppermute | solution.py:450
  343.9 33.1 %collective-permute-start.24 = (bf16[128,2048]{1,0:T(8,128)(2,1)S(1)}, bf16[128,2048]{1,0:T(8,128)(2,1)S(1)}, u32[]{:S(2)}, u32[]{:S(2)}) collective-permute-start(bf16[128,2048]{1,0:T(8,128)(2,1)S(1)} %add_convert_fusion.7), channel_id=1, source_target_pairs={{4,8},{10,6},{5,9},{11,7},{20,24},{26,22},{21,25},{27,23}} | collective-permute-start | bytes 1572872 | tf_op jit(solution)/shard_map/ppermute | solution.py:450
  345.3 33.1 %collective-permute-start.23 = (bf16[256,2048]{1,0:T(8,128)(2,1)S(1)}, bf16[256,2048]{1,0:T(8,128)(2,1)S(1)}, u32[]{:S(2)}, u32[]{:S(2)}) collective-permute-start(bf16[256,2048]{1,0:T(8,128)(2,1)S(1)} %add_convert_fusion.1), channel_id=1, source_target_pairs={{8,12},{6,2},{9,13},{7,3},{24,28},{22,18},{25,29},{23,19}} | collective-permute-start | bytes 3145736 | tf_op jit(solution)/shard_map/ppermute | solution.py:450
  355.4 16.0 %collective-permute-start.16 = (bf16[128,2048]{1,0:T(8,128)(2,1)S(1)}, bf16[128,2048]{1,0:T(8,128)(2,1)S(1)}, u32[]{:S(2)}, u32[]{:S(2)}) collective-permute-start(bf16[128,2048]{1,0:T(8,128)(2,1)S(1)} %select_convert_fusion.1), channel_id=1, source_target_pairs={{0,4},{12,8},{2,6},{14,10},{1,5},{13,9},{3,7},{15,11},{16,20},{28,... | collective-permute-start | bytes 1572872 | tf_op jit(solution)/shard_map/ppermute | solution.py:450
  359.4 28.8 %collective-permute-start.26 = (bf16[128,2048]{1,0:T(8,128)(2,1)S(1)}, bf16[128,2048]{1,0:T(8,128)(2,1)S(1)}, u32[]{:S(2)}, u32[]{:S(2)}) collective-permute-start(bf16[128,2048]{1,0:T(8,128)(2,1)S(1)} %add_convert_fusion.6), channel_id=1, source_target_pairs={{4,8},{10,6},{5,9},{11,7},{20,24},{26,22},{21,25},{27,23}} | collective-permute-start | bytes 1572872 | tf_op jit(solution)/shard_map/ppermute | solution.py:450
  366.1 6.8 %copy-start.14 = (bf16[272,2048]{1,0:T(8,128)(2,1)S(1)}, bf16[272,2048]{1,0:T(8,128)(2,1)}, u32[]{:S(2)}) copy-start(bf16[272,2048]{1,0:T(8,128)(2,1)} %copy-done.13) | copy-start | bytes 3342340
  366.2 12.6 %collective-permute-start.25 = (bf16[128,2048]{1,0:T(8,128)(2,1)S(1)}, bf16[128,2048]{1,0:T(8,128)(2,1)S(1)}, u32[]{:S(2)}, u32[]{:S(2)}) collective-permute-start(bf16[128,2048]{1,0:T(8,128)(2,1)S(1)} %select_convert_fusion), channel_id=1, source_target_pairs={{0,4},{12,8},{2,6},{14,10},{1,5},{13,9},{3,7},{15,11},{16,20},{28,... | collective-permute-start | bytes 1572872 | tf_op jit(solution)/shard_map/ppermute | solution.py:450
  371.6 27.6 %collective-permute-start.28 = (bf16[128,2048]{1,0:T(8,128)(2,1)S(1)}, bf16[128,2048]{1,0:T(8,128)(2,1)S(1)}, u32[]{:S(2)}, u32[]{:S(2)}) collective-permute-start(bf16[128,2048]{1,0:T(8,128)(2,1)S(1)} %add_convert_fusion.5), channel_id=1, source_target_pairs={{4,8},{10,6},{5,9},{11,7},{20,24},{26,22},{21,25},{27,23}} | collective-permute-start | bytes 1572872 | tf_op jit(solution)/shard_map/ppermute | solution.py:450
  377.0 22.1 %collective-permute-start.27 = (bf16[256,2048]{1,0:T(8,128)(2,1)S(1)}, bf16[256,2048]{1,0:T(8,128)(2,1)S(1)}, u32[]{:S(2)}, u32[]{:S(2)}) collective-permute-start(bf16[256,2048]{1,0:T(8,128)(2,1)S(1)} %add_convert_fusion), channel_id=1, source_target_pairs={{8,12},{6,2},{9,13},{7,3},{24,28},{22,18},{25,29},{23,19}} | collective-permute-start | bytes 3145736 | tf_op jit(solution)/shard_map/ppermute | solution.py:450
  378.9 25.8 %collective-permute-start.29 = (bf16[128,2048]{1,0:T(8,128)(2,1)S(1)}, bf16[128,2048]{1,0:T(8,128)(2,1)S(1)}, u32[]{:S(2)}, u32[]{:S(2)}) collective-permute-start(bf16[128,2048]{1,0:T(8,128)(2,1)S(1)} %add_convert_fusion.4), channel_id=1, source_target_pairs={{4,8},{10,6},{5,9},{11,7},{20,24},{26,22},{21,25},{27,23}} | collective-permute-start | bytes 1572872 | tf_op jit(solution)/shard_map/ppermute | solution.py:450
  399.8 4.9 %copy-start.12 = (f32[512,2048]{1,0:T(8,128)}, f32[512,2048]{1,0:T(8,128)S(1)}, u32[]{:S(2)}) copy-start(f32[512,2048]{1,0:T(8,128)S(1)} %fusion.4) | copy-start | bytes 12582916
  (10 other events, 21.3 us)

commit v4 on v3

--- a/solution.py
+++ b/solution.py
@@ -8,7 +8,8 @@
 from jax.sharding import PartitionSpec as P
 
 GROUP = 4
-VMEM_LIMIT = 40 * 1024 * 1024
+VMEM_LIMIT = 36 * 1024 * 1024
+SMALL_VMEM_LIMIT = 20 * 1024 * 1024
 COST = 1024
 EXTRA = 16
 
@@ -131,32 +132,27 @@
     )(order, columns, bounds, three_index, *coeff_parts, *([early] * last))
 
 
-def collect_kernel(index, *refs, parts):
-    view_refs, out_refs, sems = refs[:parts], refs[parts:-1], refs[-1]
-    copies = []
-    for q, out_ref in enumerate(out_refs):
-        for t, ref in enumerate(view_refs):
-            copies.append(pltpu.make_async_copy(ref.at[index[q]], out_ref.at[t], sems.at[q, t]))
-            copies[-1].start()
-    for copy in copies:
-        copy.wait()
-
-
-def collect(index, views, count):
+def collect_kernel(index, *refs):
+    for t, ref in enumerate(refs[:-1]):
+        refs[-1][t] = ref[0]
+
+
+def collect(index, views):
     parts = len(views)
-    shape = (parts,) + views[0].shape[1:]
+    height, depth = views[0].shape[1:]
+    tall = height // 2 if height % 256 == 0 else height
     return pl.pallas_call(
-        functools.partial(collect_kernel, parts=parts),
+        collect_kernel,
         grid_spec=pltpu.PrefetchScalarGridSpec(
             num_scalar_prefetch=1,
-            grid=(1,),
-            in_specs=[pl.BlockSpec(memory_space=pl.ANY)] * parts,
-            out_specs=[pl.BlockSpec(memory_space=pl.ANY)] * count,
-            scratch_shapes=[pltpu.SemaphoreType.DMA((count, parts))],
+            grid=(height // tall,),
+            in_specs=[pl.BlockSpec((1, tall, depth), lambda r, index: (index[0], r, 0))] * parts,
+            out_specs=pl.BlockSpec((parts, tall, depth), lambda r, index: (0, r, 0)),
         ),
-        out_shape=[jax.ShapeDtypeStruct(shape, views[0].dtype)] * count,
+        out_shape=jax.ShapeDtypeStruct((parts, height, depth), views[0].dtype),
+        compiler_params=pltpu.CompilerParams(vmem_limit_bytes=SMALL_VMEM_LIMIT),
         cost_estimate=pl.CostEstimate(flops=COST, bytes_accessed=COST, transcendentals=0),
-    )(index, *views)
+    )(index[None], *views)
 
 
 def store_rounded(out_ref, total, first_diagonal, carried):
@@ -175,31 +171,87 @@
     out_ref[rows:] = jnp.where(extra == 0, lost, 0.0).astype(out_ref.dtype)
 
 
-def forward_kernel(index, sums_ref, came_ref, out_ref, *, first):
-    rows = sums_ref.shape[0]
-    total = sums_ref[...] + came_ref[:rows].astype(jnp.float32)
-    carried = came_ref[rows : rows + 1].astype(jnp.float32)
-    store_rounded(out_ref, total, index[0] + first, carried)
-
-
-def forward(index, sums, came, piece, c):
-    length = sums.shape[1]
-    tile = min(length, 1024)
+def forward_kernel(flags, *refs, choices, first):
+    out_ref = refs[-1]
+    for i in range(choices):
+        sums_ref, came_ref = refs[2 * i], refs[2 * i + 1]
+
+        @pl.when(flags[i] > 0)
+        def _(sums_ref=sums_ref, came_ref=came_ref):
+            rows = sums_ref.shape[0]
+            total = sums_ref[...] + came_ref[:rows].astype(jnp.float32)
+            carried = came_ref[rows : rows + 1].astype(jnp.float32) if came_ref.shape[0] > rows else None
+            store_rounded(out_ref, total, flags[choices] + first, carried)
+
+
+def forward(flags, sums, came, piece, c):
+    choices, length = len(sums), sums[0].shape[1]
+    tile = min(length, 512)
+    sent = came[0].shape[0]
+    in_specs, operands = [], []
+    for i in range(choices):
+        in_specs.append(pl.BlockSpec((piece, tile), lambda j, flags, i=i: (c, j * flags[i])))
+        in_specs.append(pl.BlockSpec((sent, tile), lambda j, flags, i=i: (0, j * flags[i])))
+        operands += [sums[i], came[i]]
     return pl.pallas_call(
-        functools.partial(forward_kernel, first=c * piece),
+        functools.partial(forward_kernel, choices=choices, first=c * piece),
+        grid_spec=pltpu.PrefetchScalarGridSpec(
+            num_scalar_prefetch=1,
+            grid=(length // tile,),
+            in_specs=in_specs,
+            out_specs=pl.BlockSpec((sent, tile), lambda j, flags: (0, j)),
+        ),
+        out_shape=jax.ShapeDtypeStruct(came[0].shape, came[0].dtype),
+        compiler_params=pltpu.CompilerParams(vmem_limit_bytes=SMALL_VMEM_LIMIT),
+        cost_estimate=pl.CostEstimate(flops=COST, bytes_accessed=COST, transcendentals=0),
+    )(flags, *operands)
+
+
+def fold_kernel(flags, *refs, extra, first):
+    before_ref, sums_ref, came_refs, out_ref = refs[0], refs[1], refs[2:-1], refs[-1]
+    rows, tile = out_ref.shape
+    out_ref[...] = jnp.zeros_like(out_ref) if first else before_ref[...]
+
+    @pl.when(flags[0] > 0)
+    def _():
+        out_ref[...] += sums_ref[...]
+
+    for i, ref in enumerate(came_refs):
+
+        @pl.when(flags[i + 1] > 0)
+        def _(ref=ref):
+            term = ref[:rows].astype(jnp.float32)
+            if extra:
+                row = lax.broadcasted_iota(jnp.int32, (rows, tile), 0) + flags[len(came_refs) + 1]
+                col = lax.broadcasted_iota(jnp.int32, (rows, tile), 1) + pl.program_id(0) * tile
+                term = term + jnp.where(row == col, ref[rows : rows + 1].astype(jnp.float32), 0.0)
+            out_ref[...] += term
+
+
+def fold(flags, before, sums, came, rows, at, extra, first):
+    height, length = before.shape
+    tile = min(length, 512)
+    in_place = pl.BlockSpec((rows, tile), lambda j, flags: (at, j))
+    return pl.pallas_call(
+        functools.partial(fold_kernel, extra=extra, first=first),
         grid_spec=pltpu.PrefetchScalarGridSpec(
             num_scalar_prefetch=1,
             grid=(length // tile,),
             in_specs=[
-                pl.BlockSpec((piece, tile), lambda j, index: (c, j)),
-                pl.BlockSpec((piece + EXTRA, tile), lambda j, index: (0, j)),
+                pl.BlockSpec((rows, tile), lambda j, flags: (at, 0)) if first else in_place,
+                pl.BlockSpec((rows, tile), lambda j, flags: (at, j * flags[0])),
+            ]
+            + [
+                pl.BlockSpec((message.shape[0], tile), lambda j, flags, i=i: (0, j * flags[i + 1]))
+                for i, message in enumerate(came)
             ],
-            out_specs=pl.BlockSpec((piece + EXTRA, tile), lambda j, index: (0, j)),
+            out_specs=in_place,
         ),
-        out_shape=jax.ShapeDtypeStruct(came.shape, came.dtype),
-        compiler_params=pltpu.CompilerParams(vmem_limit_bytes=VMEM_LIMIT),
+        out_shape=jax.ShapeDtypeStruct(before.shape, before.dtype),
+        input_output_aliases={} if first else {1: 0},
+        compiler_params=pltpu.CompilerParams(vmem_limit_bytes=SMALL_VMEM_LIMIT),
         cost_estimate=pl.CostEstimate(flops=COST, bytes_accessed=COST, transcendentals=0),
-    )(index, sums, came)
+    )(flags, before, sums, *came)
 
 
 def product_kernel(index, *refs, parts, extra):
@@ -216,7 +268,7 @@
         store_rounded(ref, total[c * rows : (c + 1) * rows], index[0] * total.shape[0] + c * rows, None)
 
 
-def row_product(index, rows, cols, pieces, extra):
+def row_product(index, rows, cols, pieces, extra, cost):
     parts = len(rows)
     height, depth = rows[0].shape[1:]
     length = cols[0].shape[0]
@@ -236,8 +288,8 @@
         ),
         out_shape=[jax.ShapeDtypeStruct((height, length), jnp.float32)]
         + [jax.ShapeDtypeStruct((taller, length), jnp.bfloat16)] * pieces,
-        compiler_params=pltpu.CompilerParams(vmem_limit_bytes=VMEM_LIMIT),
-        cost_estimate=pl.CostEstimate(flops=COST, bytes_accessed=COST, transcendentals=0),
+        compiler_params=pltpu.CompilerParams(vmem_limit_bytes=SMALL_VMEM_LIMIT),
+        cost_estimate=pl.CostEstimate(flops=cost, bytes_accessed=COST, transcendentals=0),
     )(index, *rows, *cols)
 
 
@@ -277,6 +329,30 @@
                     if z + direction == target:
                         final[target * self.orb + o] = True
         return pairs, position, final
+
+    def merged(self, phase):
+        groups = []
+        for due in range(self.owned + self.aux - 2):
+            open_groups = []
+            for rank in range(self.owned):
+                step = due - rank
+                if not 0 <= step < self.aux - 1 or not self.hop(phase, rank, step)[0]:
+                    continue
+                pairs = self.hop(phase, rank, step)[0]
+                for group in open_groups if step >= 1 and due >= 2 else []:
+                    others = [p for r, st in group for p in self.hop(phase, r, st)[0]]
+                    if not {p[0] for p in pairs} & {p[0] for p in others} and not {p[1] for p in pairs} & {
+                        p[1] for p in others
+                    }:
+                        group.append((rank, step))
+                        break
+                else:
+                    if step >= 1 and due >= 2:
+                        open_groups.append([(rank, step)])
+                    else:
+                        groups.append([(rank, step)])
+            groups += open_groups
+        return groups
 
 
 def lookup(table, place):
@@ -347,26 +423,19 @@
     height = length // (owned * sub)
     halves = 2 if height % 256 == 0 else 1
 
-    def pieces(k, rank):
-        return 2 * halves if k == orb - 1 and rank == owned - 1 and k else halves
+    def pieces(k):
+        return halves if k else 1
 
     cols = [own]
     for t in range(1, sub):
         cols.append(lax.ppermute(own, "sub", [((u + t) % sub, u) for u in range(sub)]))
     views = [c.reshape(owned * sub, height, depth) for c in cols]
 
-    blocks_sent = []
-    for k in range(1, orb):
-        for q in range(owned):
-            table = [line.order(k, (b - k) % orb, a)[q] % owned for a in range(aux) for b in range(orb)]
-            blocks_sent.append(lookup(table, place) * sub + s)
-    came_rows = {}
-    if blocks_sent:
-        messages = collect(jnp.stack(blocks_sent), views, len(blocks_sent))
-        for k in range(1, orb):
-            for q in range(owned):
-                pairs = [((b + k) % orb, b) for b in range(orb)]
-                came_rows[k, q] = lax.ppermute(messages[(k - 1) * owned + q], "orb", pairs)
+    def rows_to_send(k, q, earlier):
+        table = [line.order(k, (b - k) % orb, a)[q] % owned for a in range(aux) for b in range(orb)]
+        message = collect(after(lookup(table, place) * sub + s, earlier), views)
+        return message, lax.ppermute(message, "orb", [((b + k) % orb, b) for b in range(orb)])
+
     own_blocks = [
         lookup([line.order(0, b, a)[q] % owned for a in range(aux) for b in range(orb)], place) * sub + s
         for q in range(owned)
@@ -375,105 +444,83 @@
     events, finals = [], []
     for k in range(orb):
         base = (owned * k - 1 if k else 0) * halves
+        wide = halves // pieces(k)
         ready = [base + q * halves - 0.4 if k else 0.25 * q - 1 for q in range(owned)]
         for q in range(owned):
-            events.append((ready[q], 0, "product", k, q, 0, 0))
-        arrivals = [0]
-        for rank in range(owned):
-            wide = halves / pieces(k, rank)
-            for step in range(aux - 1):
-                pairs, _, final = line.hop(k, rank, step)
-                if not pairs:
-                    continue
-                for c in range(pieces(k, rank)):
-                    when = base + rank * halves + (c + step) * wide
-                    events.append((when if step or c else ready[rank] + 0.1, step, "hop", k, rank, step, c))
-                    arrivals.append(when + wide)
-                if final:
-                    finals.append((k, rank, step))
-        if k < orb - 1:
-            for c in range(halves):
-                events.append((max(arrivals) + 0.6, 0, "fold", k, c, halves, 0))
-        else:
-            count = max(pieces(k, rank) for rank in range(owned))
-            for c in range(count):
-                late = max(arrivals) - (count - 1 - c) * halves / count
-                events.append((late + 0.6, 0, "fold", k, c, count, 0))
+            if k:
+                events.append((-1.1 if q == 0 and k == 1 else -0.7, 0, "rows", k, q, 0))
+            events.append((ready[q], 0, "product", k, q, 0))
+        for group in line.merged(k):
+            step = group[0][1]
+            for c in range(pieces(k)):
+                when = max(base + rank * halves + (c + st) * wide for rank, st in group)
+                if step == 0 and c == 0:
+                    when = ready[group[0][0]] + 0.1
+                events.append((when, step, "hop", k, tuple(group), c))
+            if any(line.hop(k, *member)[2] for member in group):
+                finals.append((k, tuple(group)))
+    end = max(e[0] for e in events)
+    for k in range(orb):
+        for c in range(pieces(k)):
+            events.append((end + 1 + k, c, "fold", k, c, 0))
     events.sort(key=lambda e: e[:2])
 
-    sums, heads, came, result, last = {}, {}, {}, None, None
-    for _, _, kind, k, a1, a2, c in events:
+    came_rows, sums, heads, came, result, last = {}, {}, {}, {}, None, None
+    for _, _, kind, k, what, c in events:
         extra = 0 if k else EXTRA
-        if kind == "product":
-            q = a1
+        piece = height // pieces(k)
+        if kind == "rows":
+            last, came_rows[k, what] = rows_to_send(k, what, last)
+        elif kind == "product":
+            q = what
             if k == 0:
                 index = jnp.broadcast_to(own_blocks[q], (sub,))
                 rows = views
             else:
                 index = jnp.arange(sub, dtype=jnp.int32)
                 rows = [came_rows[k, q]] * sub
-            sums[k, q], *heads[k, q] = row_product(after(index, last), rows, cols, halves, extra)
+            flops = 2 * sub * height * length * depth
+            sums[k, q], *heads[k, q] = row_product(after(index, last), rows, cols, pieces(k), extra, flops if k else COST)
             last = sums[k, q]
         elif kind == "hop":
-            rank, step = a1, a2
-            pairs, position, final = line.hop(k, rank, step)
-            used = sorted(set(position.values()))
-            flags = [lookup([position.get(i) == q for i in range(aux * orb)], place) for q in used]
-            piece = height // pieces(k, rank)
-            if step == 0 and len(used) == 1 and pieces(k, rank) == halves:
-                value = heads[k, used[0]][c]
-                value = after(value, last) if c else value
-            elif k == 0:
-                index, value = own_blocks[used[0]], sums[k, used[0]]
-                head = heads[k, used[0]][c]
-                for q, flag in zip(used[1:], flags[1:]):
-                    index = jnp.where(flag > 0, own_blocks[q], index)
-                    if step:
-                        value = jnp.where(flag > 0, sums[k, q], value)
-                    else:
-                        head = jnp.where(flag > 0, heads[k, q][c], head)
-                if step:
-                    index = after((index * height)[None], last)
-                    value = forward(index, value, came[k, rank, step - 1, c], piece, c)
-                else:
-                    value = after(head, last)
-                last = value
+            pairs, choices = [], []
+            for rank, step in what:
+                more, position, _ = line.hop(k, rank, step)
+                pairs += more
+                for q in sorted(set(position.values())):
+                    choices.append((rank, step, q, [position.get(i) == q for i in range(aux * orb)]))
+            if step == 0:
+                value = heads[k, choices[0][2]][c]
+                for _, _, q, table in choices[1:]:
+                    value = jnp.where(lookup(table, place) > 0, heads[k, q][c], value)
+                value = after(value, last) if c or len(choices) > 1 else value
             else:
-                value = sums[k, used[0]] if step else after(sums[k, used[0]], last)
-                value = value[c * piece : (c + 1) * piece]
-                for q, flag in zip(used[1:], flags[1:]):
-                    value = jnp.where(flag > 0, sums[k, q][c * piece : (c + 1) * piece], value)
-                if step:
-                    value = value + after(came[k, rank, step - 1, c], last).astype(jnp.float32)
-                value = value.astype(jnp.bfloat16)
-                last = value
-            came[k, rank, step, c] = lax.ppermute(value, ("aux", "orb"), pairs)
+                flags = [lookup(table, place) for _, _, _, table in choices]
+                start = sum(flag * own_blocks[q] for flag, (_, _, q, _) in zip(flags, choices)) * height
+                value = forward(
+                    after(jnp.stack(flags + [start]), last),
+                    [sums[k, q] for _, _, q, _ in choices],
+                    [came[k, rank, step - 1, c] for rank, step, _, _ in choices],
+                    piece,
+                    c,
+                )
+            last = value
+            arrived = lax.ppermute(value, ("aux", "orb"), pairs)
+            for rank, step in what:
+                came[k, rank, step, c] = arrived
         else:
-            at, count = a1, a2
-            piece = height // count
-            rows = slice(at * piece, (at + 1) * piece)
-            flag = lookup([z_ in line.targets(k, o_) for z_ in range(aux) for o_ in range(orb)], place)
-            total = jnp.where(flag > 0, after(sums[k, owned - 1], last)[rows], 0.0)
-            for k_, rank, step in finals:
-                if k_ != k:
-                    continue
-                final = line.hop(k, rank, step)[2]
-                flag = lookup([i in final for i in range(aux * orb)], place)
-                sent = height // pieces(k, rank)
-                first = at * piece % sent
-                message = came[k, rank, step, at * piece // sent]
-                term = message[first : first + piece].astype(jnp.float32)
-                if extra:
-                    start = (lax.rem(z, owned) * sub + s) * height + at * piece
-                    row = lax.broadcasted_iota(jnp.int32, total.shape, 0) + start
-                    col = lax.broadcasted_iota(jnp.int32, total.shape, 1)
-                    term = term + jnp.where(row == col, message[sent : sent + 1].astype(jnp.float32), 0.0)
-                total = total + jnp.where(flag > 0, term, 0.0)
-            if result is None:
-                result = jnp.zeros((height, length), jnp.float32)
-            if k:
-                total = total + result[rows]
-            result = lax.dynamic_update_slice(result, total, (at * piece, 0))
+            flags = [[z_ in line.targets(k, o_) for z_ in range(aux) for o_ in range(orb)]]
+            parts = []
+            for k_, group in finals:
+                if k_ == k:
+                    places = {i for member in group for i in line.hop(k, *member)[2]}
+                    flags.append([i in places for i in range(aux * orb)])
+                    parts.append(came[(k,) + group[0] + (what,)])
+            flags = [lookup(table, place) for table in flags]
+            flags = jnp.stack(flags + [(lax.rem(z, owned) * sub + s) * height + what * piece])
+            mine = sums[k, owned - 1]
+            before = mine if result is None else result
+            result = fold(after(flags, last), before, mine, parts, piece, what, extra, result is None)
             last = result
     return result
 

time: 410 us -> 285 us (0.70)
  Pallas kernels: 203 us -> 99.8 us
  starting transfers between devices: 58.4 us -> 48.1 us
  other arithmetic: 22.7 us -> 15.8 us
  waiting for transfers between devices: 91.8 us -> 85.4 us
    pallas_call x7 -> x11, Pallas kernels: 141 us -> 42.8 us  [the longest x6 22.5 us: forward(): pl.pallas_call(functools.partial(forward_kernel, choices=choices, first=c...]
    ppermute x26 -> x14, waiting for transfers between devices: 73.4 us -> 65.1 us  [the longest x12 50.8 us: shards(): arrived = lax.ppermute(value, ('aux', 'orb'), pairs)]
    another operation x1 -> x7, other arithmetic: 0.61 us -> 7.76 us  [the longest x4 3.94 us: shards(): jnp.stack(flags + [start])]
    convert_element_type x12 -> x0, other arithmetic: 7.01 us -> none  [shards(): value = value.astype(jnp.bfloat16)]
    ppermute x1, waiting for transfers between devices: 8.9 us -> 3.03 us  [shards(): lax.ppermute(after(firsts[k - 1], early), 'aux', [(i, i ^ 1) for i in ran...]
    ppermute x1, waiting for transfers between devices: 5.17 us -> 11 us  [shards(): rests.append(lax.ppermute(coefficients[2 * share * side:], 'orb', pairs))]
    ppermute x26 -> x14, starting transfers between devices: 48.5 us -> 43.3 us  [the longest x12 41.3 us: shards(): arrived = lax.ppermute(value, ('aux', 'orb'), pairs)]
    ppermute x1, starting transfers between devices: 7.79 us -> 2.67 us  [shards(): lax.ppermute(after(firsts[k - 1], early), 'aux', [(i, i ^ 1) for i in ran...]
  transfers between devices with their start and end apart: 30 -> 18, of which waited for: 14 -> 10; matrix products, arithmetic and copies ran while one was open for 7% -> 8% of each run, Pallas kernels for 15% -> 29%
where the time goes in v4:
time: 285 us; the launch traced here: 282 us
  Pallas kernels  99.8 us (35%)
  waiting for transfers between devices  85.4 us (30%)
  starting transfers between devices  48.1 us (17%)
  local copies, waits for them, and re-layouts  28.2 us (10%)
  other arithmetic  15.8 us (6%)
  between operations  4.68 us (2%)
    ppermute x12, waiting for transfers between devices, shards(): arrived = lax.ppermute(value, ('aux', 'orb'), pairs)  50.8 us
    ppermute x12, starting transfers between devices, shards(): arrived = lax.ppermute(value, ('aux', 'orb'), pairs)  41.3 us
    pallas_call x4, Pallas kernels, row_product(): pl.pallas_call(functools.partial(product_kernel, parts=parts, extra=extra...  37.4 us
    pallas_call x6, Pallas kernels, forward(): pl.pallas_call(functools.partial(forward_kernel, choices=choices, first=c...  22.5 us
    pallas_call x2, Pallas kernels, transform(): pl.pallas_call(functools.partial(transform_kernel, parts=parts, last=last...  19.6 us
    unnamed x62, local copies, waits for them, and re-layouts  19.5 us
    ppermute x2, waiting for transfers between devices, rows_to_send(): lax.ppermute(message, 'orb', [((b + k) % orb, b) for b in range(orb)])  14.3 us
    pallas_call x3, Pallas kernels, fold(): pl.pallas_call(functools.partial(fold_kernel, extra=extra, first=first),...  14.3 us
  transfers between devices with their start and end apart: 18, of which 10 were waited for; matrix products, arithmetic and copies ran while one was open for 8% of the time, Pallas kernels for 29%

profile of v4, /device:TPU:20, one launch (start us, length us, event | category | flops | bytes accessed | tf_op | source)
XLA Modules:
  0.0 282.0 jit_solution(6908497027863536683)
XLA Ops:
  0.0 2.1 constant_dynamic-slice_fusion
  2.2 1.5 collective-permute-start
  3.7 2.1 slice.3
  8.7 1.3 select_reduce_fusion
  10.1 8.5 %shard_map.262.refs_3_ = f32[16,256,512]{2,1,0:T(8,128)S(1)} custom-call(s32[16,16]{1,0:T(8,128)S(1)} %get-tuple-element.62.order, s32[16,16]{1,0:T(8,128)S(1)} %get-tuple-element.61.columns, s32[16,2]{1,0:T(8,128)S(1)} %stack.79.bounds, bf16[2,16,16,128,128]{4,3,2,1,0:T(8,128)(2,1)} %x_ref.3, bf16[2048,512]{1,0:T(8,128)(2,1)S(1)} %copy-done.15), custom_call_target="tpu_custom_call" | custom-call | flops 1024 | bytes 1024 | tf_op jit(solution)/shard_map/pallas_call | solution.py:112
  18.6 3.3 %copy-done.10 = f32[16,256,512]{2,1,0:T(8,128)} copy-done((f32[16,256,512]{2,1,0:T(8,128)}, f32[16,256,512]{2,1,0:T(8,128)S(1)}, u32[]{:S(2)}) %copy-start.10) | copy-done | bytes 8388632
  21.9 2.7 collective-permute-start.2
  24.7 11.0 %collective-permute-done.1.refs_1_ = bf16[768,512]{1,0:T(8,128)(2,1)S(1)} collective-permute-done((bf16[768,512]{1,0:T(8,128)(2,1)}, bf16[768,512]{1,0:T(8,128)(2,1)S(1)}, u32[]{:S(2)}, u32[]{:S(2)}) %collective-permute-start.1) | collective-permute-done | bytes 786464 | tf_op jit(solution)/shard_map/ppermute | solution.py:383
  35.7 3.0 %collective-permute-done.2.refs_2_ = bf16[640,512]{1,0:T(8,128)(2,1)S(1)} collective-permute-done((bf16[640,512]{1,0:T(8,128)(2,1)S(1)}, bf16[640,512]{1,0:T(8,128)(2,1)S(1)}, u32[]{:S(2)}, u32[]{:S(2)}) %collective-permute-start.2) | collective-permute-done | bytes 655392 | tf_op jit(solution)/shard_map/ppermute | solution.py:413
  38.7 3.4 %copy-done.11 = f32[16,256,512]{2,1,0:T(8,128)S(1)} copy-done((f32[16,256,512]{2,1,0:T(8,128)S(1)}, f32[16,256,512]{2,1,0:T(8,128)}, u32[]{:S(2)}) %copy-start.11) | copy-done | bytes 8388632
  42.1 11.2 %shard_map.263.refs_2_ = bf16[2048,1024]{1,0:T(8,128)(2,1)} custom-call(s32[16,16]{1,0:T(8,128)S(1)} %get-tuple-element.62.order, s32[16,16]{1,0:T(8,128)S(1)} %get-tuple-element.61.columns, s32[16,2]{1,0:T(8,128)S(1)} %copy.37.bounds, bf16[2,16,16,128,128]{4,3,2,1,0:T(8,128)(2,1)} %x_ref.3, bf16[640,512]{1,0:T(8,128)(2,1)S(1)} %collective-permute-done.refs_0_, ...), custom_call_target="tpu_custom_call" | custom-call | flops 1024 | bytes 1024 | tf_op jit(solution)/shard_map/pallas_call | solution.py:112
  54.6 6.2 %collective-permute-done.3.refs_3_ = bf16[2048,1024]{1,0:T(8,128)(2,1)} collective-permute-done((bf16[2048,1024]{1,0:T(8,128)(2,1)}, bf16[2048,1024]{1,0:T(8,128)(2,1)}, u32[]{:S(2)}, u32[]{:S(2)}) %collective-permute-start.3) | collective-permute-done | bytes 4194336 | tf_op jit(solution)/shard_map/ppermute | solution.py:431
  60.9 2.6 shard_map.264
  63.4 1.6 collective-permute-start.4
  65.1 10.3 %shard_map.265 = (f32[512,2048]{1,0:T(8,128)S(1)}, bf16[528,2048]{1,0:T(8,128)(2,1)}) custom-call(s32[2]{0:T(128)S(1)} %broadcast_in_dim.42.index, bf16[4,512,1024]{2,1,0:T(8,128)(2,1)} %bitcast.14.refs_0_, bf16[4,512,1024]{2,1,0:T(8,128)(2,1)} %bitcast.15.refs_1_, bf16[2048,1024]{1,0:T(8,128)(2,1)} %shard_map.263.refs_2_, ...), custom_call_target="tpu_custom_call" | custom-call | flops 1024 | bytes 1024 | tf_op jit(solution)/shard_map/pallas_call | solution.py:277
  75.3 2.0 copy-done.12
  79.9 8.8 %shard_map.266 = (f32[512,2048]{1,0:T(8,128)S(1)}, bf16[528,2048]{1,0:T(8,128)(2,1)S(1)}) custom-call(s32[2]{0:T(128)S(1)} %broadcast_in_dim.41.index, bf16[4,512,1024]{2,1,0:T(8,128)(2,1)} %bitcast.14.refs_0_, bf16[4,512,1024]{2,1,0:T(8,128)(2,1)} %bitcast.15.refs_1_, bf16[2048,1024]{1,0:T(8,128)(2,1)} %shard_map.263.refs_2_, ...), custom_call_target="tpu_custom_call" | custom-call | flops 1024 | bytes 1024 | tf_op jit(solution)/shard_map/pallas_call | solution.py:277
  88.7 2.0 copy-done.7
  90.6 3.5 %shard_map.270 = bf16[2,512,1024]{2,1,0:T(8,128)(2,1)} custom-call(s32[1]{0:T(128)} %bitcast.17.index, bf16[4,512,1024]{2,1,0:T(8,128)(2,1)} %bitcast.14.refs_0_, bf16[4,512,1024]{2,1,0:T(8,128)(2,1)} %bitcast.15.refs_1_), custom_call_target="tpu_custom_call" | custom-call | flops 1024 | bytes 1024 | tf_op jit(solution)/shard_map/pallas_call | solution.py:144
  97.9 14.3 %collective-permute-done.4.refs_0_.refs_1_ = bf16[2,512,1024]{2,1,0:T(8,128)(2,1)} collective-permute-done((bf16[2,512,1024]{2,1,0:T(8,128)(2,1)}, bf16[2,512,1024]{2,1,0:T(8,128)(2,1)}, u32[]{:S(2)}, u32[]{:S(2)}) %collective-permute-start.4) | collective-permute-done | bytes 2097184 | tf_op jit(solution)/shard_map/ppermute | solution.py:437
  112.2 9.5 %shard_map.267 = (f32[512,2048]{1,0:T(8,128)S(1)}, bf16[256,2048]{1,0:T(8,128)(2,1)}, bf16[256,2048]{1,0:T(8,128)(2,1)S(1)}) custom-call(s32[2]{0:T(128)S(1)} %iota.26.index, bf16[2,512,1024]{2,1,0:T(8,128)(2,1)} %collective-permute-done.4.refs_0_.refs_1_, bf16[2,512,1024]{2,1,0:T(8,128)(2,1)} %collective-permute-done.4.refs_0_.refs_1_, ...), custom_call_target="tpu_custom_call" | custom-call | flops 4294967296 | bytes 1024 | tf_op jit(solution)/shard_map/pallas_call | solution.py:277
  121.8 7.7 %collective-permute-done.5.refs_1_.refs_2_ = bf16[528,2048]{1,0:T(8,128)(2,1)S(1)} collective-permute-done((bf16[528,2048]{1,0:T(8,128)(2,1)}, bf16[528,2048]{1,0:T(8,128)(2,1)S(1)}, u32[]{:S(2)}, u32[]{:S(2)}) %collective-permute-start.5) | collective-permute-done | bytes 2162720 | tf_op jit(solution)/shard_map/ppermute | solution.py:508
  129.4 3.6 %shard_map.268 = bf16[528,2048]{1,0:T(8,128)(2,1)} custom-call(s32[2]{0:T(128)S(1)} %pad_add_fusion.5.flags, f32[512,2048]{1,0:T(8,128)S(1)} %copy-done.13, bf16[528,2048]{1,0:T(8,128)(2,1)S(1)} %collective-permute-done.5.refs_1_.refs_2_), custom_call_target="tpu_custom_call" | custom-call | flops 1024 | bytes 1024 | tf_op jit(solution)/shard_map/pallas_call | solution.py:196
  133.0 12.1 %collective-permute-start.9 = (bf16[528,2048]{1,0:T(8,128)(2,1)}, bf16[528,2048]{1,0:T(8,128)(2,1)}, u32[]{:S(2)}, u32[]{:S(2)}) collective-permute-start(bf16[528,2048]{1,0:T(8,128)(2,1)} %shard_map.268), channel_id=1, source_target_pairs={{8,4},{6,10},{9,5},{7,11},{24,20},{22,26},{25,21},{23,27}} | collective-permute-start | bytes 6488072 | tf_op jit(solution)/shard_map/ppermute | solution.py:508
  146.9 1.6 collective-permute-start.8
  152.4 2.2 copy-done.4
  154.6 2.2 shard_map.269
  156.8 8.8 %shard_map.271 = (f32[512,2048]{1,0:T(8,128)S(1)}, bf16[256,2048]{1,0:T(8,128)(2,1)S(1)}, bf16[256,2048]{1,0:T(8,128)(2,1)S(1)}) custom-call(s32[2]{0:T(128)S(1)} %iota.25.index, bf16[2,512,1024]{2,1,0:T(8,128)(2,1)} %collective-permute-done.7.refs_0_.refs_1_, bf16[2,512,1024]{2,1,0:T(8,128)(2,1)} %collective-permute-done.7.refs_0_.refs_1_, ...), custom_call_target="tpu_custom_call" | custom-call | flops 4294967296 | bytes 1024 | tf_op jit(solution)/shard_map/pallas_call | solution.py:277
  165.6 3.2 %broadcast_select_fusion = bf16[256,2048]{1,0:T(8,128)(2,1)} fusion(bf16[256,2048]{1,0:T(8,128)(2,1)S(1)} %get-tuple-element.50, bf16[256,2048]{1,0:T(8,128)(2,1)} %get-tuple-element.40, pred[]{:T(512)} %bitcast.7), kind=kLoop, calls=%fused_computation | loop fusion | flops 524288 | bytes 3145729 | tf_op jit(solution)/shard_map/jit(_where)/select_n | solution.py:495
  168.9 1.5 collective-permute-start.12
  171.7 3.1 %shard_map.272 = bf16[256,2048]{1,0:T(8,128)(2,1)} custom-call(s32[2]{0:T(128)S(1)} %pad_add_fusion.4.flags, f32[512,2048]{1,0:T(8,128)S(1)} %copy-done.5, bf16[256,2048]{1,0:T(8,128)(2,1)} %collective-permute-done.8.refs_1_), custom_call_target="tpu_custom_call" | custom-call | flops 1024 | bytes 1024 | tf_op jit(solution)/shard_map/pallas_call | solution.py:196
  175.5 13.5 %collective-permute-done.9.refs_1_ = bf16[528,2048]{1,0:T(8,128)(2,1)} collective-permute-done((bf16[528,2048]{1,0:T(8,128)(2,1)}, bf16[528,2048]{1,0:T(8,128)(2,1)}, u32[]{:S(2)}, u32[]{:S(2)}) %collective-permute-start.9) | collective-permute-done | bytes 2162720 | tf_op jit(solution)/shard_map/ppermute | solution.py:508
  189.0 5.2 %shard_map.273 = bf16[528,2048]{1,0:T(8,128)(2,1)} custom-call(s32[3]{0:T(128)S(1)} %pad_add_fusion.6.flags, f32[512,2048]{1,0:T(8,128)S(1)} %copy-done.14, bf16[528,2048]{1,0:T(8,128)(2,1)} %collective-permute-done.9.refs_1_, f32[512,2048]{1,0:T(8,128)S(1)} %copy-done.8, bf16[528,2048]{1,0:T(8,128)(2,1)} %collective-permute-done.10.refs_3_), custom_call_target="tpu_custom_call" | custom-call | flops 1024 | bytes 1024 | tf_op jit(solution)/shard_map/pallas_call | solution.py:196
  194.2 12.3 %collective-permute-start.15 = (bf16[528,2048]{1,0:T(8,128)(2,1)}, bf16[528,2048]{1,0:T(8,128)(2,1)}, u32[]{:S(2)}, u32[]{:S(2)}) collective-permute-start(bf16[528,2048]{1,0:T(8,128)(2,1)} %shard_map.273), channel_id=1, source_target_pairs={{4,0},{10,14},{8,4},{6,10},{5,1},{11,15},{9,5},{7,11},{20,16},{26,... | collective-permute-start | bytes 6488072 | tf_op jit(solution)/shard_map/ppermute | solution.py:508
  212.2 2.2 copy-done.1
  214.3 2.2 copy-done.6
  216.5 4.1 %shard_map.274 = bf16[256,2048]{1,0:T(8,128)(2,1)} custom-call(s32[3]{0:T(128)S(1)} %pad_add_fusion.3.flags, f32[512,2048]{1,0:T(8,128)S(1)} %copy-done.6, bf16[256,2048]{1,0:T(8,128)(2,1)} %collective-permute-done.11.refs_1_, f32[512,2048]{1,0:T(8,128)S(1)} %copy-done.1, bf16[256,2048]{1,0:T(8,128)(2,1)S(1)} %collective-permute-done.12.refs_3_.refs_2_), custom_call_target="tpu_custom_call" | custom-call | flops 1024 | bytes 1024 | tf_op jit(solution)/shard_map/pallas_call | solution.py:196
  220.6 4.7 %collective-permute-start.16 = (bf16[256,2048]{1,0:T(8,128)(2,1)}, bf16[256,2048]{1,0:T(8,128)(2,1)}, u32[]{:S(2)}, u32[]{:S(2)}) collective-permute-start(bf16[256,2048]{1,0:T(8,128)(2,1)} %shard_map.274), channel_id=1, source_target_pairs={{8,12},{6,2},{4,8},{10,6},{9,13},{7,3},{5,9},{11,7},{24,28},{22,18... | collective-permute-start | bytes 3145736 | tf_op jit(solution)/shard_map/ppermute | solution.py:508
  225.3 10.7 %collective-permute-done.13.refs_1_ = bf16[256,2048]{1,0:T(8,128)(2,1)} collective-permute-done((bf16[256,2048]{1,0:T(8,128)(2,1)}, bf16[256,2048]{1,0:T(8,128)(2,1)}, u32[]{:S(2)}, u32[]{:S(2)}) %collective-permute-start.13) | collective-permute-done | bytes 1048608 | tf_op jit(solution)/shard_map/ppermute | solution.py:508
  236.0 4.2 %shard_map.275 = bf16[256,2048]{1,0:T(8,128)(2,1)} custom-call(s32[3]{0:T(128)S(1)} %pad_add_fusion.3.flags, f32[512,2048]{1,0:T(8,128)S(1)} %copy-done.6, bf16[256,2048]{1,0:T(8,128)(2,1)} %collective-permute-done.13.refs_1_, f32[512,2048]{1,0:T(8,128)S(1)} %copy-done.1, bf16[256,2048]{1,0:T(8,128)(2,1)} %collective-permute-done.14.refs_3_.refs_2_), custom_call_target="tpu_custom_call" | custom-call | flops 1024 | bytes 1024 | tf_op jit(solution)/shard_map/pallas_call | solution.py:196
  240.2 1.9 collective-permute-start.17
  244.5 1.3 pad_add_fusion.7.flags
  247.2 2.2 copy-done.9
  249.4 4.5 %shard_map.276.refs_0_ = f32[512,2048]{1,0:T(8,128)} custom-call(s32[4]{0:T(128)S(1)} %add_add_fusion.flags, f32[512,2048]{1,0:T(8,128)S(1)} %copy-done.9, f32[512,2048]{1,0:T(8,128)S(1)} %copy-done.9, bf16[528,2048]{1,0:T(8,128)(2,1)S(1)} %collective-permute-done.5.refs_1_.refs_2_, bf16[528,2048]{1,0:T(8,128)(2,1)} %collective-permute-done.15.refs_3_), custom_call_target="tpu_custom_call" | custom-call | flops 1024 | bytes 1024 | tf_op jit(solution)/shard_map/pallas_call | solution.py:235
  253.9 4.6 %collective-permute-done.16.refs_3_ = bf16[256,2048]{1,0:T(8,128)(2,1)} collective-permute-done((bf16[256,2048]{1,0:T(8,128)(2,1)}, bf16[256,2048]{1,0:T(8,128)(2,1)}, u32[]{:S(2)}, u32[]{:S(2)}) %collective-permute-start.16) | collective-permute-done | bytes 1048608 | tf_op jit(solution)/shard_map/ppermute | solution.py:508
  258.5 4.8 %shard_map.277.refs_0_ = f32[512,2048]{1,0:T(8,128)} custom-call(s32[4]{0:T(128)S(1)} %pad_add_fusion.7.flags, f32[512,2048]{1,0:T(8,128)} %shard_map.276.refs_0_, f32[512,2048]{1,0:T(8,128)S(1)} %copy-done.2, bf16[256,2048]{1,0:T(8,128)(2,1)S(1)} %collective-permute-done.12.refs_3_.refs_2_, ...), custom_call_target="tpu_custom_call", output_to_operand_aliasing={{}: (1, {})} | custom-call | flops 1024 | bytes 1024 | tf_op jit(solution)/shard_map/pallas_call | solution.py:235
  263.3 13.7 %collective-permute-done.17.refs_3_ = bf16[256,2048]{1,0:T(8,128)(2,1)} collective-permute-done((bf16[256,2048]{1,0:T(8,128)(2,1)}, bf16[256,2048]{1,0:T(8,128)(2,1)}, u32[]{:S(2)}, u32[]{:S(2)}) %collective-permute-start.17) | collective-permute-done | bytes 1048608 | tf_op jit(solution)/shard_map/ppermute | solution.py:508
  277.0 5.0 %shard_map.278 = f32[512,2048]{1,0:T(8,128)} custom-call(s32[4]{0:T(128)S(1)} %pad_add_fusion.1.flags, f32[512,2048]{1,0:T(8,128)} %shard_map.277.refs_0_, f32[512,2048]{1,0:T(8,128)S(1)} %copy-done.2, bf16[256,2048]{1,0:T(8,128)(2,1)} %collective-permute-done.14.refs_3_.refs_2_, ...), custom_call_target="tpu_custom_call", output_to_operand_aliasing={{}: (1, {})} | custom-call | flops 1024 | bytes 1024 | tf_op jit(solution)/shard_map/pallas_call | solution.py:235
  (97 shorter events, 23.3 us)
Async XLA Ops:
  0.0 10.1 %copy-start.15 = (bf16[2048,512]{1,0:T(8,128)(2,1)S(1)}, bf16[2048,512]{1,0:T(8,128)(2,1)}, u32[]{:S(2)}) copy-start(bf16[2048,512]{1,0:T(8,128)(2,1)} %refs_0_.1) | copy-start | bytes 6291460
  0.0 6.3 %copy-start.19 = (s32[1,16,16]{2,1,0:T(8,128)S(1)}, s32[1,16,16]{2,1,0:T(8,128)}, u32[]{:S(2)}) copy-start(s32[1,16,16]{2,1,0:T(8,128)} %param.29) | copy-start | bytes 3076
  0.0 6.3 %copy-start.22 = (s32[1,16]{1,0:T(1,128)S(1)}, s32[1,16]{1,0:T(1,128)}, u32[]{:S(2)}) copy-start(s32[1,16]{1,0:T(1,128)} %param.30) | copy-start | bytes 196
  2.2 19.7 %collective-permute-start = (bf16[640,512]{1,0:T(8,128)(2,1)}, bf16[640,512]{1,0:T(8,128)(2,1)S(1)}, u32[]{:S(2)}, u32[]{:S(2)}) collective-permute-start(bf16[640,512]{1,0:T(8,128)(2,1)} %constant_dynamic-slice_fusion), channel_id=1, source_target_pairs={{2,0},{0,2},{3,1},{1,3},{6,4},{4,6},{7,5},{5,7},{10,8},{8,10},{11,... | collective-permute-start | bytes 1966088 | tf_op jit(solution)/shard_map/ppermute | solution.py:382
  5.7 30.0 %collective-permute-start.1 = (bf16[768,512]{1,0:T(8,128)(2,1)}, bf16[768,512]{1,0:T(8,128)(2,1)S(1)}, u32[]{:S(2)}, u32[]{:S(2)}) collective-permute-start(bf16[768,512]{1,0:T(8,128)(2,1)} %slice.3), channel_id=1, source_target_pairs={{2,0},{0,2},{3,1},{1,3},{6,4},{4,6},{7,5},{5,7},{10,8},{8,10},{11,... | collective-permute-start | bytes 2359304 | tf_op jit(solution)/shard_map/ppermute | solution.py:383
  10.1 14.5 %copy-start.21 = (s32[16]{0:T(128)S(1)}, s32[16]{0:T(128)}, u32[]{:S(2)}) copy-start(s32[16]{0:T(128)} %copy-done.20) | copy-start | bytes 196
  10.1 14.5 %copy-start.23 = (s32[16]{0:T(128)S(1)}, s32[16]{0:T(128)}, u32[]{:S(2)}) copy-start(s32[16]{0:T(128)} %get-tuple-element.64) | copy-start | bytes 196
  18.6 3.3 %copy-start.10 = (f32[16,256,512]{2,1,0:T(8,128)}, f32[16,256,512]{2,1,0:T(8,128)S(1)}, u32[]{:S(2)}) copy-start(f32[16,256,512]{2,1,0:T(8,128)S(1)} %shard_map.262.refs_3_) | copy-start | bytes 25165828
  21.9 16.8 %collective-permute-start.2 = (bf16[640,512]{1,0:T(8,128)(2,1)S(1)}, bf16[640,512]{1,0:T(8,128)(2,1)S(1)}, u32[]{:S(2)}, u32[]{:S(2)}) collective-permute-start(bf16[640,512]{1,0:T(8,128)(2,1)S(1)} %collective-permute-done.refs_0_), channel_id=1, source_target_pairs={{0,4},{4,0},{8,12},{12,8},{1,5},{5,1},{9,13},{13,9},{2,6},{6,2},{1... | collective-permute-start | bytes 1966088 | tf_op jit(solution)/shard_map/ppermute | solution.py:413
  24.6 28.8 %copy-start.30 = (s32[8]{0:T(128)S(1)}, s32[8]{0:T(128)}, u32[]{:S(2)}) copy-start(s32[8]{0:T(128)} %constant.76.clone) | copy-start | bytes 100
  38.7 3.4 %copy-start.11 = (f32[16,256,512]{2,1,0:T(8,128)S(1)}, f32[16,256,512]{2,1,0:T(8,128)}, u32[]{:S(2)}) copy-start(f32[16,256,512]{2,1,0:T(8,128)} %copy-done.10) | copy-start | bytes 25165828
  53.3 7.6 %collective-permute-start.3 = (bf16[2048,1024]{1,0:T(8,128)(2,1)}, bf16[2048,1024]{1,0:T(8,128)(2,1)}, u32[]{:S(2)}, u32[]{:S(2)}) collective-permute-start(bf16[2048,1024]{1,0:T(8,128)(2,1)} %shard_map.263.refs_2_), channel_id=1, source_target_pairs={{1,0},{0,1},{3,2},{2,3},{5,4},{4,5},{7,6},{6,7},{9,8},{8,9},{11,10... | collective-permute-start | bytes 12582920 | tf_op jit(solution)/shard_map/ppermute | solution.py:431
  63.4 48.8 %collective-permute-start.4 = (bf16[2,512,1024]{2,1,0:T(8,128)(2,1)}, bf16[2,512,1024]{2,1,0:T(8,128)(2,1)}, u32[]{:S(2)}, u32[]{:S(2)}) collective-permute-start(bf16[2,512,1024]{2,1,0:T(8,128)(2,1)} %shard_map.264), channel_id=1, source_target_pairs={{2,0},{0,2},{3,1},{1,3},{6,4},{4,6},{7,5},{5,7},{10,8},{8,10},{11,... | collective-permute-start | bytes 6291464 | tf_op jit(solution)/shard_map/ppermute | solution.py:437
  65.0 13.6 %copy-start.29 = (s32[8]{0:T(128)S(1)}, s32[8]{0:T(128)}, u32[]{:S(2)}) copy-start(s32[8]{0:T(128)} %constant.77.clone) | copy-start | bytes 100
  75.3 2.0 copy-start.12
  77.4 52.1 %collective-permute-start.5 = (bf16[528,2048]{1,0:T(8,128)(2,1)}, bf16[528,2048]{1,0:T(8,128)(2,1)S(1)}, u32[]{:S(2)}, u32[]{:S(2)}) collective-permute-start(bf16[528,2048]{1,0:T(8,128)(2,1)} %get-tuple-element.35), channel_id=1, source_target_pairs={{0,4},{12,8},{2,6},{14,10},{1,5},{13,9},{3,7},{15,11},{16,20},{28,... | collective-permute-start | bytes 6488072 | tf_op jit(solution)/shard_map/ppermute | solution.py:508
  88.7 2.0 copy-start.7
  90.6 3.5 %copy-start.18 = (bf16[528,2048]{1,0:T(8,128)(2,1)}, bf16[528,2048]{1,0:T(8,128)(2,1)S(1)}, u32[]{:S(2)}) copy-start(bf16[528,2048]{1,0:T(8,128)(2,1)S(1)} %get-tuple-element.37) | copy-start | bytes 6488068
  90.6 3.9 %copy-start.28 = (s32[8]{0:T(128)S(1)}, s32[8]{0:T(128)}, u32[]{:S(2)}) copy-start(s32[8]{0:T(128)} %constant.78.clone) | copy-start | bytes 100
  94.1 62.7 %collective-permute-start.7 = (bf16[2,512,1024]{2,1,0:T(8,128)(2,1)}, bf16[2,512,1024]{2,1,0:T(8,128)(2,1)}, u32[]{:S(2)}, u32[]{:S(2)}) collective-permute-start(bf16[2,512,1024]{2,1,0:T(8,128)(2,1)} %shard_map.270), channel_id=1, source_target_pairs={{2,0},{0,2},{3,1},{1,3},{6,4},{4,6},{7,5},{5,7},{10,8},{8,10},{11,... | collective-permute-start | bytes 6291464 | tf_op jit(solution)/shard_map/ppermute | solution.py:437
  96.6 78.8 %collective-permute-start.10 = (bf16[528,2048]{1,0:T(8,128)(2,1)}, bf16[528,2048]{1,0:T(8,128)(2,1)}, u32[]{:S(2)}, u32[]{:S(2)}) collective-permute-start(bf16[528,2048]{1,0:T(8,128)(2,1)} %copy-done.18), channel_id=1, source_target_pairs={{12,8},{2,6},{13,9},{3,7},{28,24},{18,22},{29,25},{19,23}} | collective-permute-start | bytes 6488072 | tf_op jit(solution)/shard_map/ppermute | solution.py:508
  112.2 17.2 %copy-start.13 = (f32[512,2048]{1,0:T(8,128)S(1)}, f32[512,2048]{1,0:T(8,128)}, u32[]{:S(2)}) copy-start(f32[512,2048]{1,0:T(8,128)} %copy-done.12) | copy-start | bytes 12582916
  121.8 11.3 %copy-start.3 = (f32[512,2048]{1,0:T(8,128)}, f32[512,2048]{1,0:T(8,128)S(1)}, u32[]{:S(2)}) copy-start(f32[512,2048]{1,0:T(8,128)S(1)} %get-tuple-element.45.refs_0_) | copy-start | bytes 12582916
  121.8 11.3 %copy-start.16 = (bf16[256,2048]{1,0:T(8,128)(2,1)}, bf16[256,2048]{1,0:T(8,128)(2,1)S(1)}, u32[]{:S(2)}) copy-start(bf16[256,2048]{1,0:T(8,128)(2,1)S(1)} %get-tuple-element.43) | copy-start | bytes 3145732
  129.4 16.4 %copy-start.27 = (s32[8]{0:T(128)S(1)}, s32[8]{0:T(128)}, u32[]{:S(2)}) copy-start(s32[8]{0:T(128)} %constant.79.clone) | copy-start | bytes 100
  129.4 20.4 %copy-start.26 = (s32[8]{0:T(128)S(1)}, s32[8]{0:T(128)}, u32[]{:S(2)}) copy-start(s32[8]{0:T(128)} %constant.80.clone) | copy-start | bytes 100
  133.0 55.9 %collective-permute-start.9 = (bf16[528,2048]{1,0:T(8,128)(2,1)}, bf16[528,2048]{1,0:T(8,128)(2,1)}, u32[]{:S(2)}, u32[]{:S(2)}) collective-permute-start(bf16[528,2048]{1,0:T(8,128)(2,1)} %shard_map.268), channel_id=1, source_target_pairs={{8,4},{6,10},{9,5},{7,11},{24,20},{22,26},{25,21},{23,27}} | collective-permute-start | bytes 6488072 | tf_op jit(solution)/shard_map/ppermute | solution.py:508
  145.1 7.3 %collective-permute-start.6 = (bf16[256,2048]{1,0:T(8,128)(2,1)}, bf16[256,2048]{1,0:T(8,128)(2,1)S(1)}, u32[]{:S(2)}, u32[]{:S(2)}) collective-permute-start(bf16[256,2048]{1,0:T(8,128)(2,1)} %get-tuple-element.40), channel_id=1, source_target_pairs={{0,4},{14,10},{1,5},{15,11},{16,20},{30,26},{17,21},{31,27}} | collective-permute-start | bytes 3145736 | tf_op jit(solution)/shard_map/ppermute | solution.py:508
  146.9 24.8 %collective-permute-start.8 = (bf16[256,2048]{1,0:T(8,128)(2,1)}, bf16[256,2048]{1,0:T(8,128)(2,1)}, u32[]{:S(2)}, u32[]{:S(2)}) collective-permute-start(bf16[256,2048]{1,0:T(8,128)(2,1)} %copy-done.16), channel_id=1, source_target_pairs={{0,4},{14,10},{1,5},{15,11},{16,20},{30,26},{17,21},{31,27}} | collective-permute-start | bytes 3145736 | tf_op jit(solution)/shard_map/ppermute | solution.py:508
  152.4 2.2 copy-start.4
  156.8 14.9 %copy-start.5 = (f32[512,2048]{1,0:T(8,128)S(1)}, f32[512,2048]{1,0:T(8,128)}, u32[]{:S(2)}) copy-start(f32[512,2048]{1,0:T(8,128)} %copy-done.3) | copy-start | bytes 12582916
  165.6 9.3 %copy-start = (f32[512,2048]{1,0:T(8,128)}, f32[512,2048]{1,0:T(8,128)S(1)}, u32[]{:S(2)}) copy-start(f32[512,2048]{1,0:T(8,128)S(1)} %get-tuple-element.51.refs_2_.refs_1_) | copy-start | bytes 12582916
  165.6 23.4 %copy-start.14 = (f32[512,2048]{1,0:T(8,128)S(1)}, f32[512,2048]{1,0:T(8,128)}, u32[]{:S(2)}) copy-start(f32[512,2048]{1,0:T(8,128)} %copy-done.12) | copy-start | bytes 12582916
  168.9 20.1 %copy-start.8 = (f32[512,2048]{1,0:T(8,128)S(1)}, f32[512,2048]{1,0:T(8,128)}, u32[]{:S(2)}) copy-start(f32[512,2048]{1,0:T(8,128)} %copy-done.7) | copy-start | bytes 12582916
  168.9 43.3 %collective-permute-start.12 = (bf16[256,2048]{1,0:T(8,128)(2,1)}, bf16[256,2048]{1,0:T(8,128)(2,1)S(1)}, u32[]{:S(2)}, u32[]{:S(2)}) collective-permute-start(bf16[256,2048]{1,0:T(8,128)(2,1)} %broadcast_select_fusion), channel_id=1, source_target_pairs={{0,4},{12,8},{2,6},{14,10},{1,5},{13,9},{3,7},{15,11},{16,20},{28,... | collective-permute-start | bytes 3145736 | tf_op jit(solution)/shard_map/ppermute | solution.py:508
  170.4 41.7 %collective-permute-start.11 = (bf16[256,2048]{1,0:T(8,128)(2,1)}, bf16[256,2048]{1,0:T(8,128)(2,1)}, u32[]{:S(2)}, u32[]{:S(2)}) collective-permute-start(bf16[256,2048]{1,0:T(8,128)(2,1)} %shard_map.269), channel_id=1, source_target_pairs={{4,8},{10,6},{5,9},{11,7},{20,24},{26,22},{21,25},{27,23}} | collective-permute-start | bytes 3145736 | tf_op jit(solution)/shard_map/ppermute | solution.py:508
  174.9 31.7 %copy-start.17 = (bf16[256,2048]{1,0:T(8,128)(2,1)S(1)}, bf16[256,2048]{1,0:T(8,128)(2,1)}, u32[]{:S(2)}) copy-start(bf16[256,2048]{1,0:T(8,128)(2,1)} %copy-done.16) | copy-start | bytes 3145732
  194.2 53.0 %collective-permute-start.15 = (bf16[528,2048]{1,0:T(8,128)(2,1)}, bf16[528,2048]{1,0:T(8,128)(2,1)}, u32[]{:S(2)}, u32[]{:S(2)}) collective-permute-start(bf16[528,2048]{1,0:T(8,128)(2,1)} %shard_map.273), channel_id=1, source_target_pairs={{4,0},{10,14},{8,4},{6,10},{5,1},{11,15},{9,5},{7,11},{20,16},{26,... | collective-permute-start | bytes 6488072 | tf_op jit(solution)/shard_map/ppermute | solution.py:508
  207.7 28.3 %collective-permute-start.13 = (bf16[256,2048]{1,0:T(8,128)(2,1)}, bf16[256,2048]{1,0:T(8,128)(2,1)}, u32[]{:S(2)}, u32[]{:S(2)}) collective-permute-start(bf16[256,2048]{1,0:T(8,128)(2,1)} %shard_map.272), channel_id=1, source_target_pairs={{4,8},{10,6},{5,9},{11,7},{20,24},{26,22},{21,25},{27,23}} | collective-permute-start | bytes 3145736 | tf_op jit(solution)/shard_map/ppermute | solution.py:508
  209.0 27.0 %collective-permute-start.14 = (bf16[256,2048]{1,0:T(8,128)(2,1)}, bf16[256,2048]{1,0:T(8,128)(2,1)}, u32[]{:S(2)}, u32[]{:S(2)}) collective-permute-start(bf16[256,2048]{1,0:T(8,128)(2,1)} %broadcast_select_fusion.1), channel_id=1, source_target_pairs={{0,4},{12,8},{2,6},{14,10},{1,5},{13,9},{3,7},{15,11},{16,20},{28,... | collective-permute-start | bytes 3145736 | tf_op jit(solution)/shard_map/ppermute | solution.py:508
  212.2 2.2 copy-start.1
  214.3 2.2 copy-start.6
  220.6 21.6 %copy-start.25 = (s32[8]{0:T(128)S(1)}, s32[8]{0:T(128)}, u32[]{:S(2)}) copy-start(s32[8]{0:T(128)} %constant.82.clone) | copy-start | bytes 100
  220.6 22.2 %copy-start.24 = (s32[8]{0:T(128)S(1)}, s32[8]{0:T(128)}, u32[]{:S(2)}) copy-start(s32[8]{0:T(128)} %constant.81.clone) | copy-start | bytes 100
  220.6 37.9 %collective-permute-start.16 = (bf16[256,2048]{1,0:T(8,128)(2,1)}, bf16[256,2048]{1,0:T(8,128)(2,1)}, u32[]{:S(2)}, u32[]{:S(2)}) collective-permute-start(bf16[256,2048]{1,0:T(8,128)(2,1)} %shard_map.274), channel_id=1, source_target_pairs={{8,12},{6,2},{4,8},{10,6},{9,13},{7,3},{5,9},{11,7},{24,28},{22,18... | collective-permute-start | bytes 3145736 | tf_op jit(solution)/shard_map/ppermute | solution.py:508
  240.2 36.8 %collective-permute-start.17 = (bf16[256,2048]{1,0:T(8,128)(2,1)}, bf16[256,2048]{1,0:T(8,128)(2,1)}, u32[]{:S(2)}, u32[]{:S(2)}) collective-permute-start(bf16[256,2048]{1,0:T(8,128)(2,1)} %shard_map.275), channel_id=1, source_target_pairs={{8,12},{6,2},{4,8},{10,6},{9,13},{7,3},{5,9},{11,7},{24,28},{22,18... | collective-permute-start | bytes 3145736 | tf_op jit(solution)/shard_map/ppermute | solution.py:508
  247.2 2.2 copy-start.9
  249.4 9.1 %copy-start.2 = (f32[512,2048]{1,0:T(8,128)S(1)}, f32[512,2048]{1,0:T(8,128)}, u32[]{:S(2)}) copy-start(f32[512,2048]{1,0:T(8,128)} %copy-done) | copy-start | bytes 12582916
  (1 other events, 1.8 us)

commit v5 on v4

--- a/solution.py
+++ b/solution.py
@@ -8,9 +8,9 @@
 from jax.sharding import PartitionSpec as P
 
 GROUP = 4
-VMEM_LIMIT = 36 * 1024 * 1024
-SMALL_VMEM_LIMIT = 20 * 1024 * 1024
+VMEM_LIMIT = 58 * 1024 * 1024
 COST = 1024
+FORWARD_COST = 4 * 10**9
 EXTRA = 16
 
 
@@ -106,7 +106,7 @@
     functions, blocks, slots, side, _ = three_index.shape
     width = coeff_parts[0].shape[1]
     parts = len(coeff_parts)
-    together = next(t for t in (2, 1) if blocks % t == 0)
+    together = next(t for t in (4, 2, 1) if blocks % t == 0)
     sums = pl.BlockSpec((together, functions * side, width), lambda m, *_: (m, 0, 0))
     last = early is not None
     return pl.pallas_call(
@@ -137,7 +137,7 @@
         refs[-1][t] = ref[0]
 
 
-def collect(index, views):
+def collect(index, at, views):
     parts = len(views)
     height, depth = views[0].shape[1:]
     tall = height // 2 if height % 256 == 0 else height
@@ -146,13 +146,13 @@
         grid_spec=pltpu.PrefetchScalarGridSpec(
             num_scalar_prefetch=1,
             grid=(height // tall,),
-            in_specs=[pl.BlockSpec((1, tall, depth), lambda r, index: (index[0], r, 0))] * parts,
+            in_specs=[pl.BlockSpec((1, tall, depth), lambda r, index: (index[at], r, 0))] * parts,
             out_specs=pl.BlockSpec((parts, tall, depth), lambda r, index: (0, r, 0)),
         ),
         out_shape=jax.ShapeDtypeStruct((parts, height, depth), views[0].dtype),
-        compiler_params=pltpu.CompilerParams(vmem_limit_bytes=SMALL_VMEM_LIMIT),
+        compiler_params=pltpu.CompilerParams(vmem_limit_bytes=VMEM_LIMIT),
         cost_estimate=pl.CostEstimate(flops=COST, bytes_accessed=COST, transcendentals=0),
-    )(index[None], *views)
+    )(index, *views)
 
 
 def store_rounded(out_ref, total, first_diagonal, carried):
@@ -171,30 +171,30 @@
     out_ref[rows:] = jnp.where(extra == 0, lost, 0.0).astype(out_ref.dtype)
 
 
-def forward_kernel(flags, *refs, choices, first):
+def forward_kernel(flags, *refs, at, choices, first):
     out_ref = refs[-1]
     for i in range(choices):
         sums_ref, came_ref = refs[2 * i], refs[2 * i + 1]
 
-        @pl.when(flags[i] > 0)
+        @pl.when(flags[at + i] > 0)
         def _(sums_ref=sums_ref, came_ref=came_ref):
             rows = sums_ref.shape[0]
             total = sums_ref[...] + came_ref[:rows].astype(jnp.float32)
             carried = came_ref[rows : rows + 1].astype(jnp.float32) if came_ref.shape[0] > rows else None
-            store_rounded(out_ref, total, flags[choices] + first, carried)
-
-
-def forward(flags, sums, came, piece, c):
+            store_rounded(out_ref, total, flags[at + choices] + first, carried)
+
+
+def forward(flags, at, sums, came, piece, c, cost):
     choices, length = len(sums), sums[0].shape[1]
-    tile = min(length, 512)
+    tile = min(length, 1024)
     sent = came[0].shape[0]
     in_specs, operands = [], []
     for i in range(choices):
-        in_specs.append(pl.BlockSpec((piece, tile), lambda j, flags, i=i: (c, j * flags[i])))
-        in_specs.append(pl.BlockSpec((sent, tile), lambda j, flags, i=i: (0, j * flags[i])))
+        in_specs.append(pl.BlockSpec((piece, tile), lambda j, flags, i=i: (c, j * flags[at + i])))
+        in_specs.append(pl.BlockSpec((sent, tile), lambda j, flags, i=i: (0, j * flags[at + i])))
         operands += [sums[i], came[i]]
     return pl.pallas_call(
-        functools.partial(forward_kernel, choices=choices, first=c * piece),
+        functools.partial(forward_kernel, at=at, choices=choices, first=c * piece),
         grid_spec=pltpu.PrefetchScalarGridSpec(
             num_scalar_prefetch=1,
             grid=(length // tile,),
@@ -202,59 +202,56 @@
             out_specs=pl.BlockSpec((sent, tile), lambda j, flags: (0, j)),
         ),
         out_shape=jax.ShapeDtypeStruct(came[0].shape, came[0].dtype),
-        compiler_params=pltpu.CompilerParams(vmem_limit_bytes=SMALL_VMEM_LIMIT),
-        cost_estimate=pl.CostEstimate(flops=COST, bytes_accessed=COST, transcendentals=0),
+        compiler_params=pltpu.CompilerParams(vmem_limit_bytes=VMEM_LIMIT),
+        cost_estimate=pl.CostEstimate(flops=cost, bytes_accessed=COST, transcendentals=0),
     )(flags, *operands)
 
 
-def fold_kernel(flags, *refs, extra, first):
+def fold_kernel(flags, *refs, at, extra, first):
     before_ref, sums_ref, came_refs, out_ref = refs[0], refs[1], refs[2:-1], refs[-1]
     rows, tile = out_ref.shape
-    out_ref[...] = jnp.zeros_like(out_ref) if first else before_ref[...]
-
-    @pl.when(flags[0] > 0)
-    def _():
-        out_ref[...] += sums_ref[...]
-
+    total = jnp.where(flags[at] > 0, sums_ref[...], 0.0)
+    if not first:
+        total = total + before_ref[...]
+    lost = jnp.zeros((1, tile), jnp.float32)
     for i, ref in enumerate(came_refs):
-
-        @pl.when(flags[i + 1] > 0)
-        def _(ref=ref):
-            term = ref[:rows].astype(jnp.float32)
-            if extra:
-                row = lax.broadcasted_iota(jnp.int32, (rows, tile), 0) + flags[len(came_refs) + 1]
-                col = lax.broadcasted_iota(jnp.int32, (rows, tile), 1) + pl.program_id(0) * tile
-                term = term + jnp.where(row == col, ref[rows : rows + 1].astype(jnp.float32), 0.0)
-            out_ref[...] += term
-
-
-def fold(flags, before, sums, came, rows, at, extra, first):
+        total = total + jnp.where(flags[at + i + 1] > 0, ref[:rows].astype(jnp.float32), 0.0)
+        if extra:
+            lost = lost + jnp.where(flags[at + i + 1] > 0, ref[rows : rows + 1].astype(jnp.float32), 0.0)
+    if extra:
+        row = lax.broadcasted_iota(jnp.int32, (rows, tile), 0) + flags[at + len(came_refs) + 1]
+        col = lax.broadcasted_iota(jnp.int32, (rows, tile), 1) + pl.program_id(0) * tile
+        total = total + jnp.where(row == col, lost, 0.0)
+    out_ref[...] = total
+
+
+def fold(flags, at, before, sums, came, rows, piece, extra, first):
     height, length = before.shape
-    tile = min(length, 512)
-    in_place = pl.BlockSpec((rows, tile), lambda j, flags: (at, j))
+    tile = min(length, 1024)
+    in_place = pl.BlockSpec((rows, tile), lambda j, flags: (piece, j))
     return pl.pallas_call(
-        functools.partial(fold_kernel, extra=extra, first=first),
+        functools.partial(fold_kernel, at=at, extra=extra, first=first),
         grid_spec=pltpu.PrefetchScalarGridSpec(
             num_scalar_prefetch=1,
             grid=(length // tile,),
             in_specs=[
-                pl.BlockSpec((rows, tile), lambda j, flags: (at, 0)) if first else in_place,
-                pl.BlockSpec((rows, tile), lambda j, flags: (at, j * flags[0])),
+                pl.BlockSpec((rows, tile), lambda j, flags: (piece, 0)) if first else in_place,
+                pl.BlockSpec((rows, tile), lambda j, flags: (piece, j * flags[at])),
             ]
             + [
-                pl.BlockSpec((message.shape[0], tile), lambda j, flags, i=i: (0, j * flags[i + 1]))
+                pl.BlockSpec((message.shape[0], tile), lambda j, flags, i=i: (0, j * flags[at + i + 1]))
                 for i, message in enumerate(came)
             ],
             out_specs=in_place,
         ),
         out_shape=jax.ShapeDtypeStruct(before.shape, before.dtype),
         input_output_aliases={} if first else {1: 0},
-        compiler_params=pltpu.CompilerParams(vmem_limit_bytes=SMALL_VMEM_LIMIT),
+        compiler_params=pltpu.CompilerParams(vmem_limit_bytes=VMEM_LIMIT),
         cost_estimate=pl.CostEstimate(flops=COST, bytes_accessed=COST, transcendentals=0),
     )(flags, before, sums, *came)
 
 
-def product_kernel(index, *refs, parts, extra):
+def product_kernel(index, *refs, at, parts, extra):
     out_ref, piece_refs = refs[2 * parts], refs[2 * parts + 1 :]
     total = None
     for rows_ref, cols_ref in zip(refs[:parts], refs[parts : 2 * parts]):
@@ -265,22 +262,22 @@
     out_ref[...] = total
     for c, ref in enumerate(piece_refs):
         rows = ref.shape[0] - extra
-        store_rounded(ref, total[c * rows : (c + 1) * rows], index[0] * total.shape[0] + c * rows, None)
-
-
-def row_product(index, rows, cols, pieces, extra, cost):
+        store_rounded(ref, total[c * rows : (c + 1) * rows], index[at] * total.shape[0] + c * rows, None)
+
+
+def row_product(index, at, rows, cols, pieces, extra, cost):
     parts = len(rows)
     height, depth = rows[0].shape[1:]
     length = cols[0].shape[0]
     tile = min(length, 512)
     taller = height // max(pieces, 1) + extra
     return pl.pallas_call(
-        functools.partial(product_kernel, parts=parts, extra=extra),
+        functools.partial(product_kernel, at=at, parts=parts, extra=extra),
         grid_spec=pltpu.PrefetchScalarGridSpec(
             num_scalar_prefetch=1,
             grid=(length // tile,),
             in_specs=[
-                pl.BlockSpec((1, height, depth), lambda c, index, t=t: (index[t], 0, 0)) for t in range(parts)
+                pl.BlockSpec((1, height, depth), lambda c, index, t=t: (index[at + t], 0, 0)) for t in range(parts)
             ]
             + [pl.BlockSpec((tile, depth), lambda c, index: (c, 0))] * parts,
             out_specs=[pl.BlockSpec((height, tile), lambda c, index: (0, c))]
@@ -288,7 +285,7 @@
         ),
         out_shape=[jax.ShapeDtypeStruct((height, length), jnp.float32)]
         + [jax.ShapeDtypeStruct((taller, length), jnp.bfloat16)] * pieces,
-        compiler_params=pltpu.CompilerParams(vmem_limit_bytes=SMALL_VMEM_LIMIT),
+        compiler_params=pltpu.CompilerParams(vmem_limit_bytes=VMEM_LIMIT),
         cost_estimate=pl.CostEstimate(flops=cost, bytes_accessed=COST, transcendentals=0),
     )(index, *rows, *cols)
 
@@ -339,7 +336,7 @@
                 if not 0 <= step < self.aux - 1 or not self.hop(phase, rank, step)[0]:
                     continue
                 pairs = self.hop(phase, rank, step)[0]
-                for group in open_groups if step >= 1 and due >= 2 else []:
+                for group in open_groups if step >= 1 and due >= 2 and phase == 0 else []:
                     others = [p for r, st in group for p in self.hop(phase, r, st)[0]]
                     if not {p[0] for p in pairs} & {p[0] for p in others} and not {p[1] for p in pairs} & {
                         p[1] for p in others
@@ -431,15 +428,17 @@
         cols.append(lax.ppermute(own, "sub", [((u + t) % sub, u) for u in range(sub)]))
     views = [c.reshape(owned * sub, height, depth) for c in cols]
 
-    def rows_to_send(k, q, earlier):
-        table = [line.order(k, (b - k) % orb, a)[q] % owned for a in range(aux) for b in range(orb)]
-        message = collect(after(lookup(table, place) * sub + s, earlier), views)
-        return message, lax.ppermute(message, "orb", [((b + k) % orb, b) for b in range(orb)])
-
-    own_blocks = [
-        lookup([line.order(0, b, a)[q] % owned for a in range(aux) for b in range(orb)], place) * sub + s
-        for q in range(owned)
-    ]
+    places = [(a, b, c) for a in range(aux) for b in range(orb) for c in range(sub)]
+    table = [[] for _ in places]
+
+    def scalars(rows):
+        at = len(table[0])
+        for line_, row in zip(table, rows):
+            line_.extend(int(value) for value in row)
+        return at
+
+    def own_block(a, b, c, q):
+        return line.order(0, b, a)[q] % owned * sub + c
 
     events, finals = [], []
     for k in range(orb):
@@ -456,6 +455,8 @@
                 when = max(base + rank * halves + (c + st) * wide for rank, st in group)
                 if step == 0 and c == 0:
                     when = ready[group[0][0]] + 0.1
+                if not k and len(group) > 1:
+                    when += 0.5
                 events.append((when, step, "hop", k, tuple(group), c))
             if any(line.hop(k, *member)[2] for member in group):
                 finals.append((k, tuple(group)))
@@ -465,62 +466,83 @@
             events.append((end + 1 + k, c, "fold", k, c, 0))
     events.sort(key=lambda e: e[:2])
 
-    came_rows, sums, heads, came, result, last = {}, {}, {}, {}, None, None
+    plans = []
     for _, _, kind, k, what, c in events:
-        extra = 0 if k else EXTRA
         piece = height // pieces(k)
+        plan = dict(kind=kind, k=k, what=what, c=c)
         if kind == "rows":
-            last, came_rows[k, what] = rows_to_send(k, what, last)
+            rows = [[line.order(k, (b - k) % orb, a)[what] % owned * sub + d] for a, b, d in places]
         elif kind == "product":
-            q = what
-            if k == 0:
-                index = jnp.broadcast_to(own_blocks[q], (sub,))
-                rows = views
-            else:
-                index = jnp.arange(sub, dtype=jnp.int32)
-                rows = [came_rows[k, q]] * sub
-            flops = 2 * sub * height * length * depth
-            sums[k, q], *heads[k, q] = row_product(after(index, last), rows, cols, pieces(k), extra, flops if k else COST)
-            last = sums[k, q]
+            rows = [[t if k else own_block(a, b, d, what) for t in range(sub)] for a, b, d in places]
         elif kind == "hop":
-            pairs, choices = [], []
+            pairs, choices, tables = [], [], []
             for rank, step in what:
                 more, position, _ = line.hop(k, rank, step)
                 pairs += more
                 for q in sorted(set(position.values())):
-                    choices.append((rank, step, q, [position.get(i) == q for i in range(aux * orb)]))
-            if step == 0:
+                    choices.append((rank, step, q))
+                    tables.append([position.get(a * orb + b) == q for a, b, _ in places])
+            plan.update(pairs=pairs, choices=choices)
+            rows = []
+            for i, (a, b, d) in enumerate(places):
+                chosen = [t[i] for t in tables]
+                start = sum(own_block(a, b, d, q) for (_, _, q), flag in zip(choices, chosen) if flag)
+                rows.append(chosen + [start * height])
+        else:
+            groups = [group for k_, group in finals if k_ == k]
+            ends = [{i for member in group for i in line.hop(k, *member)[2]} for group in groups]
+            plan.update(groups=groups)
+            rows = [
+                [a in line.targets(k, b)]
+                + [a * orb + b in end_ for end_ in ends]
+                + [(a % owned * sub + d) * height + what * piece]
+                for a, b, d in places
+            ]
+        plan.update(at=scalars(rows), piece=piece)
+        plans.append(plan)
+    everywhere = lookup(table, place * sub + s)
+
+    came_rows, sums, heads, came, result, last = {}, {}, {}, {}, None, None
+    for plan in plans:
+        k, what, c, at, piece = (plan[name] for name in ("k", "what", "c", "at", "piece"))
+        extra = 0 if k else EXTRA
+        if plan["kind"] == "rows":
+            last = collect(after(everywhere, last), at, views)
+            pairs = [((b + k) % orb, b) for b in range(orb)]
+            came_rows[k, what] = lax.ppermute(last, "orb", pairs)
+        elif plan["kind"] == "product":
+            rows = [came_rows[k, what]] * sub if k else views
+            flops = 2 * sub * height * length * depth if k and what == 0 else COST
+            sums[k, what], *heads[k, what] = row_product(
+                after(everywhere, last), at, rows, cols, pieces(k), extra, flops
+            )
+            last = sums[k, what]
+        elif plan["kind"] == "hop":
+            choices = plan["choices"]
+            if choices[0][1] == 0:
                 value = heads[k, choices[0][2]][c]
-                for _, _, q, table in choices[1:]:
-                    value = jnp.where(lookup(table, place) > 0, heads[k, q][c], value)
+                for i, (_, _, q) in enumerate(choices[1:]):
+                    value = jnp.where(everywhere[at + 1 + i] > 0, heads[k, q][c], value)
                 value = after(value, last) if c or len(choices) > 1 else value
             else:
-                flags = [lookup(table, place) for _, _, _, table in choices]
-                start = sum(flag * own_blocks[q] for flag, (_, _, q, _) in zip(flags, choices)) * height
                 value = forward(
-                    after(jnp.stack(flags + [start]), last),
-                    [sums[k, q] for _, _, q, _ in choices],
-                    [came[k, rank, step - 1, c] for rank, step, _, _ in choices],
+                    after(everywhere, last),
+                    at,
+                    [sums[k, q] for _, _, q in choices],
+                    [came[k, rank, step - 1, c] for rank, step, _ in choices],
                     piece,
                     c,
+                    FORWARD_COST if k and c == 0 and choices[0][:2] == (0, 1) else COST,
                 )
             last = value
-            arrived = lax.ppermute(value, ("aux", "orb"), pairs)
-            for rank, step in what:
-                came[k, rank, step, c] = arrived
+            arrived = lax.ppermute(value, ("aux", "orb"), plan["pairs"])
+            for member in what:
+                came[(k,) + member + (c,)] = arrived
         else:
-            flags = [[z_ in line.targets(k, o_) for z_ in range(aux) for o_ in range(orb)]]
-            parts = []
-            for k_, group in finals:
-                if k_ == k:
-                    places = {i for member in group for i in line.hop(k, *member)[2]}
-                    flags.append([i in places for i in range(aux * orb)])
-                    parts.append(came[(k,) + group[0] + (what,)])
-            flags = [lookup(table, place) for table in flags]
-            flags = jnp.stack(flags + [(lax.rem(z, owned) * sub + s) * height + what * piece])
+            messages = [came[(k,) + group[0] + (what,)] for group in plan["groups"]]
             mine = sums[k, owned - 1]
             before = mine if result is None else result
-            result = fold(after(flags, last), before, mine, parts, piece, what, extra, result is None)
+            result = fold(after(everywhere, last), at, before, mine, messages, piece, what, extra, result is None)
             last = result
     return result
 

time: 285 us -> 267 us (0.937)
  Pallas kernels: 99.8 us -> 130 us
  starting transfers between devices: 48.1 us -> 31.3 us
  local copies, waits for them, and re-layouts: 28.2 us -> 16.5 us
  other arithmetic: 15.8 us -> 5.34 us
  waiting for transfers between devices: 85.4 us -> 80.7 us
  between operations: 4.68 us -> 1.61 us
    pallas_call x2, Pallas kernels: 19.6 us -> 35.3 us  [transform(): pl.pallas_call(functools.partial(transform_kernel, parts=parts, last=last...]
    ppermute x14 -> x16, starting transfers between devices: 43.3 us -> 29 us  [the longest x14 27 us: shards(): arrived = lax.ppermute(value, ('aux', 'orb'), plan['pairs'])]
    pallas_call x13 -> x15, Pallas kernels: 74.1 us -> 88.2 us  [the longest x4 41.7 us: row_product(): pl.pallas_call(functools.partial(product_kernel, at=at, parts=parts, extr...]
    unnamed x62 -> x36, local copies, waits for them, and re-layouts: 19.5 us -> 10.9 us
    another operation x7 -> x0, other arithmetic: 7.76 us -> none  [the longest x4 3.94 us: shards(): jnp.stack(flags + [start])]
    ppermute x14 -> x16, waiting for transfers between devices: 65.1 us -> 59.3 us  [the longest x2 34 us: shards(): came_rows[k, what] = lax.ppermute(last, 'orb', pairs)]
    dynamic_slice x7 -> x1, local copies, waits for them, and re-layouts: 4.23 us -> 1.2 us  [lookup(): return jnp.asarray(table, jnp.int32)[place]]
  transfers between devices with their start and end apart: 18 -> 20, of which waited for: 10 -> 9; matrix products, arithmetic and copies ran while one was open for 8% -> 4% of each run, Pallas kernels for 29% -> 39%
where the time goes in v5:
time: 267 us; the launch traced here: 266 us
  Pallas kernels  130 us (49%)
  waiting for transfers between devices  80.7 us (30%)
  starting transfers between devices  31.3 us (12%)
  local copies, waits for them, and re-layouts  16.5 us (6%)
  other arithmetic  5.34 us (2%)
    pallas_call x4, Pallas kernels, row_product(): pl.pallas_call(functools.partial(product_kernel, at=at, parts=parts, extr...  41.7 us
    pallas_call x2, Pallas kernels, transform(): pl.pallas_call(functools.partial(transform_kernel, parts=parts, last=last...  35.3 us
    ppermute x2, waiting for transfers between devices, shards(): came_rows[k, what] = lax.ppermute(last, 'orb', pairs)  34 us
    pallas_call x8, Pallas kernels, forward(): pl.pallas_call(functools.partial(forward_kernel, at=at, choices=choices,...  30.3 us
    ppermute x14, starting transfers between devices, shards(): arrived = lax.ppermute(value, ('aux', 'orb'), plan['pairs'])  27 us
    ppermute x14, waiting for transfers between devices, shards(): arrived = lax.ppermute(value, ('aux', 'orb'), plan['pairs'])  25.3 us
    pallas_call x3, Pallas kernels, fold(): pl.pallas_call(functools.partial(fold_kernel, at=at, extra=extra, first=f...  16.2 us
    unnamed x36, local copies, waits for them, and re-layouts  10.9 us
  transfers between devices with their start and end apart: 20, of which 9 were waited for; matrix products, arithmetic and copies ran while one was open for 4% of the time, Pallas kernels for 39%

profile of v5, /device:TPU:20, one launch (start us, length us, event | category | flops | bytes accessed | tf_op | source)
XLA Modules:
  0.0 265.6 jit_solution(5448949394782932153)
XLA Ops:
  1.2 1.6 collective-permute-start
  2.7 1.2 slice.12
  6.0 1.2 select_reduce_fusion
  7.2 16.8 %shard_map.55.refs_3_ = f32[16,256,512]{2,1,0:T(8,128)} custom-call(s32[16,16]{1,0:T(8,128)} %get-tuple-element.66.order, s32[16,16]{1,0:T(8,128)} %get-tuple-element.65.columns, s32[16,2]{1,0:T(8,128)} %stack.16.bounds, bf16[2,16,16,128,128]{4,3,2,1,0:T(8,128)(2,1)} %x_ref.3, bf16[2048,512]{1,0:T(8,128)(2,1)} %refs_0_.1), custom_call_target="tpu_custom_call" | custom-call | flops 1024 | bytes 1024 | tf_op jit(solution)/shard_map/pallas_call | solution.py:112
  24.8 9.8 %collective-permute-done.1.refs_1_ = bf16[768,512]{1,0:T(8,128)(2,1)S(1)} collective-permute-done((bf16[768,512]{1,0:T(8,128)(2,1)S(1)}, bf16[768,512]{1,0:T(8,128)(2,1)S(1)}, u32[]{:S(2)}, u32[]{:S(2)}) %collective-permute-start.1) | collective-permute-done | bytes 786464 | tf_op jit(solution)/shard_map/ppermute | solution.py:380
  34.6 5.4 %collective-permute-done.2.refs_2_ = bf16[640,512]{1,0:T(8,128)(2,1)S(1)} collective-permute-done((bf16[640,512]{1,0:T(8,128)(2,1)S(1)}, bf16[640,512]{1,0:T(8,128)(2,1)S(1)}, u32[]{:S(2)}, u32[]{:S(2)}) %collective-permute-start.2) | collective-permute-done | bytes 655392 | tf_op jit(solution)/shard_map/ppermute | solution.py:410
  40.8 18.5 %shard_map.56.refs_2_ = bf16[2048,1024]{1,0:T(8,128)(2,1)} custom-call(s32[16,16]{1,0:T(8,128)} %get-tuple-element.66.order, s32[16,16]{1,0:T(8,128)} %get-tuple-element.65.columns, s32[16,2]{1,0:T(8,128)} %copy.14.bounds, bf16[2,16,16,128,128]{4,3,2,1,0:T(8,128)(2,1)} %x_ref.3, bf16[640,512]{1,0:T(8,128)(2,1)} %copy-done.13, bf16[768,512]{1,0:T(8,128)(2,1)} %copy-done.12, ...), custom_call_target="tpu_custom_call" | custom-call | flops 1024 | bytes 1024 | tf_op jit(solution)/shard_map/pallas_call | solution.py:112
  59.5 1.2 constant_dynamic-slice_fusion.1
  60.7 6.3 %collective-permute-done.3.refs_3_ = bf16[2048,1024]{1,0:T(8,128)(2,1)} collective-permute-done((bf16[2048,1024]{1,0:T(8,128)(2,1)}, bf16[2048,1024]{1,0:T(8,128)(2,1)}, u32[]{:S(2)}, u32[]{:S(2)}) %collective-permute-start.3) | collective-permute-done | bytes 4194336 | tf_op jit(solution)/shard_map/ppermute | solution.py:428
  67.0 3.3 %shard_map.57 = bf16[2,512,1024]{2,1,0:T(8,128)(2,1)} custom-call(s32[55]{0:T(128)} %get-tuple-element.64.index.flags, bf16[4,512,1024]{2,1,0:T(8,128)(2,1)} %bitcast.16, bf16[4,512,1024]{2,1,0:T(8,128)(2,1)} %bitcast.7.refs_1_), custom_call_target="tpu_custom_call" | custom-call | flops 1024 | bytes 1024 | tf_op jit(solution)/shard_map/pallas_call | solution.py:144
  71.3 11.0 %shard_map.58 = (f32[512,2048]{1,0:T(8,128)}, bf16[528,2048]{1,0:T(8,128)(2,1)}) custom-call(s32[55]{0:T(128)} %get-tuple-element.64.index.flags, bf16[4,512,1024]{2,1,0:T(8,128)(2,1)} %bitcast.17, bf16[4,512,1024]{2,1,0:T(8,128)(2,1)} %bitcast.7.refs_1_, bf16[2048,1024]{1,0:T(8,128)(2,1)} %shard_map.56.refs_2_, ...), custom_call_target="tpu_custom_call" | custom-call | flops 1024 | bytes 1024 | tf_op jit(solution)/shard_map/pallas_call | solution.py:274
  82.2 1.3 collective-permute-start.5
  83.5 10.4 %shard_map.59 = (f32[512,2048]{1,0:T(8,128)}, bf16[528,2048]{1,0:T(8,128)(2,1)}) custom-call(s32[55]{0:T(128)} %get-tuple-element.64.index.flags, bf16[4,512,1024]{2,1,0:T(8,128)(2,1)} %bitcast.18, bf16[4,512,1024]{2,1,0:T(8,128)(2,1)} %bitcast.7.refs_1_, bf16[2048,1024]{1,0:T(8,128)(2,1)} %shard_map.56.refs_2_, ...), custom_call_target="tpu_custom_call" | custom-call | flops 1024 | bytes 1024 | tf_op jit(solution)/shard_map/pallas_call | solution.py:274
  93.9 3.3 %shard_map.63 = bf16[2,512,1024]{2,1,0:T(8,128)(2,1)} custom-call(s32[55]{0:T(128)} %get-tuple-element.64.index.flags, bf16[4,512,1024]{2,1,0:T(8,128)(2,1)} %bitcast.19, bf16[4,512,1024]{2,1,0:T(8,128)(2,1)} %bitcast.7.refs_1_), custom_call_target="tpu_custom_call" | custom-call | flops 1024 | bytes 1024 | tf_op jit(solution)/shard_map/pallas_call | solution.py:144
  98.3 20.8 %collective-permute-done.4.refs_0_.refs_1_ = bf16[2,512,1024]{2,1,0:T(8,128)(2,1)} collective-permute-done((bf16[2,512,1024]{2,1,0:T(8,128)(2,1)}, bf16[2,512,1024]{2,1,0:T(8,128)(2,1)}, u32[]{:S(2)}, u32[]{:S(2)}) %collective-permute-start.4) | collective-permute-done | bytes 2097184 | tf_op jit(solution)/shard_map/ppermute | solution.py:512
  119.0 10.2 %shard_map.60 = (f32[512,2048]{1,0:T(8,128)}, bf16[256,2048]{1,0:T(8,128)(2,1)}, bf16[256,2048]{1,0:T(8,128)(2,1)}) custom-call(s32[55]{0:T(128)} %get-tuple-element.64.index.flags, bf16[2,512,1024]{2,1,0:T(8,128)(2,1)} %collective-permute-done.4.refs_0_.refs_1_, bf16[2,512,1024]{2,1,0:T(8,128)(2,1)} %collective-permute-done.4.refs_0_.refs_1_, ...), custom_call_target="tpu_custom_call" | custom-call | flops 4294967296 | bytes 1024 | tf_op jit(solution)/shard_map/pallas_call | solution.py:274
  130.0 1.3 collective-permute-start.11
  131.3 1.4 collective-permute-done.5.refs_1_.refs_2_
  132.6 1.4 copy-done
  134.0 5.1 %shard_map.61 = bf16[528,2048]{1,0:T(8,128)(2,1)} custom-call(s32[55]{0:T(128)} %get-tuple-element.64.index.flags, f32[512,2048]{1,0:T(8,128)} %get-tuple-element.44.refs_0_, bf16[528,2048]{1,0:T(8,128)(2,1)} %copy-done), custom_call_target="tpu_custom_call" | custom-call | flops 1024 | bytes 1024 | tf_op jit(solution)/shard_map/pallas_call | solution.py:196
  139.1 2.7 %collective-permute-start.10 = (bf16[528,2048]{1,0:T(8,128)(2,1)}, bf16[528,2048]{1,0:T(8,128)(2,1)}, u32[]{:S(2)}, u32[]{:S(2)}) collective-permute-start(bf16[528,2048]{1,0:T(8,128)(2,1)} %shard_map.61), channel_id=1, source_target_pairs={{8,4},{6,10},{9,5},{7,11},{24,20},{22,26},{25,21},{23,27}} | collective-permute-start | bytes 6488072 | tf_op jit(solution)/shard_map/ppermute | solution.py:538
  143.6 3.1 %shard_map.62 = bf16[256,2048]{1,0:T(8,128)(2,1)} custom-call(s32[55]{0:T(128)} %get-tuple-element.64.index.flags, f32[512,2048]{1,0:T(8,128)} %get-tuple-element.47.refs_0_, bf16[256,2048]{1,0:T(8,128)(2,1)} %copy-done.17), custom_call_target="tpu_custom_call" | custom-call | flops 4000000000 | bytes 1024 | tf_op jit(solution)/shard_map/pallas_call | solution.py:196
  146.6 1.3 collective-permute-start.9
  149.9 13.2 %collective-permute-done.7.refs_0_.refs_1_ = bf16[2,512,1024]{2,1,0:T(8,128)(2,1)S(1)} collective-permute-done((bf16[2,512,1024]{2,1,0:T(8,128)(2,1)}, bf16[2,512,1024]{2,1,0:T(8,128)(2,1)S(1)}, u32[]{:S(2)}, u32[]{:S(2)}) %collective-permute-start.7) | collective-permute-done | bytes 2097184 | tf_op jit(solution)/shard_map/ppermute | solution.py:512
  163.1 1.3 copy-done.1
  164.4 10.2 %shard_map.64 = (f32[512,2048]{1,0:T(8,128)}, bf16[256,2048]{1,0:T(8,128)(2,1)}, bf16[256,2048]{1,0:T(8,128)(2,1)}) custom-call(s32[55]{0:T(128)} %get-tuple-element.64.index.flags, bf16[2,512,1024]{2,1,0:T(8,128)(2,1)} %copy-done.1, bf16[2,512,1024]{2,1,0:T(8,128)(2,1)} %copy-done.1, bf16[2048,1024]{1,0:T(8,128)(2,1)} %shard_map.56.refs_2_, ...), custom_call_target="tpu_custom_call" | custom-call | flops 1024 | bytes 1024 | tf_op jit(solution)/shard_map/pallas_call | solution.py:274
  175.7 1.3 collective-permute-start.12
  178.0 3.1 %shard_map.65 = bf16[256,2048]{1,0:T(8,128)(2,1)} custom-call(s32[55]{0:T(128)} %get-tuple-element.64.index.flags, f32[512,2048]{1,0:T(8,128)} %get-tuple-element.47.refs_0_, bf16[256,2048]{1,0:T(8,128)(2,1)} %copy-done.6), custom_call_target="tpu_custom_call" | custom-call | flops 1024 | bytes 1024 | tf_op jit(solution)/shard_map/pallas_call | solution.py:196
  181.0 1.3 collective-permute-start.13
  183.3 3.4 %shard_map.66 = bf16[256,2048]{1,0:T(8,128)(2,1)} custom-call(s32[55]{0:T(128)} %get-tuple-element.64.index.flags, f32[512,2048]{1,0:T(8,128)} %get-tuple-element.47.refs_0_, bf16[256,2048]{1,0:T(8,128)(2,1)} %copy-done.7), custom_call_target="tpu_custom_call" | custom-call | flops 1024 | bytes 1024 | tf_op jit(solution)/shard_map/pallas_call | solution.py:196
  186.7 6.1 %shard_map.67 = bf16[528,2048]{1,0:T(8,128)(2,1)} custom-call(s32[55]{0:T(128)} %get-tuple-element.64.index.flags, f32[512,2048]{1,0:T(8,128)} %get-tuple-element.44.refs_0_, bf16[528,2048]{1,0:T(8,128)(2,1)} %collective-permute-done.10.refs_1_, f32[512,2048]{1,0:T(8,128)} %get-tuple-element.49.refs_2_.refs_0_.refs_1_, ...), custom_call_target="tpu_custom_call" | custom-call | flops 1024 | bytes 1024 | tf_op jit(solution)/shard_map/pallas_call | solution.py:196
  192.8 5.7 %collective-permute-start.15 = (bf16[528,2048]{1,0:T(8,128)(2,1)}, bf16[528,2048]{1,0:T(8,128)(2,1)S(1)}, u32[]{:S(2)}, u32[]{:S(2)}) collective-permute-start(bf16[528,2048]{1,0:T(8,128)(2,1)} %shard_map.67), channel_id=1, source_target_pairs={{4,0},{10,14},{8,4},{6,10},{5,1},{11,15},{9,5},{7,11},{20,16},{26,... | collective-permute-start | bytes 6488072 | tf_op jit(solution)/shard_map/ppermute | solution.py:538
  198.5 2.3 broadcast_select_fusion.1
  200.8 1.3 collective-permute-start.14
  202.1 5.6 %collective-permute-start.16 = (bf16[256,2048]{1,0:T(8,128)(2,1)S(1)}, bf16[256,2048]{1,0:T(8,128)(2,1)}, u32[]{:S(2)}, u32[]{:S(2)}) collective-permute-start(bf16[256,2048]{1,0:T(8,128)(2,1)S(1)} %copy-done.5), channel_id=1, source_target_pairs={{8,12},{6,2},{9,13},{7,3},{24,28},{22,18},{25,29},{23,19}} | collective-permute-start | bytes 3145736 | tf_op jit(solution)/shard_map/ppermute | solution.py:538
  208.7 3.1 %shard_map.68 = bf16[256,2048]{1,0:T(8,128)(2,1)} custom-call(s32[55]{0:T(128)} %get-tuple-element.64.index.flags, f32[512,2048]{1,0:T(8,128)} %get-tuple-element.53.refs_0_.refs_1_, bf16[256,2048]{1,0:T(8,128)(2,1)} %copy-done.2), custom_call_target="tpu_custom_call" | custom-call | flops 1024 | bytes 1024 | tf_op jit(solution)/shard_map/pallas_call | solution.py:196
  211.8 1.3 collective-permute-start.17
  213.1 3.4 %shard_map.69 = bf16[256,2048]{1,0:T(8,128)(2,1)} custom-call(s32[55]{0:T(128)} %get-tuple-element.64.index.flags, f32[512,2048]{1,0:T(8,128)} %get-tuple-element.47.refs_0_, bf16[256,2048]{1,0:T(8,128)(2,1)} %collective-permute-done.13.refs_1_), custom_call_target="tpu_custom_call" | custom-call | flops 1024 | bytes 1024 | tf_op jit(solution)/shard_map/pallas_call | solution.py:196
  216.5 1.3 collective-permute-start.18
  217.9 9.0 %collective-permute-done.14.refs_1_.refs_2_ = bf16[256,2048]{1,0:T(8,128)(2,1)S(1)} collective-permute-done((bf16[256,2048]{1,0:T(8,128)(2,1)}, bf16[256,2048]{1,0:T(8,128)(2,1)S(1)}, u32[]{:S(2)}, u32[]{:S(2)}) %collective-permute-start.14) | collective-permute-done | bytes 1048608 | tf_op jit(solution)/shard_map/ppermute | solution.py:538
  227.8 3.0 %shard_map.70 = bf16[256,2048]{1,0:T(8,128)(2,1)} custom-call(s32[55]{0:T(128)} %get-tuple-element.64.index.flags, f32[512,2048]{1,0:T(8,128)} %get-tuple-element.53.refs_0_.refs_1_, bf16[256,2048]{1,0:T(8,128)(2,1)} %copy-done.3), custom_call_target="tpu_custom_call" | custom-call | flops 1024 | bytes 1024 | tf_op jit(solution)/shard_map/pallas_call | solution.py:196
  230.9 1.3 collective-permute-start.19
  232.1 11.9 %collective-permute-done.15.refs_3_ = bf16[528,2048]{1,0:T(8,128)(2,1)S(1)} collective-permute-done((bf16[528,2048]{1,0:T(8,128)(2,1)}, bf16[528,2048]{1,0:T(8,128)(2,1)S(1)}, u32[]{:S(2)}, u32[]{:S(2)}) %collective-permute-start.15) | collective-permute-done | bytes 2162720 | tf_op jit(solution)/shard_map/ppermute | solution.py:538
  244.1 1.4 copy-done.4
  245.5 6.3 %shard_map.71.refs_0_ = f32[512,2048]{1,0:T(8,128)} custom-call(s32[55]{0:T(128)} %get-tuple-element.64.index.flags, f32[512,2048]{1,0:T(8,128)} %get-tuple-element.49.refs_2_.refs_0_.refs_1_, f32[512,2048]{1,0:T(8,128)} %get-tuple-element.49.refs_2_.refs_0_.refs_1_, bf16[528,2048]{1,0:T(8,128)(2,1)} %copy-done, bf16[528,2048]{1,0:T(8,128)(2,1)} %copy-done.4), custom_call_target="tpu_custom_call" | custom-call | flops 1024 | bytes 1024 | tf_op jit(solution)/shard_map/pallas_call | solution.py:232
  251.8 4.9 %shard_map.72.refs_0_ = f32[512,2048]{1,0:T(8,128)} custom-call(s32[55]{0:T(128)} %get-tuple-element.64.index.flags, f32[512,2048]{1,0:T(8,128)} %shard_map.71.refs_0_, f32[512,2048]{1,0:T(8,128)} %get-tuple-element.53.refs_0_.refs_1_, bf16[256,2048]{1,0:T(8,128)(2,1)} %copy-done.2, ...), custom_call_target="tpu_custom_call", output_to_operand_aliasing={{}: (1, {})} | custom-call | flops 1024 | bytes 1024 | tf_op jit(solution)/shard_map/pallas_call | solution.py:232
  256.8 3.0 %collective-permute-done.19.refs_4_ = bf16[256,2048]{1,0:T(8,128)(2,1)S(1)} collective-permute-done((bf16[256,2048]{1,0:T(8,128)(2,1)}, bf16[256,2048]{1,0:T(8,128)(2,1)S(1)}, u32[]{:S(2)}, u32[]{:S(2)}) %collective-permute-start.19) | collective-permute-done | bytes 1048608 | tf_op jit(solution)/shard_map/ppermute | solution.py:538
  260.7 4.9 %shard_map.73 = f32[512,2048]{1,0:T(8,128)} custom-call(s32[55]{0:T(128)} %get-tuple-element.64.index.flags, f32[512,2048]{1,0:T(8,128)} %shard_map.72.refs_0_, f32[512,2048]{1,0:T(8,128)} %get-tuple-element.53.refs_0_.refs_1_, bf16[256,2048]{1,0:T(8,128)(2,1)} %copy-done.3, bf16[256,2048]{1,0:T(8,128)(2,1)} %copy-done.8, ...), custom_call_target="tpu_custom_call", output_to_operand_aliasing={{}: (1, {})} | custom-call | flops 1024 | bytes 1024 | tf_op jit(solution)/shard_map/pallas_call | solution.py:232
  (61 shorter events, 16.1 us)
Async XLA Ops:
  0.0 4.5 %copy-start.16 = (s32[1,16]{1,0:T(1,128)S(1)}, s32[1,16]{1,0:T(1,128)}, u32[]{:S(2)}) copy-start(s32[1,16]{1,0:T(1,128)} %param.7) | copy-start | bytes 196
  0.0 4.5 %copy-start.15 = (s32[1,16,16]{2,1,0:T(8,128)S(1)}, s32[1,16,16]{2,1,0:T(8,128)}, u32[]{:S(2)}) copy-start(s32[1,16,16]{2,1,0:T(8,128)} %param.6) | copy-start | bytes 3076
  1.2 22.8 %collective-permute-start = (bf16[640,512]{1,0:T(8,128)(2,1)S(1)}, bf16[640,512]{1,0:T(8,128)(2,1)S(1)}, u32[]{:S(2)}, u32[]{:S(2)}) collective-permute-start(bf16[640,512]{1,0:T(8,128)(2,1)S(1)} %constant_dynamic-slice_fusion), channel_id=1, source_target_pairs={{2,0},{0,2},{3,1},{1,3},{6,4},{4,6},{7,5},{5,7},{10,8},{8,10},{11,... | collective-permute-start | bytes 1966088 | tf_op jit(solution)/shard_map/ppermute | solution.py:379
  3.9 30.6 %collective-permute-start.1 = (bf16[768,512]{1,0:T(8,128)(2,1)S(1)}, bf16[768,512]{1,0:T(8,128)(2,1)S(1)}, u32[]{:S(2)}, u32[]{:S(2)}) collective-permute-start(bf16[768,512]{1,0:T(8,128)(2,1)S(1)} %slice.12), channel_id=1, source_target_pairs={{2,0},{0,2},{3,1},{1,3},{6,4},{4,6},{7,5},{5,7},{10,8},{8,10},{11,... | collective-permute-start | bytes 2359304 | tf_op jit(solution)/shard_map/ppermute | solution.py:380
  24.0 16.0 %copy-start.13 = (bf16[640,512]{1,0:T(8,128)(2,1)}, bf16[640,512]{1,0:T(8,128)(2,1)S(1)}, u32[]{:S(2)}) copy-start(bf16[640,512]{1,0:T(8,128)(2,1)S(1)} %collective-permute-done.refs_0_) | copy-start | bytes 1966084
  24.0 16.0 %collective-permute-start.2 = (bf16[640,512]{1,0:T(8,128)(2,1)S(1)}, bf16[640,512]{1,0:T(8,128)(2,1)S(1)}, u32[]{:S(2)}, u32[]{:S(2)}) collective-permute-start(bf16[640,512]{1,0:T(8,128)(2,1)S(1)} %collective-permute-done.refs_0_), channel_id=1, source_target_pairs={{0,4},{4,0},{8,12},{12,8},{1,5},{5,1},{9,13},{13,9},{2,6},{6,2},{1... | collective-permute-start | bytes 1966088 | tf_op jit(solution)/shard_map/ppermute | solution.py:410
  34.6 5.4 %copy-start.12 = (bf16[768,512]{1,0:T(8,128)(2,1)}, bf16[768,512]{1,0:T(8,128)(2,1)S(1)}, u32[]{:S(2)}) copy-start(bf16[768,512]{1,0:T(8,128)(2,1)S(1)} %collective-permute-done.1.refs_1_) | copy-start | bytes 2359300
  40.0 0.9 copy-start.14
  59.4 7.6 %collective-permute-start.3 = (bf16[2048,1024]{1,0:T(8,128)(2,1)}, bf16[2048,1024]{1,0:T(8,128)(2,1)}, u32[]{:S(2)}, u32[]{:S(2)}) collective-permute-start(bf16[2048,1024]{1,0:T(8,128)(2,1)} %shard_map.56.refs_2_), channel_id=1, source_target_pairs={{1,0},{0,1},{3,2},{2,3},{5,4},{4,5},{7,6},{6,7},{9,8},{8,9},{11,10... | collective-permute-start | bytes 12582920 | tf_op jit(solution)/shard_map/ppermute | solution.py:428
  70.3 48.8 %collective-permute-start.4 = (bf16[2,512,1024]{2,1,0:T(8,128)(2,1)}, bf16[2,512,1024]{2,1,0:T(8,128)(2,1)}, u32[]{:S(2)}, u32[]{:S(2)}) collective-permute-start(bf16[2,512,1024]{2,1,0:T(8,128)(2,1)} %shard_map.57), channel_id=1, source_target_pairs={{2,0},{0,2},{3,1},{1,3},{6,4},{4,6},{7,5},{5,7},{10,8},{8,10},{11,... | collective-permute-start | bytes 6291464 | tf_op jit(solution)/shard_map/ppermute | solution.py:512
  82.2 50.4 %collective-permute-start.5 = (bf16[528,2048]{1,0:T(8,128)(2,1)}, bf16[528,2048]{1,0:T(8,128)(2,1)S(1)}, u32[]{:S(2)}, u32[]{:S(2)}) collective-permute-start(bf16[528,2048]{1,0:T(8,128)(2,1)} %get-tuple-element.37), channel_id=1, source_target_pairs={{0,4},{12,8},{2,6},{14,10},{1,5},{13,9},{3,7},{15,11},{16,20},{28,... | collective-permute-start | bytes 6488072 | tf_op jit(solution)/shard_map/ppermute | solution.py:538
  97.2 65.8 %collective-permute-start.7 = (bf16[2,512,1024]{2,1,0:T(8,128)(2,1)}, bf16[2,512,1024]{2,1,0:T(8,128)(2,1)S(1)}, u32[]{:S(2)}, u32[]{:S(2)}) collective-permute-start(bf16[2,512,1024]{2,1,0:T(8,128)(2,1)} %shard_map.63), channel_id=1, source_target_pairs={{2,0},{0,2},{3,1},{1,3},{6,4},{4,6},{7,5},{5,7},{10,8},{8,10},{11,... | collective-permute-start | bytes 6291464 | tf_op jit(solution)/shard_map/ppermute | solution.py:512
  129.2 13.4 %collective-permute-start.6 = (bf16[256,2048]{1,0:T(8,128)(2,1)}, bf16[256,2048]{1,0:T(8,128)(2,1)S(1)}, u32[]{:S(2)}, u32[]{:S(2)}) collective-permute-start(bf16[256,2048]{1,0:T(8,128)(2,1)} %get-tuple-element.42), channel_id=1, source_target_pairs={{0,4},{14,10},{1,5},{15,11},{16,20},{30,26},{17,21},{31,27}} | collective-permute-start | bytes 3145736 | tf_op jit(solution)/shard_map/ppermute | solution.py:538
  130.0 56.8 %collective-permute-start.11 = (bf16[528,2048]{1,0:T(8,128)(2,1)}, bf16[528,2048]{1,0:T(8,128)(2,1)}, u32[]{:S(2)}, u32[]{:S(2)}) collective-permute-start(bf16[528,2048]{1,0:T(8,128)(2,1)} %get-tuple-element.39), channel_id=1, source_target_pairs={{12,8},{2,6},{13,9},{3,7},{28,24},{18,22},{29,25},{19,23}} | collective-permute-start | bytes 6488072 | tf_op jit(solution)/shard_map/ppermute | solution.py:538
  132.6 1.4 copy-start
  139.1 47.6 %collective-permute-start.10 = (bf16[528,2048]{1,0:T(8,128)(2,1)}, bf16[528,2048]{1,0:T(8,128)(2,1)}, u32[]{:S(2)}, u32[]{:S(2)}) collective-permute-start(bf16[528,2048]{1,0:T(8,128)(2,1)} %shard_map.61), channel_id=1, source_target_pairs={{8,4},{6,10},{9,5},{7,11},{24,20},{22,26},{25,21},{23,27}} | collective-permute-start | bytes 6488072 | tf_op jit(solution)/shard_map/ppermute | solution.py:538
  141.9 35.1 %collective-permute-start.8 = (bf16[256,2048]{1,0:T(8,128)(2,1)}, bf16[256,2048]{1,0:T(8,128)(2,1)S(1)}, u32[]{:S(2)}, u32[]{:S(2)}) collective-permute-start(bf16[256,2048]{1,0:T(8,128)(2,1)} %get-tuple-element.45), channel_id=1, source_target_pairs={{0,4},{14,10},{1,5},{15,11},{16,20},{30,26},{17,21},{31,27}} | collective-permute-start | bytes 3145736 | tf_op jit(solution)/shard_map/ppermute | solution.py:538
  142.6 1.0 copy-start.17
  146.6 35.7 %collective-permute-start.9 = (bf16[256,2048]{1,0:T(8,128)(2,1)}, bf16[256,2048]{1,0:T(8,128)(2,1)S(1)}, u32[]{:S(2)}, u32[]{:S(2)}) collective-permute-start(bf16[256,2048]{1,0:T(8,128)(2,1)} %shard_map.62), channel_id=1, source_target_pairs={{4,8},{10,6},{5,9},{11,7},{20,24},{26,22},{21,25},{27,23}} | collective-permute-start | bytes 3145736 | tf_op jit(solution)/shard_map/ppermute | solution.py:538
  149.9 24.7 %copy-start.10 = (bf16[256,2048]{1,0:T(8,128)(2,1)S(1)}, bf16[256,2048]{1,0:T(8,128)(2,1)}, u32[]{:S(2)}) copy-start(bf16[256,2048]{1,0:T(8,128)(2,1)} %get-tuple-element.42) | copy-start | bytes 3145732
  163.1 1.3 copy-start.1
  175.7 32.0 %collective-permute-start.12 = (bf16[256,2048]{1,0:T(8,128)(2,1)}, bf16[256,2048]{1,0:T(8,128)(2,1)S(1)}, u32[]{:S(2)}, u32[]{:S(2)}) collective-permute-start(bf16[256,2048]{1,0:T(8,128)(2,1)} %broadcast_select_fusion), channel_id=1, source_target_pairs={{0,4},{12,8},{2,6},{14,10},{1,5},{13,9},{3,7},{15,11},{16,20},{28,... | collective-permute-start | bytes 3145736 | tf_op jit(solution)/shard_map/ppermute | solution.py:538
  177.0 1.0 copy-start.6
  181.0 32.1 %collective-permute-start.13 = (bf16[256,2048]{1,0:T(8,128)(2,1)}, bf16[256,2048]{1,0:T(8,128)(2,1)}, u32[]{:S(2)}, u32[]{:S(2)}) collective-permute-start(bf16[256,2048]{1,0:T(8,128)(2,1)} %shard_map.65), channel_id=1, source_target_pairs={{4,8},{10,6},{5,9},{11,7},{20,24},{26,22},{21,25},{27,23}} | collective-permute-start | bytes 3145736 | tf_op jit(solution)/shard_map/ppermute | solution.py:538
  182.3 1.0 copy-start.7
  186.7 11.8 %copy-start.11 = (bf16[256,2048]{1,0:T(8,128)(2,1)S(1)}, bf16[256,2048]{1,0:T(8,128)(2,1)}, u32[]{:S(2)}) copy-start(bf16[256,2048]{1,0:T(8,128)(2,1)} %get-tuple-element.51) | copy-start | bytes 3145732
  192.8 9.3 %copy-start.5 = (bf16[256,2048]{1,0:T(8,128)(2,1)S(1)}, bf16[256,2048]{1,0:T(8,128)(2,1)}, u32[]{:S(2)}) copy-start(bf16[256,2048]{1,0:T(8,128)(2,1)} %shard_map.66) | copy-start | bytes 3145732
  192.8 51.2 %collective-permute-start.15 = (bf16[528,2048]{1,0:T(8,128)(2,1)}, bf16[528,2048]{1,0:T(8,128)(2,1)S(1)}, u32[]{:S(2)}, u32[]{:S(2)}) collective-permute-start(bf16[528,2048]{1,0:T(8,128)(2,1)} %shard_map.67), channel_id=1, source_target_pairs={{4,0},{10,14},{8,4},{6,10},{5,1},{11,15},{9,5},{7,11},{20,16},{26,... | collective-permute-start | bytes 6488072 | tf_op jit(solution)/shard_map/ppermute | solution.py:538
  200.8 26.0 %collective-permute-start.14 = (bf16[256,2048]{1,0:T(8,128)(2,1)}, bf16[256,2048]{1,0:T(8,128)(2,1)S(1)}, u32[]{:S(2)}, u32[]{:S(2)}) collective-permute-start(bf16[256,2048]{1,0:T(8,128)(2,1)} %broadcast_select_fusion.1), channel_id=1, source_target_pairs={{0,4},{12,8},{2,6},{14,10},{1,5},{13,9},{3,7},{15,11},{16,20},{28,... | collective-permute-start | bytes 3145736 | tf_op jit(solution)/shard_map/ppermute | solution.py:538
  202.1 49.7 %collective-permute-start.16 = (bf16[256,2048]{1,0:T(8,128)(2,1)S(1)}, bf16[256,2048]{1,0:T(8,128)(2,1)}, u32[]{:S(2)}, u32[]{:S(2)}) collective-permute-start(bf16[256,2048]{1,0:T(8,128)(2,1)S(1)} %copy-done.5), channel_id=1, source_target_pairs={{8,12},{6,2},{9,13},{7,3},{24,28},{22,18},{25,29},{23,19}} | collective-permute-start | bytes 3145736 | tf_op jit(solution)/shard_map/ppermute | solution.py:538
  207.7 1.0 copy-start.2
  211.8 40.0 %collective-permute-start.17 = (bf16[256,2048]{1,0:T(8,128)(2,1)}, bf16[256,2048]{1,0:T(8,128)(2,1)}, u32[]{:S(2)}, u32[]{:S(2)}) collective-permute-start(bf16[256,2048]{1,0:T(8,128)(2,1)} %shard_map.68), channel_id=1, source_target_pairs={{4,8},{10,6},{5,9},{11,7},{20,24},{26,22},{21,25},{27,23}} | collective-permute-start | bytes 3145736 | tf_op jit(solution)/shard_map/ppermute | solution.py:538
  216.5 40.3 %collective-permute-start.18 = (bf16[256,2048]{1,0:T(8,128)(2,1)}, bf16[256,2048]{1,0:T(8,128)(2,1)S(1)}, u32[]{:S(2)}, u32[]{:S(2)}) collective-permute-start(bf16[256,2048]{1,0:T(8,128)(2,1)} %shard_map.69), channel_id=1, source_target_pairs={{8,12},{6,2},{9,13},{7,3},{24,28},{22,18},{25,29},{23,19}} | collective-permute-start | bytes 3145736 | tf_op jit(solution)/shard_map/ppermute | solution.py:538
  226.9 1.0 copy-start.3
  230.9 28.9 %collective-permute-start.19 = (bf16[256,2048]{1,0:T(8,128)(2,1)}, bf16[256,2048]{1,0:T(8,128)(2,1)S(1)}, u32[]{:S(2)}, u32[]{:S(2)}) collective-permute-start(bf16[256,2048]{1,0:T(8,128)(2,1)} %shard_map.70), channel_id=1, source_target_pairs={{4,8},{10,6},{5,9},{11,7},{20,24},{26,22},{21,25},{27,23}} | collective-permute-start | bytes 3145736 | tf_op jit(solution)/shard_map/ppermute | solution.py:538
  244.1 1.4 copy-start.4
  256.8 3.0 %copy-start.8 = (bf16[256,2048]{1,0:T(8,128)(2,1)}, bf16[256,2048]{1,0:T(8,128)(2,1)S(1)}, u32[]{:S(2)}) copy-start(bf16[256,2048]{1,0:T(8,128)(2,1)S(1)} %collective-permute-done.18.refs_3_) | copy-start | bytes 3145732
  259.7 1.0 copy-start.9

commit v6 on v5

--- a/solution.py
+++ b/solution.py
@@ -76,30 +76,41 @@
             )
             return jnp.dot(left, right, preferred_element_type=jnp.float32)
 
-        total[...] = early_ref[inner] if last else jnp.zeros_like(total)
-        full = lax.div(count, GROUP)
-        rest = count - full * GROUP
-
-        @pl.loop(0, full)
-        def _(g):
-            total[...] += product(g * GROUP, GROUP, False)
-
-        @pl.when(rest > GROUP // 2)
-        def _():
-            total[...] += product(full * GROUP, GROUP, True)
-
-        @pl.when((rest > 0) & (rest <= GROUP // 2))
-        def _():
-            total[...] += product(full * GROUP, GROUP // 2, True)
-
-        if last:
+        def emit(value):
+            if not last:
+                out_ref[inner] = value
+                return
             rows = pl.ds(pl.multiple_of(inner * side, side), side)
             for p in range(functions):
-                out_ref[rows, p * width : (p + 1) * width] = total[p * side : (p + 1) * side, :].astype(
+                out_ref[rows, p * width : (p + 1) * width] = value[p * side : (p + 1) * side, :].astype(
                     out_ref.dtype
                 )
-        else:
-            out_ref[inner] = total[...]
+
+        def begin(value):
+            return early_ref[inner] + value if last else value
+
+        @pl.when(count == 0)
+        def _():
+            emit(begin(jnp.zeros_like(total)))
+
+        @pl.when((count > 0) & (count <= GROUP // 2))
+        def _():
+            emit(begin(product(0, GROUP // 2, True)))
+
+        @pl.when((count > GROUP // 2) & (count <= GROUP))
+        def _():
+            emit(begin(product(0, GROUP, True)))
+
+        @pl.when(count > GROUP)
+        def _():
+            total[...] = begin(product(0, GROUP, False))
+            groups = lax.div(count - 1, GROUP)
+
+            @pl.loop(1, groups)
+            def _(g):
+                total[...] += product(g * GROUP, GROUP, False)
+
+            emit(total[...] + product(groups * GROUP, GROUP, True))
 
 
 def transform(three_index, order, columns, bounds, coeff_parts, early=None):
@@ -207,53 +218,60 @@
     )(flags, *operands)
 
 
-def fold_kernel(flags, *refs, at, extra, first):
-    before_ref, sums_ref, came_refs, out_ref = refs[0], refs[1], refs[2:-1], refs[-1]
+def fold_kernel(flags, *refs, at, terms):
+    term_refs, out_ref = refs[: len(terms)], refs[-1]
     rows, tile = out_ref.shape
-    total = jnp.where(flags[at] > 0, sums_ref[...], 0.0)
-    if not first:
-        total = total + before_ref[...]
+    total = jnp.zeros((rows, tile), jnp.float32)
     lost = jnp.zeros((1, tile), jnp.float32)
-    for i, ref in enumerate(came_refs):
-        total = total + jnp.where(flags[at + i + 1] > 0, ref[:rows].astype(jnp.float32), 0.0)
-        if extra:
-            lost = lost + jnp.where(flags[at + i + 1] > 0, ref[rows : rows + 1].astype(jnp.float32), 0.0)
-    if extra:
-        row = lax.broadcasted_iota(jnp.int32, (rows, tile), 0) + flags[at + len(came_refs) + 1]
-        col = lax.broadcasted_iota(jnp.int32, (rows, tile), 1) + pl.program_id(0) * tile
-        total = total + jnp.where(row == col, lost, 0.0)
-    out_ref[...] = total
-
-
-def fold(flags, at, before, sums, came, rows, piece, extra, first):
-    height, length = before.shape
+    for ref, (flag, is_extra) in zip(term_refs, terms):
+        if is_extra:
+            lost = lost + jnp.where(flags[at + flag] > 0, ref[:1].astype(jnp.float32), 0.0)
+        else:
+            total = total + jnp.where(flags[at + flag] > 0, ref[...].astype(jnp.float32), 0.0)
+    row = lax.broadcasted_iota(jnp.int32, (rows, tile), 0) + flags[at + max(flag for flag, _ in terms) + 1]
+    col = lax.broadcasted_iota(jnp.int32, (rows, tile), 1) + pl.program_id(0) * tile
+    out_ref[...] = total + jnp.where(row == col, lost, 0.0)
+
+
+def fold(flags, at, phases, before, piece, c):
+    height, length = phases[0][0].shape
     tile = min(length, 1024)
-    in_place = pl.BlockSpec((rows, tile), lambda j, flags: (piece, j))
+    operands, in_specs, terms = [], [], []
+
+    def add(array, rows, block, flag, is_extra):
+        operands.append(array)
+        in_specs.append(pl.BlockSpec((rows, tile), lambda j, flags: (block, j * flags[at + flag])))
+        terms.append((flag, is_extra))
+
+    flag = 0
+    for sums, messages in phases:
+        add(sums, piece, c, flag, False)
+        flag += 1
+        for message in messages:
+            whole = message.shape[0] > piece
+            add(message, piece, c if whole else 0, flag, False)
+            if message.shape[0] % piece:
+                add(message, EXTRA, message.shape[0] // EXTRA - 1, flag, True)
+            flag += 1
+    again = [] if before is None else [before]
     return pl.pallas_call(
-        functools.partial(fold_kernel, at=at, extra=extra, first=first),
+        functools.partial(fold_kernel, at=at, terms=terms),
         grid_spec=pltpu.PrefetchScalarGridSpec(
             num_scalar_prefetch=1,
             grid=(length // tile,),
-            in_specs=[
-                pl.BlockSpec((rows, tile), lambda j, flags: (piece, 0)) if first else in_place,
-                pl.BlockSpec((rows, tile), lambda j, flags: (piece, j * flags[at])),
-            ]
-            + [
-                pl.BlockSpec((message.shape[0], tile), lambda j, flags, i=i: (0, j * flags[at + i + 1]))
-                for i, message in enumerate(came)
-            ],
-            out_specs=in_place,
-        ),
-        out_shape=jax.ShapeDtypeStruct(before.shape, before.dtype),
-        input_output_aliases={} if first else {1: 0},
+            in_specs=in_specs + [pl.BlockSpec(memory_space=pl.ANY)] * len(again),
+            out_specs=pl.BlockSpec((piece, tile), lambda j, flags: (c, j)),
+        ),
+        out_shape=jax.ShapeDtypeStruct((height, length), jnp.float32),
+        input_output_aliases={1 + len(operands): 0} if again else {},
         compiler_params=pltpu.CompilerParams(vmem_limit_bytes=VMEM_LIMIT),
         cost_estimate=pl.CostEstimate(flops=COST, bytes_accessed=COST, transcendentals=0),
-    )(flags, before, sums, *came)
-
-
-def product_kernel(index, *refs, at, parts, extra):
-    out_ref, piece_refs = refs[2 * parts], refs[2 * parts + 1 :]
-    total = None
+    )(flags, *operands, *again)
+
+
+def product_kernel(index, *refs, at, parts, extra, begun):
+    out_ref, piece_refs = refs[2 * parts + begun], refs[2 * parts + begun + 1 :]
+    total = refs[2 * parts][...] if begun else None
     for rows_ref, cols_ref in zip(refs[:parts], refs[parts : 2 * parts]):
         term = lax.dot_general(
             rows_ref[0], cols_ref[...], (((1,), (1,)), ((), ())), preferred_element_type=jnp.float32
@@ -265,21 +283,22 @@
         store_rounded(ref, total[c * rows : (c + 1) * rows], index[at] * total.shape[0] + c * rows, None)
 
 
-def row_product(index, at, rows, cols, pieces, extra, cost):
+def row_product(index, at, rows, cols, pieces, extra, cost, early=()):
     parts = len(rows)
     height, depth = rows[0].shape[1:]
     length = cols[0].shape[0]
     tile = min(length, 512)
     taller = height // max(pieces, 1) + extra
     return pl.pallas_call(
-        functools.partial(product_kernel, at=at, parts=parts, extra=extra),
+        functools.partial(product_kernel, at=at, parts=parts, extra=extra, begun=len(early)),
         grid_spec=pltpu.PrefetchScalarGridSpec(
             num_scalar_prefetch=1,
             grid=(length // tile,),
             in_specs=[
                 pl.BlockSpec((1, height, depth), lambda c, index, t=t: (index[at + t], 0, 0)) for t in range(parts)
             ]
-            + [pl.BlockSpec((tile, depth), lambda c, index: (c, 0))] * parts,
+            + [pl.BlockSpec((tile, depth), lambda c, index: (c, 0))] * parts
+            + [pl.BlockSpec((height, tile), lambda c, index: (0, c))] * len(early),
             out_specs=[pl.BlockSpec((height, tile), lambda c, index: (0, c))]
             + [pl.BlockSpec((taller, tile), lambda c, index: (0, c))] * pieces,
         ),
@@ -287,7 +306,7 @@
         + [jax.ShapeDtypeStruct((taller, length), jnp.bfloat16)] * pieces,
         compiler_params=pltpu.CompilerParams(vmem_limit_bytes=VMEM_LIMIT),
         cost_estimate=pl.CostEstimate(flops=cost, bytes_accessed=COST, transcendentals=0),
-    )(index, *rows, *cols)
+    )(index, *rows, *cols, *early)
 
 
 class Line:
@@ -384,31 +403,35 @@
     columns = lax.rem(block_cols[0] - o * blocks + all_blocks, all_blocks)
     slot = lax.broadcasted_iota(jnp.int32, columns.shape, 1)
     alive = slot < live_count[0][:, None]
-    mine = columns < blocks
+    within = lax.rem(columns, blocks)
+    shard = lax.div(columns, blocks)
+    half = lax.div(within, max(share, 1))
+    shared = within < 2 * share
+    mine = (shard == 0) | (shared & (half == parity))
+    placed = jnp.where(
+        shard == 0,
+        within,
+        jnp.where(
+            mine,
+            blocks + (shard - 1) * share + within - half * share,
+            (shard - 1) * (blocks - share)
+            + jnp.where(shared, blocks - 2 * share + within - half * share, within - 2 * share),
+        ),
+    )
     rank_key = jnp.where(alive, jnp.where(mine, 0, slots), 2 * slots) + slot
     rank = jnp.sum((rank_key[:, None, :] < rank_key[:, :, None]).astype(jnp.int32), axis=2)
-    within = lax.rem(columns, blocks)
-    half = lax.div(within, max(share, 1))
-    moved = jnp.where(
-        within >= 2 * share,
-        within - share,
-        jnp.where(half == parity, within - half * share, within - half * share + blocks - share),
-    )
-    placed = jnp.where(mine, columns, columns - within - blocks + moved)
     at_rank = rank[:, None, :] == lax.broadcasted_iota(jnp.int32, (1, slots, 1), 1)
     order = jnp.sum(jnp.where(at_rank, slot[:, None, :], 0), axis=2)
     columns = jnp.sum(jnp.where(at_rank, placed[:, None, :], 0), axis=2)
     live = jnp.sum(alive.astype(jnp.int32), axis=1)
     near = jnp.sum((alive & mine).astype(jnp.int32), axis=1)
     bounds = jnp.stack([jnp.zeros_like(near), near], axis=1)
-    early = transform(three_index, order, columns, bounds, [coefficients])
     coeff_parts = []
     for k in range(1, orb):
-        if not share:
-            coeff_parts.append(rests[k - 1])
-            continue
-        handed = lax.ppermute(after(firsts[k - 1], early), "aux", [(i, i ^ 1) for i in range(aux)])
-        coeff_parts += [firsts[k - 1], rests[k - 1], handed]
+        coeff_parts.append(rests[k - 1])
+        if share:
+            coeff_parts.append(lax.ppermute(firsts[k - 1], "aux", [(i, i ^ 1) for i in range(aux)]))
+    early = transform(three_index, order, columns, bounds, [coefficients] + firsts)
     if coeff_parts:
         bounds = jnp.stack([near, live], axis=1)
         own = transform(three_index, order, columns, bounds, coeff_parts, early)
@@ -461,9 +484,8 @@
             if any(line.hop(k, *member)[2] for member in group):
                 finals.append((k, tuple(group)))
     end = max(e[0] for e in events)
-    for k in range(orb):
-        for c in range(pieces(k)):
-            events.append((end + 1 + k, c, "fold", k, c, 0))
+    for c in range(halves):
+        events.append((end + 1, c, "fold", orb - 1, c, 0))
     events.sort(key=lambda e: e[:2])
 
     plans = []
@@ -489,15 +511,17 @@
                 start = sum(own_block(a, b, d, q) for (_, _, q), flag in zip(choices, chosen) if flag)
                 rows.append(chosen + [start * height])
         else:
-            groups = [group for k_, group in finals if k_ == k]
-            ends = [{i for member in group for i in line.hop(k, *member)[2]} for group in groups]
+            piece = height // halves
+            groups = [[group for k_, group in finals if k_ == phase] for phase in range(orb)]
             plan.update(groups=groups)
-            rows = [
-                [a in line.targets(k, b)]
-                + [a * orb + b in end_ for end_ in ends]
-                + [(a % owned * sub + d) * height + what * piece]
-                for a, b, d in places
-            ]
+            rows = []
+            for a, b, d in places:
+                row = []
+                for phase in range(orb):
+                    row.append(a in line.targets(phase, b))
+                    for group in groups[phase]:
+                        row.append(any(a * orb + b in line.hop(phase, *member)[2] for member in group))
+                rows.append(row + [(a % owned * sub + d) * height + what * piece])
         plan.update(at=scalars(rows), piece=piece)
         plans.append(plan)
     everywhere = lookup(table, place * sub + s)
@@ -514,7 +538,13 @@
             rows = [came_rows[k, what]] * sub if k else views
             flops = 2 * sub * height * length * depth if k and what == 0 else COST
             sums[k, what], *heads[k, what] = row_product(
-                after(everywhere, last), at, rows, cols, pieces(k), extra, flops
+                after(everywhere, last),
+                at,
+                rows,
+                cols,
+                pieces(k),
+                extra,
+                flops,
             )
             last = sums[k, what]
         elif plan["kind"] == "hop":
@@ -539,10 +569,11 @@
             for member in what:
                 came[(k,) + member + (c,)] = arrived
         else:
-            messages = [came[(k,) + group[0] + (what,)] for group in plan["groups"]]
-            mine = sums[k, owned - 1]
-            before = mine if result is None else result
-            result = fold(after(everywhere, last), at, before, mine, messages, piece, what, extra, result is None)
+            phases = []
+            for phase, groups in enumerate(plan["groups"]):
+                part = what if pieces(phase) == halves else 0
+                phases.append((sums[phase, owned - 1], [came[(phase,) + g[0] + (part,)] for g in groups]))
+            result = fold(after(everywhere, last), at, phases, result, piece, what)
             last = result
     return result
 

time: 267 us -> 267 us (level)
  Pallas kernels: 130 us -> 113 us
  starting transfers between devices: 31.3 us -> 41.3 us
  waiting for transfers between devices: 80.7 us -> 85.7 us
    ppermute x1, waiting for transfers between devices: 0.01 us -> 14.3 us  [shards(): firsts.append(lax.ppermute(first, 'orb', pairs))]
    ppermute x14, waiting for transfers between devices: 25.3 us -> 38.4 us  [shards(): arrived = lax.ppermute(value, ('aux', 'orb'), plan['pairs'])]
    pallas_call x2, Pallas kernels: 35.3 us -> 24 us  [transform(): pl.pallas_call(functools.partial(transform_kernel, parts=parts, last=last...]
    ppermute x1, waiting for transfers between devices: 9.79 us -> 0.01 us  [shards(): rests.append(lax.ppermute(coefficients[2 * share * side:], 'orb', pairs))]
    ppermute x14, starting transfers between devices: 27 us -> 35.5 us  [shards(): arrived = lax.ppermute(value, ('aux', 'orb'), plan['pairs'])]
    ppermute x2, waiting for transfers between devices: 34 us -> 26.6 us  [shards(): came_rows[k, what] = lax.ppermute(last, 'orb', pairs)]
    ppermute x1, waiting for transfers between devices: 5.39 us -> 0.01 us  [shards(): lax.ppermute(firsts[k - 1], 'aux', [(i, i ^ 1) for i in range(aux)])]
    pallas_call x3 -> x2, Pallas kernels: 16.2 us -> 11 us  [fold(): pl.pallas_call(functools.partial(fold_kernel, at=at, terms=terms), grid_s...]
  transfers between devices with their start and end apart: 20 -> 20, of which waited for: 9 -> 10; matrix products, arithmetic and copies ran while one was open for 4% -> 4% of each run, Pallas kernels for 39% -> 35%
where the time goes in v6:
time: 267 us; the launch traced here: 264 us
  Pallas kernels  113 us (42%)
  waiting for transfers between devices  85.7 us (32%)
  starting transfers between devices  41.3 us (15%)
  local copies, waits for them, and re-layouts  16.6 us (6%)
  other arithmetic  5.29 us (2%)
    pallas_call x4, Pallas kernels, row_product(): pl.pallas_call(functools.partial(product_kernel, at=at, parts=parts, extr...  41.5 us
    ppermute x14, waiting for transfers between devices, shards(): arrived = lax.ppermute(value, ('aux', 'orb'), plan['pairs'])  38.4 us
    ppermute x14, starting transfers between devices, shards(): arrived = lax.ppermute(value, ('aux', 'orb'), plan['pairs'])  35.5 us
    pallas_call x8, Pallas kernels, forward(): pl.pallas_call(functools.partial(forward_kernel, at=at, choices=choices,...  30.2 us
    ppermute x2, waiting for transfers between devices, shards(): came_rows[k, what] = lax.ppermute(last, 'orb', pairs)  26.6 us
    pallas_call x2, Pallas kernels, transform(): pl.pallas_call(functools.partial(transform_kernel, parts=parts, last=last...  24 us
    ppermute x1, waiting for transfers between devices, shards(): firsts.append(lax.ppermute(first, 'orb', pairs))  14.3 us
    unnamed x32, local copies, waits for them, and re-layouts  11.1 us
  transfers between devices with their start and end apart: 20, of which 10 were waited for; matrix products, arithmetic and copies ran while one was open for 4% of the time, Pallas kernels for 35%

profile of v6, /device:TPU:20, one launch (start us, length us, event | category | flops | bytes accessed | tf_op | source)
XLA Modules:
  0.0 263.7 jit_solution(4016290501399295499)
XLA Ops:
  1.2 1.6 collective-permute-start.1
  4.5 14.3 %collective-permute-done.1.refs_1_ = bf16[640,512]{1,0:T(8,128)(2,1)S(1)} collective-permute-done((bf16[640,512]{1,0:T(8,128)(2,1)S(1)}, bf16[640,512]{1,0:T(8,128)(2,1)S(1)}, u32[]{:S(2)}, u32[]{:S(2)}) %collective-permute-start.1) | collective-permute-done | bytes 655392 | tf_op jit(solution)/shard_map/ppermute | solution.py:398
  18.9 1.6 collective-permute-start.2
  23.8 11.7 %shard_map.55.refs_2_ = f32[16,256,512]{2,1,0:T(8,128)} custom-call(s32[16,16]{1,0:T(8,128)} %get-tuple-element.62.order, s32[16,16]{1,0:T(8,128)} %get-tuple-element.61.columns, s32[16,2]{1,0:T(8,128)} %stack.16.bounds, bf16[2,16,16,128,128]{4,3,2,1,0:T(8,128)(2,1)} %x_ref.3, bf16[2048,512]{1,0:T(8,128)(2,1)} %refs_0_.1, bf16[640,512]{1,0:T(8,128)(2,1)} %copy-done.12), custom_call_target="tpu_custom_call" | custom-call | flops 1024 | bytes 1024 | tf_op jit(solution)/shard_map/pallas_call | solution.py:123
  37.4 12.3 %shard_map.56.refs_2_ = bf16[2048,1024]{1,0:T(8,128)(2,1)} custom-call(s32[16,16]{1,0:T(8,128)} %get-tuple-element.62.order, s32[16,16]{1,0:T(8,128)} %get-tuple-element.61.columns, s32[16,2]{1,0:T(8,128)} %copy.13.bounds, bf16[2,16,16,128,128]{4,3,2,1,0:T(8,128)(2,1)} %x_ref.3, bf16[768,512]{1,0:T(8,128)(2,1)} %copy-done.11, bf16[640,512]{1,0:T(8,128)(2,1)} %copy-done.13, ...), custom_call_target="tpu_custom_call" | custom-call | flops 1024 | bytes 1024 | tf_op jit(solution)/shard_map/pallas_call | solution.py:123
  50.9 6.3 %collective-permute-done.3.refs_3_ = bf16[2048,1024]{1,0:T(8,128)(2,1)} collective-permute-done((bf16[2048,1024]{1,0:T(8,128)(2,1)}, bf16[2048,1024]{1,0:T(8,128)(2,1)}, u32[]{:S(2)}, u32[]{:S(2)}) %collective-permute-start.3) | collective-permute-done | bytes 4194336 | tf_op jit(solution)/shard_map/ppermute | solution.py:451
  57.2 3.3 %shard_map.57 = bf16[2,512,1024]{2,1,0:T(8,128)(2,1)} custom-call(s32[57]{0:T(128)} %get-tuple-element.60.index.flags, bf16[4,512,1024]{2,1,0:T(8,128)(2,1)} %bitcast.16, bf16[4,512,1024]{2,1,0:T(8,128)(2,1)} %bitcast.7.refs_1_), custom_call_target="tpu_custom_call" | custom-call | flops 1024 | bytes 1024 | tf_op jit(solution)/shard_map/pallas_call | solution.py:155
  60.5 1.3 collective-permute-start.4
  61.9 10.9 %shard_map.58 = (f32[512,2048]{1,0:T(8,128)}, bf16[528,2048]{1,0:T(8,128)(2,1)}) custom-call(s32[57]{0:T(128)} %get-tuple-element.60.index.flags, bf16[4,512,1024]{2,1,0:T(8,128)(2,1)} %bitcast.17, bf16[4,512,1024]{2,1,0:T(8,128)(2,1)} %bitcast.7.refs_1_, bf16[2048,1024]{1,0:T(8,128)(2,1)} %shard_map.56.refs_2_, ...), custom_call_target="tpu_custom_call" | custom-call | flops 1024 | bytes 1024 | tf_op jit(solution)/shard_map/pallas_call | solution.py:292
  72.7 1.3 collective-permute-start.5
  74.0 10.4 %shard_map.59 = (f32[512,2048]{1,0:T(8,128)}, bf16[528,2048]{1,0:T(8,128)(2,1)}) custom-call(s32[57]{0:T(128)} %get-tuple-element.60.index.flags, bf16[4,512,1024]{2,1,0:T(8,128)(2,1)} %bitcast.18, bf16[4,512,1024]{2,1,0:T(8,128)(2,1)} %bitcast.7.refs_1_, bf16[2048,1024]{1,0:T(8,128)(2,1)} %shard_map.56.refs_2_, ...), custom_call_target="tpu_custom_call" | custom-call | flops 1024 | bytes 1024 | tf_op jit(solution)/shard_map/pallas_call | solution.py:292
  84.4 3.3 %shard_map.63 = bf16[2,512,1024]{2,1,0:T(8,128)(2,1)} custom-call(s32[57]{0:T(128)} %get-tuple-element.60.index.flags, bf16[4,512,1024]{2,1,0:T(8,128)(2,1)} %bitcast.19, bf16[4,512,1024]{2,1,0:T(8,128)(2,1)} %bitcast.7.refs_1_), custom_call_target="tpu_custom_call" | custom-call | flops 1024 | bytes 1024 | tf_op jit(solution)/shard_map/pallas_call | solution.py:155
  88.5 20.9 %collective-permute-done.4.refs_0_.refs_1_ = bf16[2,512,1024]{2,1,0:T(8,128)(2,1)} collective-permute-done((bf16[2,512,1024]{2,1,0:T(8,128)(2,1)}, bf16[2,512,1024]{2,1,0:T(8,128)(2,1)}, u32[]{:S(2)}, u32[]{:S(2)}) %collective-permute-start.4) | collective-permute-done | bytes 2097184 | tf_op jit(solution)/shard_map/ppermute | solution.py:536
  109.3 10.1 %shard_map.60 = (f32[512,2048]{1,0:T(8,128)}, bf16[256,2048]{1,0:T(8,128)(2,1)}, bf16[256,2048]{1,0:T(8,128)(2,1)}) custom-call(s32[57]{0:T(128)} %get-tuple-element.60.index.flags, bf16[2,512,1024]{2,1,0:T(8,128)(2,1)} %collective-permute-done.4.refs_0_.refs_1_, bf16[2,512,1024]{2,1,0:T(8,128)(2,1)} %collective-permute-done.4.refs_0_.refs_1_, ...), custom_call_target="tpu_custom_call" | custom-call | flops 4294967296 | bytes 1024 | tf_op jit(solution)/shard_map/pallas_call | solution.py:292
  119.4 1.6 collective-permute-start.6
  121.1 1.3 collective-permute-start.11
  123.1 1.4 copy-done
  124.5 5.1 %shard_map.61 = bf16[528,2048]{1,0:T(8,128)(2,1)} custom-call(s32[57]{0:T(128)} %get-tuple-element.60.index.flags, f32[512,2048]{1,0:T(8,128)} %get-tuple-element.41.refs_0_, bf16[528,2048]{1,0:T(8,128)(2,1)} %copy-done), custom_call_target="tpu_custom_call" | custom-call | flops 1024 | bytes 1024 | tf_op jit(solution)/shard_map/pallas_call | solution.py:207
  129.6 11.1 %collective-permute-start.10 = (bf16[528,2048]{1,0:T(8,128)(2,1)}, bf16[528,2048]{1,0:T(8,128)(2,1)S(1)}, u32[]{:S(2)}, u32[]{:S(2)}) collective-permute-start(bf16[528,2048]{1,0:T(8,128)(2,1)} %shard_map.61), channel_id=1, source_target_pairs={{8,4},{6,10},{9,5},{7,11},{24,20},{22,26},{25,21},{23,27}} | collective-permute-start | bytes 6488072 | tf_op jit(solution)/shard_map/ppermute | solution.py:568
  141.5 3.0 %shard_map.62 = bf16[256,2048]{1,0:T(8,128)(2,1)} custom-call(s32[57]{0:T(128)} %get-tuple-element.60.index.flags, f32[512,2048]{1,0:T(8,128)} %get-tuple-element.44.refs_0_, bf16[256,2048]{1,0:T(8,128)(2,1)} %collective-permute-done.6.refs_1_), custom_call_target="tpu_custom_call" | custom-call | flops 4000000000 | bytes 1024 | tf_op jit(solution)/shard_map/pallas_call | solution.py:207
  144.5 1.3 collective-permute-start.9
  147.6 5.8 %collective-permute-done.7.refs_0_.refs_1_ = bf16[2,512,1024]{2,1,0:T(8,128)(2,1)S(1)} collective-permute-done((bf16[2,512,1024]{2,1,0:T(8,128)(2,1)}, bf16[2,512,1024]{2,1,0:T(8,128)(2,1)S(1)}, u32[]{:S(2)}, u32[]{:S(2)}) %collective-permute-start.7) | collective-permute-done | bytes 2097184 | tf_op jit(solution)/shard_map/ppermute | solution.py:536
  153.4 1.3 copy-done.2
  154.6 10.1 %shard_map.64 = (f32[512,2048]{1,0:T(8,128)}, bf16[256,2048]{1,0:T(8,128)(2,1)}, bf16[256,2048]{1,0:T(8,128)(2,1)}) custom-call(s32[57]{0:T(128)} %get-tuple-element.60.index.flags, bf16[2,512,1024]{2,1,0:T(8,128)(2,1)} %copy-done.2, bf16[2,512,1024]{2,1,0:T(8,128)(2,1)} %copy-done.2, bf16[2048,1024]{1,0:T(8,128)(2,1)} %shard_map.56.refs_2_, ...), custom_call_target="tpu_custom_call" | custom-call | flops 1024 | bytes 1024 | tf_op jit(solution)/shard_map/pallas_call | solution.py:292
  164.7 2.3 broadcast_select_fusion
  167.0 1.3 collective-permute-start.12
  169.3 3.0 %shard_map.65 = bf16[256,2048]{1,0:T(8,128)(2,1)} custom-call(s32[57]{0:T(128)} %get-tuple-element.60.index.flags, f32[512,2048]{1,0:T(8,128)} %get-tuple-element.44.refs_0_, bf16[256,2048]{1,0:T(8,128)(2,1)} %copy-done.7), custom_call_target="tpu_custom_call" | custom-call | flops 1024 | bytes 1024 | tf_op jit(solution)/shard_map/pallas_call | solution.py:207
  172.3 1.5 collective-permute-start.13
  173.8 9.0 %collective-permute-done.9.refs_1_ = bf16[256,2048]{1,0:T(8,128)(2,1)} collective-permute-done((bf16[256,2048]{1,0:T(8,128)(2,1)}, bf16[256,2048]{1,0:T(8,128)(2,1)}, u32[]{:S(2)}, u32[]{:S(2)}) %collective-permute-start.9) | collective-permute-done | bytes 1048608 | tf_op jit(solution)/shard_map/ppermute | solution.py:568
  182.8 3.4 %shard_map.66 = bf16[256,2048]{1,0:T(8,128)(2,1)} custom-call(s32[57]{0:T(128)} %get-tuple-element.60.index.flags, f32[512,2048]{1,0:T(8,128)} %get-tuple-element.44.refs_0_, bf16[256,2048]{1,0:T(8,128)(2,1)} %collective-permute-done.9.refs_1_), custom_call_target="tpu_custom_call" | custom-call | flops 1024 | bytes 1024 | tf_op jit(solution)/shard_map/pallas_call | solution.py:207
  186.3 1.3 copy-done.5
  187.6 6.1 %shard_map.67 = bf16[528,2048]{1,0:T(8,128)(2,1)} custom-call(s32[57]{0:T(128)} %get-tuple-element.60.index.flags, f32[512,2048]{1,0:T(8,128)} %get-tuple-element.41.refs_0_, bf16[528,2048]{1,0:T(8,128)(2,1)} %copy-done.5, f32[512,2048]{1,0:T(8,128)} %get-tuple-element.46.refs_2_.refs_0_, bf16[528,2048]{1,0:T(8,128)(2,1)} %collective-permute-done.11.refs_3_), custom_call_target="tpu_custom_call" | custom-call | flops 1024 | bytes 1024 | tf_op jit(solution)/shard_map/pallas_call | solution.py:207
  193.7 4.6 %collective-permute-start.15 = (bf16[528,2048]{1,0:T(8,128)(2,1)}, bf16[528,2048]{1,0:T(8,128)(2,1)S(1)}, u32[]{:S(2)}, u32[]{:S(2)}) collective-permute-start(bf16[528,2048]{1,0:T(8,128)(2,1)} %shard_map.67), channel_id=1, source_target_pairs={{4,0},{10,14},{8,4},{6,10},{5,1},{11,15},{9,5},{7,11},{20,16},{26,... | collective-permute-start | bytes 6488072 | tf_op jit(solution)/shard_map/ppermute | solution.py:568
  199.4 1.3 collective-permute-start.14
  200.7 5.6 %collective-permute-start.16 = (bf16[256,2048]{1,0:T(8,128)(2,1)S(1)}, bf16[256,2048]{1,0:T(8,128)(2,1)}, u32[]{:S(2)}, u32[]{:S(2)}) collective-permute-start(bf16[256,2048]{1,0:T(8,128)(2,1)S(1)} %copy-done.6), channel_id=1, source_target_pairs={{8,12},{6,2},{9,13},{7,3},{24,28},{22,18},{25,29},{23,19}} | collective-permute-start | bytes 3145736 | tf_op jit(solution)/shard_map/ppermute | solution.py:568
  207.3 3.1 %shard_map.68 = bf16[256,2048]{1,0:T(8,128)(2,1)} custom-call(s32[57]{0:T(128)} %get-tuple-element.60.index.flags, f32[512,2048]{1,0:T(8,128)} %get-tuple-element.50.refs_0_.refs_5_, bf16[256,2048]{1,0:T(8,128)(2,1)} %copy-done.3), custom_call_target="tpu_custom_call" | custom-call | flops 1024 | bytes 1024 | tf_op jit(solution)/shard_map/pallas_call | solution.py:207
  210.3 1.3 collective-permute-start.17
  211.6 3.4 %shard_map.69 = bf16[256,2048]{1,0:T(8,128)(2,1)} custom-call(s32[57]{0:T(128)} %get-tuple-element.60.index.flags, f32[512,2048]{1,0:T(8,128)} %get-tuple-element.44.refs_0_, bf16[256,2048]{1,0:T(8,128)(2,1)} %collective-permute-done.13.refs_1_), custom_call_target="tpu_custom_call" | custom-call | flops 1024 | bytes 1024 | tf_op jit(solution)/shard_map/pallas_call | solution.py:207
  215.0 1.3 collective-permute-start.18
  216.4 8.0 %collective-permute-done.14.refs_1_.refs_6_ = bf16[256,2048]{1,0:T(8,128)(2,1)S(1)} collective-permute-done((bf16[256,2048]{1,0:T(8,128)(2,1)}, bf16[256,2048]{1,0:T(8,128)(2,1)S(1)}, u32[]{:S(2)}, u32[]{:S(2)}) %collective-permute-start.14) | collective-permute-done | bytes 1048608 | tf_op jit(solution)/shard_map/ppermute | solution.py:568
  225.3 3.0 %shard_map.70 = bf16[256,2048]{1,0:T(8,128)(2,1)} custom-call(s32[57]{0:T(128)} %get-tuple-element.60.index.flags, f32[512,2048]{1,0:T(8,128)} %get-tuple-element.50.refs_0_.refs_5_, bf16[256,2048]{1,0:T(8,128)(2,1)} %copy-done.4), custom_call_target="tpu_custom_call" | custom-call | flops 1024 | bytes 1024 | tf_op jit(solution)/shard_map/pallas_call | solution.py:207
  228.4 1.3 collective-permute-start.19
  229.7 9.0 %collective-permute-done.17.refs_8_ = bf16[256,2048]{1,0:T(8,128)(2,1)} collective-permute-done((bf16[256,2048]{1,0:T(8,128)(2,1)}, bf16[256,2048]{1,0:T(8,128)(2,1)}, u32[]{:S(2)}, u32[]{:S(2)}) %collective-permute-start.17) | collective-permute-done | bytes 1048608 | tf_op jit(solution)/shard_map/ppermute | solution.py:568
  238.6 4.4 %collective-permute-done.15.refs_3_.refs_4_ = bf16[528,2048]{1,0:T(8,128)(2,1)S(1)} collective-permute-done((bf16[528,2048]{1,0:T(8,128)(2,1)}, bf16[528,2048]{1,0:T(8,128)(2,1)S(1)}, u32[]{:S(2)}, u32[]{:S(2)}) %collective-permute-start.15) | collective-permute-done | bytes 2162720 | tf_op jit(solution)/shard_map/ppermute | solution.py:568
  243.0 1.4 copy-done.1
  244.4 5.5 %shard_map.71.refs_9_ = f32[512,2048]{1,0:T(8,128)} custom-call(s32[57]{0:T(128)} %get-tuple-element.60.index.flags, f32[512,2048]{1,0:T(8,128)} %get-tuple-element.46.refs_2_.refs_0_, bf16[528,2048]{1,0:T(8,128)(2,1)} %copy-done, bf16[528,2048]{1,0:T(8,128)(2,1)} %copy-done, bf16[528,2048]{1,0:T(8,128)(2,1)} %copy-done.1, bf16[528,2048]{1,0:T(8,128)(2,1)} %copy-done.1, ...), custom_call_target="tpu_custom_call" | custom-call | flops 1024 | bytes 1024 | tf_op jit(solution)/shard_map/pallas_call | solution.py:257
  249.9 7.3 %collective-permute-done.19.refs_8_ = bf16[256,2048]{1,0:T(8,128)(2,1)S(1)} collective-permute-done((bf16[256,2048]{1,0:T(8,128)(2,1)}, bf16[256,2048]{1,0:T(8,128)(2,1)S(1)}, u32[]{:S(2)}, u32[]{:S(2)}) %collective-permute-start.19) | collective-permute-done | bytes 1048608 | tf_op jit(solution)/shard_map/ppermute | solution.py:568
  258.2 5.5 %shard_map.72 = f32[512,2048]{1,0:T(8,128)} custom-call(s32[57]{0:T(128)} %get-tuple-element.60.index.flags, f32[512,2048]{1,0:T(8,128)} %get-tuple-element.46.refs_2_.refs_0_, bf16[528,2048]{1,0:T(8,128)(2,1)} %copy-done, bf16[528,2048]{1,0:T(8,128)(2,1)} %copy-done, bf16[528,2048]{1,0:T(8,128)(2,1)} %copy-done.1, ...), custom_call_target="tpu_custom_call", output_to_operand_aliasing={{}: (10, {})} | custom-call | flops 1024 | bytes 1024 | tf_op jit(solution)/shard_map/pallas_call | solution.py:257
  (56 shorter events, 17.1 us)
Async XLA Ops:
  0.0 20.4 %copy-start.15 = (s32[1,16]{1,0:T(1,128)S(1)}, s32[1,16]{1,0:T(1,128)}, u32[]{:S(2)}) copy-start(s32[1,16]{1,0:T(1,128)} %param.7) | copy-start | bytes 196
  0.0 20.4 %copy-start.14 = (s32[1,16,16]{2,1,0:T(8,128)S(1)}, s32[1,16,16]{2,1,0:T(8,128)}, u32[]{:S(2)}) copy-start(s32[1,16,16]{2,1,0:T(8,128)} %param.6) | copy-start | bytes 3076
  1.2 17.7 %collective-permute-start.1 = (bf16[640,512]{1,0:T(8,128)(2,1)S(1)}, bf16[640,512]{1,0:T(8,128)(2,1)S(1)}, u32[]{:S(2)}, u32[]{:S(2)}) collective-permute-start(bf16[640,512]{1,0:T(8,128)(2,1)S(1)} %constant_dynamic-slice_fusion), channel_id=1, source_target_pairs={{2,0},{0,2},{3,1},{1,3},{6,4},{4,6},{7,5},{5,7},{10,8},{8,10},{11,... | collective-permute-start | bytes 1966088 | tf_op jit(solution)/shard_map/ppermute | solution.py:398
  3.9 31.6 %collective-permute-start = (bf16[768,512]{1,0:T(8,128)(2,1)S(1)}, bf16[768,512]{1,0:T(8,128)(2,1)S(1)}, u32[]{:S(2)}, u32[]{:S(2)}) collective-permute-start(bf16[768,512]{1,0:T(8,128)(2,1)S(1)} %slice.12), channel_id=1, source_target_pairs={{2,0},{0,2},{3,1},{1,3},{6,4},{4,6},{7,5},{5,7},{10,8},{8,10},{11,... | collective-permute-start | bytes 2359304 | tf_op jit(solution)/shard_map/ppermute | solution.py:399
  18.8 4.9 %copy-start.12 = (bf16[640,512]{1,0:T(8,128)(2,1)}, bf16[640,512]{1,0:T(8,128)(2,1)S(1)}, u32[]{:S(2)}) copy-start(bf16[640,512]{1,0:T(8,128)(2,1)S(1)} %collective-permute-done.1.refs_1_) | copy-start | bytes 1966084
  18.9 16.7 %collective-permute-start.2 = (bf16[640,512]{1,0:T(8,128)(2,1)S(1)}, bf16[640,512]{1,0:T(8,128)(2,1)S(1)}, u32[]{:S(2)}, u32[]{:S(2)}) collective-permute-start(bf16[640,512]{1,0:T(8,128)(2,1)S(1)} %collective-permute-done.1.refs_1_), channel_id=1, source_target_pairs={{0,4},{4,0},{8,12},{12,8},{1,5},{5,1},{9,13},{13,9},{2,6},{6,2},{1... | collective-permute-start | bytes 1966088 | tf_op jit(solution)/shard_map/ppermute | solution.py:433
  35.6 1.0 copy-start.11
  36.5 0.8 copy-start.13
  49.7 7.6 %collective-permute-start.3 = (bf16[2048,1024]{1,0:T(8,128)(2,1)}, bf16[2048,1024]{1,0:T(8,128)(2,1)}, u32[]{:S(2)}, u32[]{:S(2)}) collective-permute-start(bf16[2048,1024]{1,0:T(8,128)(2,1)} %shard_map.56.refs_2_), channel_id=1, source_target_pairs={{1,0},{0,1},{3,2},{2,3},{5,4},{4,5},{7,6},{6,7},{9,8},{8,9},{11,10... | collective-permute-start | bytes 12582920 | tf_op jit(solution)/shard_map/ppermute | solution.py:451
  60.5 48.8 %collective-permute-start.4 = (bf16[2,512,1024]{2,1,0:T(8,128)(2,1)}, bf16[2,512,1024]{2,1,0:T(8,128)(2,1)}, u32[]{:S(2)}, u32[]{:S(2)}) collective-permute-start(bf16[2,512,1024]{2,1,0:T(8,128)(2,1)} %shard_map.57), channel_id=1, source_target_pairs={{2,0},{0,2},{3,1},{1,3},{6,4},{4,6},{7,5},{5,7},{10,8},{8,10},{11,... | collective-permute-start | bytes 6291464 | tf_op jit(solution)/shard_map/ppermute | solution.py:536
  72.7 50.4 %collective-permute-start.5 = (bf16[528,2048]{1,0:T(8,128)(2,1)}, bf16[528,2048]{1,0:T(8,128)(2,1)S(1)}, u32[]{:S(2)}, u32[]{:S(2)}) collective-permute-start(bf16[528,2048]{1,0:T(8,128)(2,1)} %get-tuple-element.34), channel_id=1, source_target_pairs={{0,4},{12,8},{2,6},{14,10},{1,5},{13,9},{3,7},{15,11},{16,20},{28,... | collective-permute-start | bytes 6488072 | tf_op jit(solution)/shard_map/ppermute | solution.py:568
  87.8 65.6 %collective-permute-start.7 = (bf16[2,512,1024]{2,1,0:T(8,128)(2,1)}, bf16[2,512,1024]{2,1,0:T(8,128)(2,1)S(1)}, u32[]{:S(2)}, u32[]{:S(2)}) collective-permute-start(bf16[2,512,1024]{2,1,0:T(8,128)(2,1)} %shard_map.63), channel_id=1, source_target_pairs={{2,0},{0,2},{3,1},{1,3},{6,4},{4,6},{7,5},{5,7},{10,8},{8,10},{11,... | collective-permute-start | bytes 6291464 | tf_op jit(solution)/shard_map/ppermute | solution.py:536
  119.4 22.1 %collective-permute-start.6 = (bf16[256,2048]{1,0:T(8,128)(2,1)}, bf16[256,2048]{1,0:T(8,128)(2,1)}, u32[]{:S(2)}, u32[]{:S(2)}) collective-permute-start(bf16[256,2048]{1,0:T(8,128)(2,1)} %get-tuple-element.39), channel_id=1, source_target_pairs={{0,4},{14,10},{1,5},{15,11},{16,20},{30,26},{17,21},{31,27}} | collective-permute-start | bytes 3145736 | tf_op jit(solution)/shard_map/ppermute | solution.py:568
  121.1 65.2 %collective-permute-start.11 = (bf16[528,2048]{1,0:T(8,128)(2,1)}, bf16[528,2048]{1,0:T(8,128)(2,1)}, u32[]{:S(2)}, u32[]{:S(2)}) collective-permute-start(bf16[528,2048]{1,0:T(8,128)(2,1)} %get-tuple-element.36), channel_id=1, source_target_pairs={{12,8},{2,6},{13,9},{3,7},{28,24},{18,22},{29,25},{19,23}} | collective-permute-start | bytes 6488072 | tf_op jit(solution)/shard_map/ppermute | solution.py:568
  123.1 1.4 copy-start
  129.6 56.7 %collective-permute-start.10 = (bf16[528,2048]{1,0:T(8,128)(2,1)}, bf16[528,2048]{1,0:T(8,128)(2,1)S(1)}, u32[]{:S(2)}, u32[]{:S(2)}) collective-permute-start(bf16[528,2048]{1,0:T(8,128)(2,1)} %shard_map.61), channel_id=1, source_target_pairs={{8,4},{6,10},{9,5},{7,11},{24,20},{22,26},{25,21},{23,27}} | collective-permute-start | bytes 6488072 | tf_op jit(solution)/shard_map/ppermute | solution.py:568
  140.8 27.6 %collective-permute-start.8 = (bf16[256,2048]{1,0:T(8,128)(2,1)}, bf16[256,2048]{1,0:T(8,128)(2,1)S(1)}, u32[]{:S(2)}, u32[]{:S(2)}) collective-permute-start(bf16[256,2048]{1,0:T(8,128)(2,1)} %get-tuple-element.42), channel_id=1, source_target_pairs={{0,4},{14,10},{1,5},{15,11},{16,20},{30,26},{17,21},{31,27}} | collective-permute-start | bytes 3145736 | tf_op jit(solution)/shard_map/ppermute | solution.py:568
  144.5 38.3 %collective-permute-start.9 = (bf16[256,2048]{1,0:T(8,128)(2,1)}, bf16[256,2048]{1,0:T(8,128)(2,1)}, u32[]{:S(2)}, u32[]{:S(2)}) collective-permute-start(bf16[256,2048]{1,0:T(8,128)(2,1)} %shard_map.62), channel_id=1, source_target_pairs={{4,8},{10,6},{5,9},{11,7},{20,24},{26,22},{21,25},{27,23}} | collective-permute-start | bytes 3145736 | tf_op jit(solution)/shard_map/ppermute | solution.py:568
  153.4 1.3 copy-start.2
  167.0 39.3 %collective-permute-start.12 = (bf16[256,2048]{1,0:T(8,128)(2,1)}, bf16[256,2048]{1,0:T(8,128)(2,1)S(1)}, u32[]{:S(2)}, u32[]{:S(2)}) collective-permute-start(bf16[256,2048]{1,0:T(8,128)(2,1)} %broadcast_select_fusion), channel_id=1, source_target_pairs={{0,4},{12,8},{2,6},{14,10},{1,5},{13,9},{3,7},{15,11},{16,20},{28,... | collective-permute-start | bytes 3145736 | tf_op jit(solution)/shard_map/ppermute | solution.py:568
  168.3 1.0 copy-start.7
  172.3 39.3 %collective-permute-start.13 = (bf16[256,2048]{1,0:T(8,128)(2,1)}, bf16[256,2048]{1,0:T(8,128)(2,1)}, u32[]{:S(2)}, u32[]{:S(2)}) collective-permute-start(bf16[256,2048]{1,0:T(8,128)(2,1)} %shard_map.65), channel_id=1, source_target_pairs={{4,8},{10,6},{5,9},{11,7},{20,24},{26,22},{21,25},{27,23}} | collective-permute-start | bytes 3145736 | tf_op jit(solution)/shard_map/ppermute | solution.py:568
  186.3 12.1 %copy-start.8 = (bf16[256,2048]{1,0:T(8,128)(2,1)S(1)}, bf16[256,2048]{1,0:T(8,128)(2,1)}, u32[]{:S(2)}) copy-start(bf16[256,2048]{1,0:T(8,128)(2,1)} %get-tuple-element.42) | copy-start | bytes 3145732
  186.3 1.3 copy-start.5
  193.7 7.0 %copy-start.6 = (bf16[256,2048]{1,0:T(8,128)(2,1)S(1)}, bf16[256,2048]{1,0:T(8,128)(2,1)}, u32[]{:S(2)}) copy-start(bf16[256,2048]{1,0:T(8,128)(2,1)} %shard_map.66) | copy-start | bytes 3145732
  193.7 49.3 %collective-permute-start.15 = (bf16[528,2048]{1,0:T(8,128)(2,1)}, bf16[528,2048]{1,0:T(8,128)(2,1)S(1)}, u32[]{:S(2)}, u32[]{:S(2)}) collective-permute-start(bf16[528,2048]{1,0:T(8,128)(2,1)} %shard_map.67), channel_id=1, source_target_pairs={{4,0},{10,14},{8,4},{6,10},{5,1},{11,15},{9,5},{7,11},{20,16},{26,... | collective-permute-start | bytes 6488072 | tf_op jit(solution)/shard_map/ppermute | solution.py:568
  199.4 24.9 %collective-permute-start.14 = (bf16[256,2048]{1,0:T(8,128)(2,1)}, bf16[256,2048]{1,0:T(8,128)(2,1)S(1)}, u32[]{:S(2)}, u32[]{:S(2)}) collective-permute-start(bf16[256,2048]{1,0:T(8,128)(2,1)} %broadcast_select_fusion.1), channel_id=1, source_target_pairs={{0,4},{12,8},{2,6},{14,10},{1,5},{13,9},{3,7},{15,11},{16,20},{28,... | collective-permute-start | bytes 3145736 | tf_op jit(solution)/shard_map/ppermute | solution.py:568
  200.7 28.9 %collective-permute-start.16 = (bf16[256,2048]{1,0:T(8,128)(2,1)S(1)}, bf16[256,2048]{1,0:T(8,128)(2,1)}, u32[]{:S(2)}, u32[]{:S(2)}) collective-permute-start(bf16[256,2048]{1,0:T(8,128)(2,1)S(1)} %copy-done.6), channel_id=1, source_target_pairs={{8,12},{6,2},{9,13},{7,3},{24,28},{22,18},{25,29},{23,19}} | collective-permute-start | bytes 3145736 | tf_op jit(solution)/shard_map/ppermute | solution.py:568
  206.3 1.0 copy-start.3
  210.3 28.3 %collective-permute-start.17 = (bf16[256,2048]{1,0:T(8,128)(2,1)}, bf16[256,2048]{1,0:T(8,128)(2,1)}, u32[]{:S(2)}, u32[]{:S(2)}) collective-permute-start(bf16[256,2048]{1,0:T(8,128)(2,1)} %shard_map.68), channel_id=1, source_target_pairs={{4,8},{10,6},{5,9},{11,7},{20,24},{26,22},{21,25},{27,23}} | collective-permute-start | bytes 3145736 | tf_op jit(solution)/shard_map/ppermute | solution.py:568
  215.0 34.8 %collective-permute-start.18 = (bf16[256,2048]{1,0:T(8,128)(2,1)}, bf16[256,2048]{1,0:T(8,128)(2,1)S(1)}, u32[]{:S(2)}, u32[]{:S(2)}) collective-permute-start(bf16[256,2048]{1,0:T(8,128)(2,1)} %shard_map.69), channel_id=1, source_target_pairs={{8,12},{6,2},{9,13},{7,3},{24,28},{22,18},{25,29},{23,19}} | collective-permute-start | bytes 3145736 | tf_op jit(solution)/shard_map/ppermute | solution.py:568
  224.4 1.0 copy-start.4
  228.4 28.8 %collective-permute-start.19 = (bf16[256,2048]{1,0:T(8,128)(2,1)}, bf16[256,2048]{1,0:T(8,128)(2,1)S(1)}, u32[]{:S(2)}, u32[]{:S(2)}) collective-permute-start(bf16[256,2048]{1,0:T(8,128)(2,1)} %shard_map.70), channel_id=1, source_target_pairs={{4,8},{10,6},{5,9},{11,7},{20,24},{26,22},{21,25},{27,23}} | collective-permute-start | bytes 3145736 | tf_op jit(solution)/shard_map/ppermute | solution.py:568
  243.0 1.4 copy-start.1
  249.9 7.3 %copy-start.9 = (bf16[256,2048]{1,0:T(8,128)(2,1)}, bf16[256,2048]{1,0:T(8,128)(2,1)S(1)}, u32[]{:S(2)}) copy-start(bf16[256,2048]{1,0:T(8,128)(2,1)S(1)} %collective-permute-done.18.refs_7_) | copy-start | bytes 3145732
  257.2 1.0 copy-start.10
